TPU v7x, 32 devices: a whole 2x2x4 slice. The times are simulated.
32 devices in a mesh: region: 4 (over y, x), tile: 8 (over z, core).
Axes of the slice: x: 2, y: 2, z: 4, core: 2. Of those that a mesh axis runs over, the one named last changes fastest.
Arguments:
- features: bfloat16 [128, 32, 512], P(('region', 'tile')), may hold values from -6 to 6
- voxel_mask: int32 [128, 512], P(('region', 'tile')), may hold values 0 or 1
- brick_cell: int32 [128], P(('region', 'tile')), may hold values from -1 to 7, as said below
- conv_one: bfloat16 [27, 32, 32], replicated, may hold values from -0.3125 to 0.3125
- conv_two: bfloat16 [27, 32, 32], replicated, may hold values from -0.3125 to 0.3125
- down_weight: bfloat16 [8, 32, 64], replicated, may hold values from -0.375 to 0.375
- cotangent: bfloat16 [128, 4096], P(('region', 'tile')), may hold values from -6 to 6
Outputs:
- down: bfloat16 [128, 4096], P(('region', 'tile'))
- grad_features: bfloat16 [128, 32, 512], P(('region', 'tile'))
- grad_conv_one: float32 [27, 32, 32], replicated
- grad_conv_two: float32 [27, 32, 32], replicated
- grad_down: float32 [8, 32, 64], replicated
Inputs may be any that keep to these rules, and one draw needn't show every extreme that they name: `brick_cell`: entries come in blocks of 4, one block a device in the order of the slots. The live entries of a block name distinct brick cells of that device's box; -1 marks an empty slot, and in at least one block every entry is live.
All inputs are finite; a program needn't handle non-finite values. No bound on the sum of `voxel_mask` on one device may be relied on, other than what follows from the above.
Results may differ from a plain program's by a relative error of at most 0.0053.
Values may be sent and summed in bfloat16 or wider, within the bound.
No kernel may reach another device: no remote copies, remote signals or barrier semaphores. Data moves between devices by JAX's collectives and lax.ppermute only.
A program may use at most 192 MiB of HBM per device.

v0:
```python
import math

import jax
import jax.numpy as jnp
from jax import lax
from jax.sharding import PartitionSpec as P


def with_halo(cells, sides, width):
    for axis, dim in sides:
        count = lax.axis_size(axis)
        ends = count - 1
        head = lax.slice_in_dim(cells, 0, width, axis=dim)
        tail = lax.slice_in_dim(cells, cells.shape[dim] - width, cells.shape[dim], axis=dim)
        cells = jnp.concatenate(
            [
                lax.ppermute(tail, axis, [(i, (i + 1) % count) for i in range(ends)]),
                cells,
                lax.ppermute(head, axis, [((i + 1) % count, i) for i in range(ends)]),
            ],
            axis=dim,
        )
    return cells


def owner_table(brick_cell, slot_count):
    cell_range = jnp.arange(2 * slot_count, dtype=jnp.int32)
    matches = (brick_cell[None, :] == cell_range[:, None]).astype(jnp.int32)
    slot_range = jnp.arange(slot_count, dtype=jnp.int32)
    return jnp.sum(matches * slot_range[None, :], axis=1) + slot_count * (
        1 - jnp.sum(matches, axis=1)
    )


def build_field(values, cell_owner):
    slot_count = values.shape[0]
    channel_count = values.shape[1]
    padding = jnp.zeros((1, channel_count, 512), values.dtype)
    bricks = jnp.concatenate([values, padding], axis=0)[cell_owner]
    bricks = bricks.reshape(2, slot_count, channel_count, 8, 8, 8).transpose(2, 0, 3, 4, 1, 5)
    return bricks.reshape(channel_count, 16, 8, 8 * slot_count)


def pad_depth(widened, depth):
    return jnp.pad(widened, ((0, 0), (0, 0), (0, 0), (depth, depth)))


def extend(values, cell_owner):
    widened = with_halo(build_field(values, cell_owner), (("region", 1), ("tile", 2)), 1)
    return pad_depth(widened, 1)


def read_slots(dense, brick_cell, slot_count):
    channels_out = dense.shape[0]
    bricks = dense.reshape(channels_out, 2, 8, 8, slot_count, 8).transpose(1, 4, 0, 2, 3, 5)
    bricks = bricks.reshape(2 * slot_count, channels_out, 512)
    return bricks[jnp.maximum(brick_cell, 0)]


def flatten_field(widened):
    chans, size_x, size_y, size_z = widened.shape
    return jnp.pad(widened.reshape(chans, size_x, size_y * size_z), ((0, 0), (0, 0), (1, 1)))


def stacked_taps(flattened, shape_full, shift_x, shift_y, sign):
    chans, size_x, size_y, size_z = shape_full
    out_x = size_x - 2
    length = (size_y - 2) * size_z
    start_x = 1 + sign * shift_x
    pieces = []
    for shift_z in (-1, 0, 1):
        start_n = (1 + sign * shift_y) * size_z + sign * shift_z + 1
        pieces.append(
            lax.slice(flattened, (0, start_x, start_n), (chans, start_x + out_x, start_n + length))
        )
    return jnp.concatenate(pieces, axis=0)


def spatial_conv(widened, weights, sign):
    shape_full = widened.shape
    size_x, size_y, size_z = (shape_full[1], shape_full[2], shape_full[3])
    flattened = flatten_field(widened)
    summed_taps = None
    for shift_x in (-1, 0, 1):
        for shift_y in (-1, 0, 1):
            first_tap = 9 * (shift_x + 1) + 3 * (shift_y + 1)
            stacked = stacked_taps(flattened, shape_full, shift_x, shift_y, sign)
            taps = weights[first_tap : first_tap + 3]
            if sign > 0:
                tap_term = jnp.einsum(
                    "ixn,io->oxn",
                    stacked,
                    taps.reshape(-1, taps.shape[2]),
                    preferred_element_type=jnp.float32,
                )
            else:
                tap_term = jnp.einsum(
                    "oxn,oi->ixn",
                    stacked,
                    taps.transpose(0, 2, 1).reshape(-1, taps.shape[1]),
                    preferred_element_type=jnp.float32,
                )
            summed_taps = tap_term if summed_taps is None else summed_taps + tap_term
    result = summed_taps.reshape(summed_taps.shape[0], size_x - 2, size_y - 2, size_z)
    return result[:, :, :, 1:-1]


def kernel_grad(widened, grad_field):
    shape_full = widened.shape
    chans = shape_full[0]
    flattened = flatten_field(widened)
    grad_flat = pad_depth(grad_field, 1)
    grad_flat = grad_flat.reshape(grad_flat.shape[0], grad_flat.shape[1], -1)
    tap_terms = []
    for shift_x in (-1, 0, 1):
        for shift_y in (-1, 0, 1):
            stacked = stacked_taps(flattened, shape_full, shift_x, shift_y, 1)
            product = jnp.einsum(
                "ixn,oxn->io", stacked, grad_flat, preferred_element_type=jnp.float32
            )
            tap_terms.append(product.reshape(3, chans, -1))
    return jnp.concatenate(tap_terms, axis=0)


def on_device(features, voxel_mask, brick_cell, conv_one, conv_two, down_weight, cotangent):
    slot_count = features.shape[0]
    channel_count = features.shape[1]
    down_count = down_weight.shape[2]
    live_slot = brick_cell >= 0
    cell_owner = owner_table(brick_cell, slot_count)
    mask_slot = (voxel_mask.astype(jnp.float32) * live_slot[:, None].astype(jnp.float32))[
        :, None, :
    ]
    inputs = features * mask_slot.astype(jnp.bfloat16)
    input_grown = extend(inputs, cell_owner)
    first_pre = (
        read_slots(spatial_conv(input_grown, conv_one, 1), brick_cell, slot_count) * mask_slot
    )
    hidden = jax.nn.silu(first_pre).astype(jnp.bfloat16)
    hidden_grown = extend(hidden, cell_owner)
    second_pre = (
        read_slots(spatial_conv(hidden_grown, conv_two, 1), brick_cell, slot_count) * mask_slot
    )
    summed = (inputs.astype(jnp.float32) + second_pre).astype(jnp.bfloat16)
    shaped = summed.reshape(slot_count, channel_count, 4, 2, 4, 2, 4, 2)
    kernel = down_weight.reshape(2, 2, 2, channel_count, down_count)
    down = jnp.einsum("tcxaybzd,abdco->toxyz", shaped, kernel, preferred_element_type=jnp.float32)
    down = down.reshape(slot_count, -1).astype(jnp.bfloat16)
    upstream = cotangent.reshape(slot_count, down_count, 4, 4, 4)
    back_sum = jnp.einsum(
        "toxyz,abdco->tcxaybzd", upstream, kernel, preferred_element_type=jnp.float32
    )
    back_sum = back_sum.reshape(slot_count, channel_count, 512)
    down_grad = jnp.einsum(
        "tcxaybzd,toxyz->abdco", shaped, upstream, preferred_element_type=jnp.float32
    )
    down_grad = down_grad.reshape(8, channel_count, down_count)
    second_grad = (back_sum * mask_slot).astype(jnp.bfloat16)
    grad_grown = extend(second_grad, cell_owner)
    weight_two = kernel_grad(hidden_grown, build_field(second_grad, cell_owner))
    spread = read_slots(spatial_conv(grad_grown, conv_two, -1), brick_cell, slot_count)
    sigmoid_value = jax.nn.sigmoid(first_pre)
    first_grad = (
        spread * sigmoid_value * (1.0 + first_pre * (1.0 - sigmoid_value)) * mask_slot
    ).astype(jnp.bfloat16)
    first_grown = extend(first_grad, cell_owner)
    weight_one = kernel_grad(input_grown, build_field(first_grad, cell_owner))
    spread_one = read_slots(spatial_conv(first_grown, conv_one, -1), brick_cell, slot_count)
    grad_features = ((back_sum + spread_one) * mask_slot).astype(jnp.bfloat16)
    weight_one, weight_two, down_grad = lax.psum(
        (weight_one, weight_two, down_grad), ("region", "tile")
    )
    total_slots = slot_count * lax.axis_size("region") * lax.axis_size("tile")
    scale = 1.0 / math.sqrt(total_slots * 512.0)
    return (down, grad_features, weight_one * scale, weight_two * scale, down_grad * scale)


def solution(mesh):
    in_specs = (
        P(("region", "tile"), None, None),
        P(("region", "tile"), None),
        P(("region", "tile")),
        P(),
        P(),
        P(),
        P(("region", "tile"), None),
    )
    out_specs = (P(("region", "tile"), None), P(("region", "tile"), None, None), P(), P(), P())
    return jax.shard_map(
        on_device, mesh=mesh, in_specs=in_specs, out_specs=out_specs, check_vma=False
    )
```

profile of v0, /device:TPU:0, one launch (start us, length us, event | category | flops | bytes accessed | tf_op | source)
XLA Modules:
  0.0 542.1 jit_solution(7006894433195453446)
XLA Ops:
  12.9 4.8 collective-permute-start
  27.4 4.5 collective-permute-start.8
  48.9 3.1 reshape.511
  54.9 4.8 collective-permute-start.10
  66.4 8.6 %fusion.320 = (bf16[32,16,272]{0,2,1:T(8,128)(2,1)}, bf16[32,16,272]{0,2,1:T(8,128)(2,1)}, bf16[32,16,272]{0,2,1:T(8,128)(2,1)}, bf16[32,16,272]{0,2,1:T(8,128)(...) fusion(bf16[32,18,340]{0,2,1:T(8,128)(2,1)S(1)} %reshape.488), kind=kLoop, calls=%fused_computation.393 | loop fusion | bytes 22474752 | tf_op jit(solution)/shard_map/slice | solution.py:74
  75.0 3.9 fusion.321
  84.0 3.7 fusion.317
  87.7 8.8 %fusion.316 = (bf16[32,16,272]{0,2,1:T(8,128)(2,1)}, bf16[32,16,272]{0,2,1:T(8,128)(2,1)}, bf16[32,16,272]{0,2,1:T(8,128)(2,1)}, bf16[32,16,272]{0,2,1:T(8,128)(...) fusion(bf16[32,18,340]{0,2,1:T(8,128)(2,1)S(1)} %reshape.490), kind=kLoop, calls=%fused_computation.389 | loop fusion | bytes 22474752 | tf_op jit(solution)/shard_map/slice | solution.py:74
  136.7 3.0 copy.703
  143.0 3.2 fusion.165
  165.3 3.1 copy.705
  200.1 4.9 collective-permute-start.4
  206.3 5.5 %collective-permute-start.12 = (bf16[32,1,8,32]{0,3,2,1:T(8,128)(2,1)S(1)}, bf16[32,1,8,32]{0,3,2,1:T(8,128)(2,1)S(1)}, u32[]{:S(2)}, u32[]{:S(2)}) collective-permute-start(bf16[32,1,8,32]{0,3,2,1:T(8,128)(2,1)S(1)} %get-tuple-element.128), channel_id=1, source_target_pairs={{0,8},{8,16},{16,24},{1,9},{9,17},{17,25},{2,10},{10,18},{18,26},{... | collective-permute-start | bytes 49160 | tf_op jit(solution)/shard_map/ppermute | solution.py:17
  213.1 3.1 reshape.510
  228.1 3.7 collective-permute-start.6
  233.2 4.8 collective-permute-start.14
  239.4 3.0 select_maximum_fusion.8
  244.9 8.7 %fusion.318 = (bf16[32,16,272]{0,2,1:T(8,128)(2,1)}, bf16[32,16,272]{0,2,1:T(8,128)(2,1)}, bf16[32,16,272]{0,2,1:T(8,128)(2,1)}, bf16[32,16,272]{0,2,1:T(8,128)(...) fusion(bf16[32,18,340]{0,2,1:T(8,128)(2,1)S(1)} %reshape.489), kind=kLoop, calls=%fused_computation.391 | loop fusion | bytes 22474752 | tf_op jit(solution)/shard_map/slice | solution.py:74
  253.6 3.9 fusion.319
  262.7 3.9 fusion.315
  266.6 8.5 %fusion.314 = (bf16[32,16,272]{0,2,1:T(8,128)(2,1)}, bf16[32,16,272]{0,2,1:T(8,128)(2,1)}, bf16[32,16,272]{0,2,1:T(8,128)(2,1)}, bf16[32,16,272]{0,2,1:T(8,128)(...) fusion(bf16[32,18,340]{0,2,1:T(8,128)(2,1)S(1)} %reshape.500), kind=kLoop, calls=%fused_computation.387 | loop fusion | bytes 22474752 | tf_op jit(solution)/shard_map/slice | solution.py:74
  282.9 3.4 fusion.303
  294.0 3.6 fusion.302
  300.3 3.6 fusion.300
  306.7 3.6 fusion.299
  310.4 3.2 copy.643
  313.6 3.6 fusion.298
  319.9 3.9 fusion.301
  326.6 3.4 convolution_add_fusion.23
  344.5 3.1 copy.704
  373.0 3.2 copy.706
  398.8 132.0 %all-reduce.17.cloned.1.call-done = (f32[27,32,32]{2,1,0:T(8,128)}, f32[27,32,32]{2,1,0:T(8,128)}, f32[8,32,64]{2,1,0:T(8,128)}) async-done(((f32[27,32,32]{2,1,0:T(8,128)}, f32[27,32,32]{2,1,0:T(8,128)}, f32[8,32,64]{2,1,0:T(8,128)}), (f32[27,32,32]{2,1,0:T(8,128)}, f32[27,32,32]{2,1,0:T(8,128)}, f32[8,32,64]{2,1,0:T(8,128)})) %all-reduce.17.cloned.1.call-update) | async-done | bytes 286736 | tf_op jit(solution)/shard_map/psum | solution.py:170
  (592 shorter events, 257.7 us)
Async XLA Ops:
  7.2 15.2 %copy-start = (bf16[8,32,64]{2,1,0:T(8,128)(2,1)S(1)}, bf16[8,32,64]{2,1,0:T(8,128)(2,1)}, u32[]{:S(2)}) copy-start(bf16[8,32,64]{2,1,0:T(8,128)(2,1)} %param.12) | copy-start | bytes 98308
  7.2 523.6 %all-reduce.17.cloned.1.call-start = ((), (), s32[]{:S(2)}) async-start(), calls=%async_computation | async-start | bytes 2031616 | tf_op jit(solution)/shard_map/psum | solution.py:170
  9.3 14.7 %copy-start.184 = (s32[1024]{0:T(1024)}, s32[1024]{0:T(1024)S(1)}, u32[]{:S(2)}) copy-start(s32[1024]{0:T(1024)S(1)} %get-tuple-element.177) | copy-start | bytes 12292
  9.3 162.5 %copy-start.183 = (s32[1024]{0:T(1024)}, s32[1024]{0:T(1024)S(1)}, u32[]{:S(2)}) copy-start(s32[1024]{0:T(1024)S(1)} %get-tuple-element.176) | copy-start | bytes 12292
  10.1 13.9 %copy-start.142 = (f32[4,512]{1,0:T(4,128)}, f32[4,512]{1,0:T(4,128)S(1)}, u32[]{:S(2)}) copy-start(f32[4,512]{1,0:T(4,128)S(1)} %get-tuple-element.11) | copy-start | bytes 24580
  12.7 6.4 %copy-start.182 = (bf16[4,4096]{1,0:T(4,128)(2,1)S(1)}, bf16[4,4096]{1,0:T(4,128)(2,1)}, u32[]{:S(2)}) copy-start(bf16[4,4096]{1,0:T(4,128)(2,1)} %param.13) | copy-start | bytes 98308
  12.9 39.2 %collective-permute-start = (bf16[32,1,8,32]{0,3,2,1:T(8,128)(2,1)S(1)}, bf16[32,1,8,32]{0,3,2,1:T(8,128)(2,1)S(1)}, u32[]{:S(2)}, u32[]{:S(2)}) collective-permute-start(bf16[32,1,8,32]{0,3,2,1:T(8,128)(2,1)S(1)} %get-tuple-element.134), channel_id=1, source_target_pairs={{0,8},{8,16},{16,24},{1,9},{9,17},{17,25},{2,10},{10,18},{18,26},{... | collective-permute-start | bytes 49160 | tf_op jit(solution)/shard_map/ppermute | solution.py:17
  17.8 34.3 %collective-permute-start.1 = (bf16[32,1,8,32]{0,3,2,1:T(8,128)(2,1)S(1)}, bf16[32,1,8,32]{0,3,2,1:T(8,128)(2,1)S(1)}, u32[]{:S(2)}, u32[]{:S(2)}) collective-permute-start(bf16[32,1,8,32]{0,3,2,1:T(8,128)(2,1)S(1)} %get-tuple-element.135), channel_id=1, source_target_pairs={{8,0},{16,8},{24,16},{9,1},{17,9},{25,17},{10,2},{18,10},{26,18},{... | collective-permute-start | bytes 49160 | tf_op jit(solution)/shard_map/ppermute | solution.py:19
  25.9 7.3 %copy-start.140 = (bf16[27,32,32]{2,1,0:T(8,128)(2,1)S(1)}, bf16[27,32,32]{2,1,0:T(8,128)(2,1)}, u32[]{:S(2)}) copy-start(bf16[27,32,32]{2,1,0:T(8,128)(2,1)} %param.10) | copy-start | bytes 165892
  25.9 8.0 %copy-start.141 = (bf16[27,32,32]{2,1,0:T(8,128)(2,1)S(1)}, bf16[27,32,32]{2,1,0:T(8,128)(2,1)}, u32[]{:S(2)}) copy-start(bf16[27,32,32]{2,1,0:T(8,128)(2,1)} %param.11) | copy-start | bytes 165892
  27.4 27.4 %collective-permute-start.8 = (bf16[32,1,8,32]{0,3,2,1:T(8,128)(2,1)S(1)}, bf16[32,1,8,32]{0,3,2,1:T(8,128)(2,1)S(1)}, u32[]{:S(2)}, u32[]{:S(2)}) collective-permute-start(bf16[32,1,8,32]{0,3,2,1:T(8,128)(2,1)S(1)} %get-tuple-element.130), channel_id=1, source_target_pairs={{0,8},{8,16},{16,24},{1,9},{9,17},{17,25},{2,10},{10,18},{18,26},{... | collective-permute-start | bytes 49160 | tf_op jit(solution)/shard_map/ppermute | solution.py:17
  31.9 22.8 %collective-permute-start.9 = (bf16[32,1,8,32]{0,3,2,1:T(8,128)(2,1)S(1)}, bf16[32,1,8,32]{0,3,2,1:T(8,128)(2,1)S(1)}, u32[]{:S(2)}, u32[]{:S(2)}) collective-permute-start(bf16[32,1,8,32]{0,3,2,1:T(8,128)(2,1)S(1)} %get-tuple-element.131), channel_id=1, source_target_pairs={{8,0},{16,8},{24,16},{9,1},{17,9},{25,17},{10,2},{18,10},{26,18},{... | collective-permute-start | bytes 49160 | tf_op jit(solution)/shard_map/ppermute | solution.py:19
  52.1 9.0 %collective-permute-start.2 = (bf16[32,18,1,32]{0,3,2,1:T(8,128)(2,1)S(1)}, bf16[32,18,1,32]{0,3,2,1:T(8,128)(2,1)S(1)}, u32[]{:S(2)}, u32[]{:S(2)}) collective-permute-start(bf16[32,18,1,32]{0,3,2,1:T(8,128)(2,1)S(1)} %get-tuple-element.126), channel_id=1, source_target_pairs={{0,1},{1,2},{2,3},{3,4},{4,5},{5,6},{6,7},{8,9},{9,10},{10,11},{11... | collective-permute-start | bytes 110600 | tf_op jit(solution)/shard_map/ppermute | solution.py:17
  53.5 7.7 %collective-permute-start.3 = (bf16[32,18,1,32]{0,3,2,1:T(8,128)(2,1)S(1)}, bf16[32,18,1,32]{0,3,2,1:T(8,128)(2,1)S(1)}, u32[]{:S(2)}, u32[]{:S(2)}) collective-permute-start(bf16[32,18,1,32]{0,3,2,1:T(8,128)(2,1)S(1)} %get-tuple-element.127), channel_id=1, source_target_pairs={{1,0},{2,1},{3,2},{4,3},{5,4},{6,5},{7,6},{9,8},{10,9},{11,10},{12... | collective-permute-start | bytes 110600 | tf_op jit(solution)/shard_map/ppermute | solution.py:19
  54.9 24.0 %collective-permute-start.10 = (bf16[32,18,1,32]{0,3,2,1:T(8,128)(2,1)S(1)}, bf16[32,18,1,32]{0,3,2,1:T(8,128)(2,1)S(1)}, u32[]{:S(2)}, u32[]{:S(2)}) collective-permute-start(bf16[32,18,1,32]{0,3,2,1:T(8,128)(2,1)S(1)} %get-tuple-element.122), channel_id=1, source_target_pairs={{0,1},{1,2},{2,3},{3,4},{4,5},{5,6},{6,7},{8,9},{9,10},{10,11},{11... | collective-permute-start | bytes 110600 | tf_op jit(solution)/shard_map/ppermute | solution.py:17
  59.7 19.2 %collective-permute-start.11 = (bf16[32,18,1,32]{0,3,2,1:T(8,128)(2,1)S(1)}, bf16[32,18,1,32]{0,3,2,1:T(8,128)(2,1)S(1)}, u32[]{:S(2)}, u32[]{:S(2)}) collective-permute-start(bf16[32,18,1,32]{0,3,2,1:T(8,128)(2,1)S(1)} %get-tuple-element.123), channel_id=1, source_target_pairs={{1,0},{2,1},{3,2},{4,3},{5,4},{6,5},{7,6},{9,8},{10,9},{11,10},{12... | collective-permute-start | bytes 110600 | tf_op jit(solution)/shard_map/ppermute | solution.py:19
  87.7 8.8 %copy-start.55 = (bf16[32,16,272]{0,2,1:T(8,128)(2,1)S(1)}, bf16[32,16,272]{0,2,1:T(8,128)(2,1)}, u32[]{:S(2)}) copy-start(bf16[32,16,272]{0,2,1:T(8,128)(2,1)} %get-tuple-element.117) | copy-start | bytes 835588
  87.7 8.8 %copy-start.56 = (bf16[32,16,272]{0,2,1:T(8,128)(2,1)S(1)}, bf16[32,16,272]{0,2,1:T(8,128)(2,1)}, u32[]{:S(2)}) copy-start(bf16[32,16,272]{0,2,1:T(8,128)(2,1)} %get-tuple-element.118) | copy-start | bytes 835588
  87.7 8.8 %copy-start.57 = (bf16[32,16,272]{0,2,1:T(8,128)(2,1)S(1)}, bf16[32,16,272]{0,2,1:T(8,128)(2,1)}, u32[]{:S(2)}) copy-start(bf16[32,16,272]{0,2,1:T(8,128)(2,1)} %get-tuple-element.119) | copy-start | bytes 835588
  200.1 27.9 %collective-permute-start.4 = (bf16[32,1,8,32]{0,3,2,1:T(8,128)(2,1)S(1)}, bf16[32,1,8,32]{0,3,2,1:T(8,128)(2,1)S(1)}, u32[]{:S(2)}, u32[]{:S(2)}) collective-permute-start(bf16[32,1,8,32]{0,3,2,1:T(8,128)(2,1)S(1)} %get-tuple-element.132), channel_id=1, source_target_pairs={{0,8},{8,16},{16,24},{1,9},{9,17},{17,25},{2,10},{10,18},{18,26},{... | collective-permute-start | bytes 49160 | tf_op jit(solution)/shard_map/ppermute | solution.py:17
  205.0 23.0 %collective-permute-start.5 = (bf16[32,1,8,32]{0,3,2,1:T(8,128)(2,1)S(1)}, bf16[32,1,8,32]{0,3,2,1:T(8,128)(2,1)S(1)}, u32[]{:S(2)}, u32[]{:S(2)}) collective-permute-start(bf16[32,1,8,32]{0,3,2,1:T(8,128)(2,1)S(1)} %get-tuple-element.133), channel_id=1, source_target_pairs={{8,0},{16,8},{24,16},{9,1},{17,9},{25,17},{10,2},{18,10},{26,18},{... | collective-permute-start | bytes 49160 | tf_op jit(solution)/shard_map/ppermute | solution.py:19
  206.3 26.8 %collective-permute-start.12 = (bf16[32,1,8,32]{0,3,2,1:T(8,128)(2,1)S(1)}, bf16[32,1,8,32]{0,3,2,1:T(8,128)(2,1)S(1)}, u32[]{:S(2)}, u32[]{:S(2)}) collective-permute-start(bf16[32,1,8,32]{0,3,2,1:T(8,128)(2,1)S(1)} %get-tuple-element.128), channel_id=1, source_target_pairs={{0,8},{8,16},{16,24},{1,9},{9,17},{17,25},{2,10},{10,18},{18,26},{... | collective-permute-start | bytes 49160 | tf_op jit(solution)/shard_map/ppermute | solution.py:17
  211.8 21.3 %collective-permute-start.13 = (bf16[32,1,8,32]{0,3,2,1:T(8,128)(2,1)S(1)}, bf16[32,1,8,32]{0,3,2,1:T(8,128)(2,1)S(1)}, u32[]{:S(2)}, u32[]{:S(2)}) collective-permute-start(bf16[32,1,8,32]{0,3,2,1:T(8,128)(2,1)S(1)} %get-tuple-element.129), channel_id=1, source_target_pairs={{8,0},{16,8},{24,16},{9,1},{17,9},{25,17},{10,2},{18,10},{26,18},{... | collective-permute-start | bytes 49160 | tf_op jit(solution)/shard_map/ppermute | solution.py:19
  228.0 5.2 copy-start.136
  228.1 11.3 %collective-permute-start.6 = (bf16[32,18,1,32]{0,3,2,1:T(8,128)(2,1)S(1)}, bf16[32,18,1,32]{0,3,2,1:T(8,128)(2,1)S(1)}, u32[]{:S(2)}, u32[]{:S(2)}) collective-permute-start(bf16[32,18,1,32]{0,3,2,1:T(8,128)(2,1)S(1)} %get-tuple-element.124), channel_id=1, source_target_pairs={{0,1},{1,2},{2,3},{3,4},{4,5},{5,6},{6,7},{8,9},{9,10},{10,11},{11... | collective-permute-start | bytes 110600 | tf_op jit(solution)/shard_map/ppermute | solution.py:17
  231.8 7.6 %collective-permute-start.7 = (bf16[32,18,1,32]{0,3,2,1:T(8,128)(2,1)S(1)}, bf16[32,18,1,32]{0,3,2,1:T(8,128)(2,1)S(1)}, u32[]{:S(2)}, u32[]{:S(2)}) collective-permute-start(bf16[32,18,1,32]{0,3,2,1:T(8,128)(2,1)S(1)} %get-tuple-element.125), channel_id=1, source_target_pairs={{1,0},{2,1},{3,2},{4,3},{5,4},{6,5},{7,6},{9,8},{10,9},{11,10},{12... | collective-permute-start | bytes 110600 | tf_op jit(solution)/shard_map/ppermute | solution.py:19
  233.2 24.3 %collective-permute-start.14 = (bf16[32,18,1,32]{0,3,2,1:T(8,128)(2,1)S(1)}, bf16[32,18,1,32]{0,3,2,1:T(8,128)(2,1)S(1)}, u32[]{:S(2)}, u32[]{:S(2)}) collective-permute-start(bf16[32,18,1,32]{0,3,2,1:T(8,128)(2,1)S(1)} %get-tuple-element.120), channel_id=1, source_target_pairs={{0,1},{1,2},{2,3},{3,4},{4,5},{5,6},{6,7},{8,9},{9,10},{10,11},{11... | collective-permute-start | bytes 110600 | tf_op jit(solution)/shard_map/ppermute | solution.py:17
  238.1 19.5 %collective-permute-start.15 = (bf16[32,18,1,32]{0,3,2,1:T(8,128)(2,1)S(1)}, bf16[32,18,1,32]{0,3,2,1:T(8,128)(2,1)S(1)}, u32[]{:S(2)}, u32[]{:S(2)}) collective-permute-start(bf16[32,18,1,32]{0,3,2,1:T(8,128)(2,1)S(1)} %get-tuple-element.121), channel_id=1, source_target_pairs={{1,0},{2,1},{3,2},{4,3},{5,4},{6,5},{7,6},{9,8},{10,9},{11,10},{12... | collective-permute-start | bytes 110600 | tf_op jit(solution)/shard_map/ppermute | solution.py:19
  266.6 8.6 %copy-start.58 = (bf16[32,16,272]{0,2,1:T(8,128)(2,1)S(1)}, bf16[32,16,272]{0,2,1:T(8,128)(2,1)}, u32[]{:S(2)}) copy-start(bf16[32,16,272]{0,2,1:T(8,128)(2,1)} %get-tuple-element.90) | copy-start | bytes 835588
  266.6 8.6 %copy-start.59 = (bf16[32,16,272]{0,2,1:T(8,128)(2,1)S(1)}, bf16[32,16,272]{0,2,1:T(8,128)(2,1)}, u32[]{:S(2)}) copy-start(bf16[32,16,272]{0,2,1:T(8,128)(2,1)} %get-tuple-element.91) | copy-start | bytes 835588
  266.6 8.6 %copy-start.60 = (bf16[32,16,272]{0,2,1:T(8,128)(2,1)S(1)}, bf16[32,16,272]{0,2,1:T(8,128)(2,1)}, u32[]{:S(2)}) copy-start(bf16[32,16,272]{0,2,1:T(8,128)(2,1)} %get-tuple-element.92) | copy-start | bytes 835588
  282.9 6.2 %copy-start.10 = (bf16[32,16,272]{0,2,1:T(8,128)(2,1)S(1)}, bf16[32,16,272]{0,2,1:T(8,128)(2,1)}, u32[]{:S(2)}) copy-start(bf16[32,16,272]{0,2,1:T(8,128)(2,1)} %get-tuple-element.85) | copy-start | bytes 835588
  (170 other events, 312.9 us)
Sparse Core Ops, SparseCore 0:
  394.7 136.0 all-reduce.16
where the time goes:
time: 550 us; the launch traced here: 542 us
  local copies, waits for them, and re-layouts  220 us (40%)
  waiting for transfers between devices  132 us (24%)
  other arithmetic  65.5 us (12%)
  matrix products  63.9 us (12%)
  starting transfers between devices  45 us (8%)
  between operations  16.1 us (3%)
    psum x1, waiting for transfers between devices, on_device(): lax.psum((weight_one, weight_two, down_grad), ('region', 'tile'))  132 us
    slice x8, local copies, waits for them, and re-layouts, stacked_taps(): lax.slice(flattened, (0, start_x, start_n), (chans, start_x + out_x, star...  50 us
    unnamed x374, local copies, waits for them, and re-layouts  45.5 us
    dot_general x18, other arithmetic, kernel_grad(): jnp.einsum('ixn,oxn->io', stacked, grad_flat, preferred_element_type=jnp....  44.7 us
    dot_general x18, local copies, waits for them, and re-layouts, kernel_grad(): jnp.einsum('ixn,oxn->io', stacked, grad_flat, preferred_element_type=jnp....  44.3 us
    ppermute x8, starting transfers between devices, with_halo(): lax.ppermute(tail, axis, [(i, (i + 1) % count) for i in range(ends)])  34.5 us
    dot_general x18, matrix products, spatial_conv(): jnp.einsum('oxn,oi->ixn', stacked, taps.transpose(0, 2, 1).reshape(-1, ta...  25.3 us
    dot_general x18, matrix products, spatial_conv(): jnp.einsum('ixn,io->oxn', stacked, taps.reshape(-1, taps.shape[2]), prefe...  24.8 us
  transfers between devices with their start and end apart: 17, of which 1 were waited for; matrix products, arithmetic and copies ran while one was open for 14% of the time, Pallas kernels for 0%

commit v1 on v0

v1 whole, which is shorter than its diff:
```python
import functools
import math

import jax
import jax.numpy as jnp
from jax import lax
from jax.experimental import pallas as pl
from jax.experimental.pallas import tpu as pltpu
from jax.sharding import PartitionSpec as P


BF = jnp.bfloat16
F32 = jnp.float32
I32 = jnp.int32
NN = (((1,), (0,)), ((), ()))
NT = (((1,), (1,)), ((), ()))
AXES = ("region", "tile")
VMEM_LIMIT = 56 * 1024 * 1024


def dot(lhs, rhs, dims=NN):
    return lax.dot_general(lhs, rhs, dims, preferred_element_type=F32)


def iota(shape, dim):
    return lax.broadcasted_iota(I32, shape, dim)


def parity_fields(v):
    return v & 1, (v >> 6) & 1, (v >> 3) & 1


def octant_rows(first=0):
    e = iota((8, 512), 0)
    d, a, b = parity_fields(iota((8, 512), 1))
    return (d == (e >> 2)) & (a == ((e >> 1) & 1)) & (b == (e & 1))


def row_codes():
    row = iota((512, 128), 0)
    code = ((row >> 6) & 3) * 16 + ((row >> 4) & 3) * 4 + (row & 3)
    cell = (row >> 8) * 4 + ((row >> 2) & 3)
    return code, cell


def place_fine(cell_ref, place):
    code, cell = row_codes()
    for q in range(4):
        code_q = jnp.where(cell == cell_ref[q], code, -1)
        for t in range(4):
            v = iota((1, 128), 1) + 128 * t
            vcode = (v >> 7) * 16 + ((v >> 4) & 3) * 4 + ((v >> 1) & 3)
            first = q * 512 + t * 128
            place[:, first : first + 128] = jnp.where(code_q == vcode, 1.0, 0.0).astype(BF)


def coarse_tile(cell_ref, t):
    code, cell = row_codes()
    lane = iota((512, 128), 1)
    wanted = jnp.where(lane < 64, cell_ref[2 * t], cell_ref[2 * t + 1])
    return jnp.where((cell == wanted) & (code == (lane & 63)), 1.0, 0.0).astype(BF)


def gather_kernel(cell_ref, feat_ref, vmask_ref, cot_ref, own, xlo, xhi, ylo, yhi, ll, lh, hl, hh, lhs, rhs):
    place_fine(cell_ref, lhs)
    for t in range(2):
        lhs[:, 2048 + t * 128 : 2048 + t * 128 + 128] = coarse_tile(cell_ref, t)
    match = octant_rows()
    for q in range(4):
        cols = slice(q * 512, q * 512 + 512)
        m8 = jnp.where(match, vmask_ref[q : q + 1, :].astype(F32), 0.0)
        x = feat_ref[q].astype(F32)
        for e in range(8):
            rhs[e * 32 : e * 32 + 32, cols] = (x * m8[e : e + 1, :]).astype(BF)
        rhs[256:320, cols] = jnp.zeros((64, 512), BF)
        rhs[320:336, cols] = jnp.concatenate([m8, jnp.zeros((8, 512), F32)], axis=0).astype(BF)
        rhs[336:384, cols] = jnp.zeros((48, 512), BF)
    rhs[0:256, 2048:2304] = jnp.zeros((256, 256), BF)
    rhs[256:320, 2048:2304] = cot_ref[...]
    rhs[320:384, 2048:2304] = jnp.zeros((64, 256), BF)
    field = dot(lhs[...], rhs[...], NT).astype(BF).reshape(8, 4, 16, 384)
    own[...] = field
    xlo[...] = field[0]
    xhi[...] = field[7]
    ylo[...] = field[:, 0]
    yhi[...] = field[:, 3]
    ll[...] = field[0, 0]
    lh[...] = field[0, 3]
    hl[...] = field[7, 0]
    hh[...] = field[7, 3]


def tap_of(far, source, target):
    position = source if far == 0 else (2 if source == 0 else -1)
    tap = position - target
    return tap if -1 <= tap <= 1 else None


def weights_kernel(w1_ref, w2_ref, dw_ref, big1, big1t, big2, big2t, down_mat, rep, tiles, tiles_t):
    lane = iota((32, 128), 1)
    spread = jnp.where((lane & 31) == iota((32, 128), 0), 1.0, 0.0).astype(BF)
    eye = jnp.where(iota((32, 32), 0) == iota((32, 32), 1), 1.0, 0.0).astype(BF)
    group = [jnp.where((lane >> 5) == g, 1.0, 0.0).astype(BF) for g in range(4)]
    for w_ref, big, big_t in ((w1_ref, big1, big1t), (w2_ref, big2, big2t)):
        tiles[...] = dot(w_ref[...], spread).astype(BF)
        w3 = w_ref[...].reshape(27, 32, 32)
        for j in range(4):
            rep[:, j] = w3
        tiles_t[...] = dot(eye, rep[...].reshape(27 * 128, 32), NT).astype(BF)
        for s in range(8):
            sx, sy, sz = s >> 2, (s >> 1) & 1, s & 1
            for e in range(8):
                d, a, b = e >> 2, (e >> 1) & 1, e & 1
                first = s * 256 + e * 32
                for td in range(2):
                    plain = None
                    turned = None
                    for g in range(4):
                        taps = (tap_of(sx, a, g >> 1), tap_of(sy, b, g & 1), tap_of(sz, d, td))
                        if None in taps:
                            continue
                        k = 9 * (taps[0] + 1) + 3 * (taps[1] + 1) + taps[2] + 1
                        back = 26 - k
                        term = tiles[k * 32 : k * 32 + 32, :] * group[g]
                        term_t = tiles_t[:, back * 128 : back * 128 + 128] * group[g]
                        plain = term if plain is None else plain + term
                        turned = term_t if turned is None else turned + term_t
                    zero = jnp.zeros((32, 128), BF)
                    big[first : first + 32, td * 128 : td * 128 + 128] = zero if plain is None else plain
                    big_t[first : first + 32, td * 128 : td * 128 + 128] = zero if turned is None else turned
    for e in range(8):
        d, a, b = e >> 2, (e >> 1) & 1, e & 1
        down_mat[e * 32 : e * 32 + 32, 0:64] = dw_ref[4 * a + 2 * b + d]
    down_mat[0:256, 64:128] = jnp.zeros((256, 64), BF)
    unit = iota((256, 128), 1) - 64 == (iota((256, 128), 0) >> 5)
    down_mat[256:512, :] = jnp.where(unit, 1.0, 0.0).astype(BF)


def lane_picks():
    lane = iota((16, 512), 1)
    low_a = jnp.where(((lane >> 6) & 1) == 0, 1.0, 0.0).astype(BF) > 0.5
    low_b = jnp.where(((lane >> 5) & 1) == 0, 1.0, 0.0).astype(BF) > 0.5
    return low_a[None], low_b[None]


def put_field(store, x, y0, value):
    ny = value.shape[0]
    z = iota((ny, 16, 128), 1)
    store[x, y0 : y0 + ny, :, 0:256] = value
    up = pltpu.roll(value[:, :, 0:128].astype(F32), 15, 1)
    store[x, y0 : y0 + ny, :, 256:384] = jnp.where(z == 15, 0.0, up).astype(BF)
    dn = pltpu.roll(value[:, :, 128:256].astype(F32), 1, 1)
    store[x, y0 : y0 + ny, :, 384:512] = jnp.where(z == 0, 0.0, dn).astype(BF)


def clear_edges(store):
    store[0] = jnp.zeros((8, 16, 512), BF)
    store[11] = jnp.zeros((8, 16, 512), BF)

    def edge(x, carry):
        store[x, 0] = jnp.zeros((16, 512), BF)
        store[x, 7] = jnp.zeros((16, 512), BF)
        return carry

    lax.fori_loop(1, 11, edge, 0)


def widen(store, wide, x, at, y0, ny, picks):
    low_a, low_b = picks
    low_a = jnp.broadcast_to(low_a, (ny, 16, 512))
    low_b = jnp.broadcast_to(low_b, (ny, 16, 512))

    def at_y(dx, dy):
        return store[x + dx, y0 + dy : y0 + dy + ny]

    wide[at, :, :, 0:512] = at_y(0, 0)
    wide[at, :, :, 512:1024] = jnp.where(low_b, at_y(0, 1), at_y(0, -1))
    wide[at, :, :, 1024:1536] = jnp.where(low_a, at_y(1, 0), at_y(-1, 0))
    upper = jnp.where(low_b, at_y(1, 1), at_y(1, -1))
    lower = jnp.where(low_b, at_y(-1, 1), at_y(-1, -1))
    wide[at, :, :, 1536:2048] = jnp.where(low_a, upper, lower)


def fold_taps(products, terms, first_tap, held):
    lane = iota((32, 128), 1)
    for k in range(27):
        tap = (k // 9 - 1, k // 3 % 3 - 1, k % 3 - 1)
        total = None
        for g in range(4):
            part = None
            for td in range(2):
                far, source, target = [], [], []
                for t, parity in ((tap[0], g >> 1), (tap[1], g & 1)):
                    b = parity if t == 0 else 1 - parity
                    far.append(0 if 0 <= b + t <= 1 else 1)
                    target.append(b)
                pos = td + tap[2]
                far_z = 0 if 0 <= pos <= 1 else 1
                source_d = pos & 1
                s = far[0] * 4 + far[1] * 2 + far_z
                rows = (td * 4 + target[0] * 2 + target[1]) * 32
                cols = s * 256 + source_d * 128
                block = products[rows : rows + 32, cols : cols + 128]
                part = block if part is None else part + block
            total = part if total is None else jnp.where((lane >> 5) == g, part, total)
        total = total + pltpu.roll(total, 64, 1)
        total = total + pltpu.roll(total, 32, 1)
        slot = (first_tap + k) % 4
        held = total if held is None else jnp.where((lane >> 5) == slot, total, held)
        if slot == 3:
            row = (first_tap + k) // 4 * 32
            terms[row : row + 32, :] = held.astype(terms.dtype)
            held = None
    return held


def main_kernel(own, xlo, xhi, ylo, yhi, ll, lh, hl, hh, big1, big2, big2t, down_mat,
                terms, fg_out, bkm_out, mask_out, sum_out,
                field, ex, eg, eh, mk, ax, ag, ah, turned, products):
    picks = lane_picks()
    field[1:9, 1:5] = own[...]
    field[0, 1:5] = xlo[...]
    field[9, 1:5] = xhi[...]
    field[1:9, 0] = ylo[...]
    field[1:9, 5] = yhi[...]
    field[0, 0] = ll[...]
    field[0, 5] = lh[...]
    field[9, 0] = hl[...]
    field[9, 5] = hh[...]
    for store in (ex, eg, eh):
        clear_edges(store)

    def start(x, carry):
        row = field[x]
        put_field(ex, x + 1, 1, row[:, :, 0:256])
        both = dot(row[:, :, 256:384].reshape(96, 128), down_mat[...], NT)
        mask = both[:, 256:512]
        bkm = both[:, 0:256] * mask
        mk[x] = mask.astype(BF).reshape(6, 16, 256)
        products[pl.ds(pl.multiple_of(x * 96, 32), 96), 0:256] = bkm
        put_field(eg, x + 1, 1, bkm.astype(BF).reshape(6, 16, 256))
        return carry

    lax.fori_loop(0, 10, start, 0)

    def save(x, carry):
        bkm_out[x] = products[pl.ds(pl.multiple_of((x + 1) * 96 + 16, 16), 64), 0:256].reshape(4, 16, 256)
        mask_out[x] = mk[x + 1, 1:5]
        return carry

    lax.fori_loop(0, 8, save, 0)

    def first(i, carry):
        for j in range(2):
            widen(ex, ax, 2 * i + j + 1, 2 * i + j, 1, 6, picks)
            widen(eg, ag, 2 * i + j + 1, j, 1, 6, picks)
        mask = mk[pl.ds(2 * i, 2)].reshape(192, 256).astype(F32)
        pre = dot(ax[pl.ds(2 * i, 2)].reshape(192, 2048), big1[...]) * mask
        spread = dot(ag[...].reshape(192, 2048), big2t[...])
        s = jax.nn.sigmoid(pre)
        hidden = (pre * s).astype(BF).reshape(2, 6, 16, 256)
        grad = (spread * s * (1.0 + pre * (1.0 - s)) * mask).astype(BF).reshape(2, 6, 16, 256)
        for j in range(2):
            put_field(eh, 2 * i + j + 1, 1, hidden[j])
            fg_out[2 * i + j] = grad[j]
        return carry

    lax.fori_loop(0, 5, first, 0)

    def second(i, carry):
        for j in range(4):
            widen(eh, ah, 4 * i + j + 2, 4 * i + j, 2, 4, picks)
        pre = dot(ah[pl.ds(4 * i, 4)].reshape(256, 2048), big2[...])
        mask = mk[pl.ds(4 * i + 1, 4), 1:5].reshape(256, 256).astype(F32)
        inputs = field[pl.ds(4 * i + 1, 4), 1:5, :, 0:256].reshape(256, 256).astype(F32)
        summed = (inputs + pre * mask).astype(BF)
        sum_out[pl.ds(pl.multiple_of(256 * i, 256), 256), :] = summed
        return carry

    lax.fori_loop(0, 2, second, 0)

    held = None
    for source, grads in ((1, fg_out[1:9, 1:5]), (2, eg[2:10, 2:6, :, 0:256])):
        turned[...] = grads.reshape(512, 256).astype(F32).T.astype(BF)
        for s in range(8):
            cols = slice(s * 256, s * 256 + 256)
            wide = (ax[1:9, 1:5, :, cols] if source == 1 else ah[:, :, :, cols]).reshape(512, 256)
            products[0:256, cols] = dot(turned[...], wide)
        held = fold_taps(products, terms, 27 * (source - 1), held)
    terms[416:448, :] = held.astype(terms.dtype)
    cot = field[1:9, 1:5, :, 256:384].reshape(512, 128).astype(F32).T.astype(BF)
    grad_down = dot(cot, sum_out[...])
    terms[448:512, :] = grad_down[0:64, 0:128].astype(terms.dtype)
    terms[512:576, :] = grad_down[0:64, 128:256].astype(terms.dtype)
    rest = terms.shape[0] - 576
    if rest:
        terms[576:, :] = jnp.zeros((rest, 128), terms.dtype)


def tail_kernel(cell_ref, fg, bkm, mask, summed, big1t, down_mat, grad_features, down, ef, af, place, dense):
    picks = lane_picks()
    clear_edges(ef)

    def start(x, carry):
        put_field(ef, x + 1, 1, fg[x])
        return carry

    lax.fori_loop(0, 10, start, 0)

    def last(i, carry):
        for j in range(4):
            widen(ef, af, 4 * i + j + 2, j, 2, 4, picks)
        spread = dot(af[...].reshape(256, 2048), big1t[...])
        rows = pl.ds(4 * i, 4)
        grad = bkm[rows].reshape(256, 256) + spread * mask[rows].reshape(256, 256).astype(F32)
        dense[pl.ds(pl.multiple_of(256 * i, 256), 256), :] = grad.astype(BF)
        return carry

    lax.fori_loop(0, 2, last, 0)
    place_fine(cell_ref, place)
    turned = dense[...].astype(F32).T.astype(BF)
    pick = jnp.where(octant_rows(), 1.0, 0.0)
    for q in range(4):
        moved = dot(turned, place[:, q * 512 : q * 512 + 512])
        total = moved[0:32] * pick[0:1]
        for e in range(1, 8):
            total = total + moved[e * 32 : e * 32 + 32] * pick[e : e + 1]
        grad_features[q] = total.astype(BF)
    lowered = dot(summed[...], down_mat[0:256, :]).T.astype(BF)
    for t in range(2):
        moved = dot(lowered, coarse_tile(cell_ref, t))
        down[:, t * 128 : t * 128 + 128] = moved[0:64].astype(BF)


def reduce_kernel(parts, out):
    count = parts.shape[0]
    total = parts[0].astype(F32)
    for i in range(1, count):
        total = total + parts[i].astype(F32)
    total = total.astype(out.dtype)
    for i in range(count):
        out[i] = total


def finish_kernel(scale, sums, one, two, down):
    for m in range(14):
        block = (sums[m * 32 : m * 32 + 32, :].astype(F32) * scale).T
        for g in range(4):
            k = 4 * m + g
            if k < 27:
                one[k] = block[g * 32 : g * 32 + 32]
            elif k < 54:
                two[k - 27] = block[g * 32 : g * 32 + 32]
    for half in range(2):
        block = (sums[448 + 64 * half : 512 + 64 * half, :].astype(F32) * scale).T
        for g in range(4):
            down[4 * (g >> 1) + 2 * (g & 1) + half] = block[g * 32 : g * 32 + 32]


def vmem_call(kernel, outs, ins, scratch=(), smem_first=False, flops=0):
    specs = [pl.BlockSpec(memory_space=pltpu.VMEM) for _ in ins]
    if smem_first:
        specs[0] = pl.BlockSpec(memory_space=pltpu.SMEM)
    moved = sum(math.prod(x.shape) * x.dtype.itemsize for x in tuple(ins) + tuple(outs))
    return pl.pallas_call(
        kernel,
        out_shape=tuple(outs),
        in_specs=specs,
        out_specs=tuple(pl.BlockSpec(memory_space=pltpu.VMEM) for _ in outs),
        scratch_shapes=list(scratch),
        compiler_params=pltpu.CompilerParams(vmem_limit_bytes=VMEM_LIMIT),
        cost_estimate=pl.CostEstimate(flops=flops, bytes_accessed=moved, transcendentals=0),
    )(*ins)


def bf(*shape):
    return jax.ShapeDtypeStruct(shape, BF)


def f32(*shape):
    return jax.ShapeDtypeStruct(shape, F32)


def neighbours(regions, tiles, dx, dy):
    pairs = []
    for r in range(regions):
        for t in range(tiles):
            if 0 <= r + dx < regions and 0 <= t + dy < tiles:
                pairs.append(((r + dx) * tiles + t + dy, r * tiles + t))
    return pairs


def on_device(features, voxel_mask, brick_cell, conv_one, conv_two, down_weight, cotangent):
    regions, tiles = lax.axis_size("region"), lax.axis_size("tile")
    devices = regions * tiles
    slots = features.shape[0]
    cot = cotangent.reshape(slots, 64, 64).transpose(1, 0, 2).reshape(64, slots * 64)
    pieces = vmem_call(
        gather_kernel,
        [bf(8, 4, 16, 384), bf(4, 16, 384), bf(4, 16, 384), bf(8, 16, 384), bf(8, 16, 384)] + [bf(16, 384)] * 4,
        (brick_cell, features, voxel_mask, cot),
        [pltpu.VMEM((512, 2304), BF), pltpu.VMEM((384, 2304), BF)],
        smem_first=True,
        flops=2 * 512 * 2304 * 384,
    )
    own, xlo, xhi, ylo, yhi, ll, lh, hl, hh = pieces

    def fetch(piece, dx, dy):
        return lax.ppermute(piece, AXES, neighbours(regions, tiles, dx, dy))

    halos = (
        fetch(xhi, -1, 0), fetch(xlo, 1, 0), fetch(yhi, 0, -1), fetch(ylo, 0, 1),
        fetch(hh, -1, -1), fetch(hl, -1, 1), fetch(lh, 1, -1), fetch(ll, 1, 1),
    )
    big1, big1t, big2, big2t, down_mat = vmem_call(
        weights_kernel,
        [bf(2048, 256)] * 4 + [bf(512, 128)],
        (conv_one.reshape(864, 32), conv_two.reshape(864, 32), down_weight),
        [pltpu.VMEM((27, 4, 32, 32), BF), pltpu.VMEM((864, 128), BF), pltpu.VMEM((32, 3456), BF)],
        flops=2 * 2 * 32 * 3456 * 256,
    )
    chunk = -(-(-(-576 // devices)) // 8) * 8
    terms, fg, bkm, mask, summed = vmem_call(
        main_kernel,
        [bf(devices * chunk, 128), bf(10, 6, 16, 256), f32(8, 4, 16, 256), bf(8, 4, 16, 256), bf(512, 256)],
        (own,) + halos + (big1, big2, big2t, down_mat),
        [
            pltpu.VMEM((10, 6, 16, 384), BF),
            pltpu.VMEM((12, 8, 16, 512), BF),
            pltpu.VMEM((12, 8, 16, 512), BF),
            pltpu.VMEM((12, 8, 16, 512), BF),
            pltpu.VMEM((10, 6, 16, 256), BF),
            pltpu.VMEM((10, 6, 16, 2048), BF),
            pltpu.VMEM((2, 6, 16, 2048), BF),
            pltpu.VMEM((8, 4, 16, 2048), BF),
            pltpu.VMEM((256, 512), BF),
            pltpu.VMEM((960, 2048), F32),
        ],
        flops=2 * 2048 * 256 * (960 * 2 + 512 * 3),
    )
    parts = lax.all_to_all(terms.reshape(devices, chunk, 128), AXES, 0, 0, tiled=True)
    (total,) = vmem_call(reduce_kernel, [f32(devices, chunk, 128)], (parts,))
    sums = lax.all_to_all(total, AXES, 0, 0, tiled=True)
    grad_features, down = vmem_call(
        tail_kernel,
        [bf(slots, 32, 512), bf(64, slots * 64)],
        (brick_cell, fg, bkm, mask, summed, big1t, down_mat),
        [
            pltpu.VMEM((12, 8, 16, 512), BF),
            pltpu.VMEM((4, 4, 16, 2048), BF),
            pltpu.VMEM((512, 2048), BF),
            pltpu.VMEM((512, 256), BF),
        ],
        smem_first=True,
        flops=2 * 2048 * 512 * 512,
    )
    down = down.reshape(64, slots, 64).transpose(1, 0, 2).reshape(slots, 4096)
    scale = 1.0 / math.sqrt(devices * slots * 512.0)
    grad_one, grad_two, grad_down = vmem_call(
        functools.partial(finish_kernel, scale),
        [f32(27, 32, 32), f32(27, 32, 32), f32(8, 32, 64)],
        (sums.reshape(devices * chunk, 128),),
    )
    return down, grad_features, grad_one, grad_two, grad_down


def solution(mesh):
    in_specs = (
        P(AXES, None, None),
        P(AXES, None),
        P(AXES),
        P(),
        P(),
        P(),
        P(AXES, None),
    )
    out_specs = (P(AXES, None), P(AXES, None, None), P(), P(), P())
    return jax.shard_map(
        on_device, mesh=mesh, in_specs=in_specs, out_specs=out_specs, check_vma=False
    )
```

time: 550 us -> 89.5 us (0.16); the launches traced: 542 us -> 88.8 us
  local copies, waits for them, and re-layouts: 220 us -> 4.68 us
  waiting for transfers between devices: 132 us -> 18.7 us
  other arithmetic: 65.5 us -> 0 us
  matrix products: 63.9 us -> 0 us
  Pallas kernels: 0 us -> 27.1 us
  starting transfers between devices: 45 us -> 20.1 us
  blocking collectives: 0 us -> 17.3 us
  between operations: 16.1 us -> 0.84 us
    psum x1 -> x0, waiting for transfers between devices: 132 us -> none  [on_device(): lax.psum((weight_one, weight_two, down_grad), ('region', 'tile'))]
    dot_general x57 -> x0, matrix products: 63.9 us -> none  [the longest x18 25.3 us: spatial_conv(): jnp.einsum('oxn,oi->ixn', stacked, taps.transpose(0, 2, 1).reshape(-1, ta...]
    slice x16 -> x0, local copies, waits for them, and re-layouts: 57.9 us -> none  [the longest x8 50 us: stacked_taps(): lax.slice(flattened, (0, start_x, start_n), (chans, start_x + out_x, star...]
    dot_general x18 -> x0, other arithmetic: 44.7 us -> none  [kernel_grad(): jnp.einsum('ixn,oxn->io', stacked, grad_flat, preferred_element_type=jnp....]
    dot_general x18 -> x0, local copies, waits for them, and re-layouts: 44.3 us -> none  [kernel_grad(): jnp.einsum('ixn,oxn->io', stacked, grad_flat, preferred_element_type=jnp....]
    unnamed x374 -> x20, local copies, waits for them, and re-layouts: 45.5 us -> 1.42 us
    reshape x35 -> x5, local copies, waits for them, and re-layouts: 41.7 us -> 3.24 us  [the longest x3 1.66 us: on_device(): cotangent.reshape(slots, 64, 64).transpose(1, 0, 2).reshape(64, slots * 64)]
    ppermute x16 -> x8, starting transfers between devices: 45 us -> 17.4 us  [fetch(): return lax.ppermute(piece, AXES, neighbours(regions, tiles, dx, dy))]
  transfers between devices with their start and end apart: 17 -> 9, of which waited for: 1 -> 2; matrix products, arithmetic and copies ran while one was open for 14% -> 2% of each run, Pallas kernels for 0% -> 10%
where the time goes in v1:
time: 89.5 us; the launch traced here: 88.8 us
  Pallas kernels  27.1 us (30%)
  starting transfers between devices  20.1 us (22%)
  waiting for transfers between devices  18.7 us (21%)
  blocking collectives  17.3 us (19%)
  local copies, waits for them, and re-layouts  4.68 us (5%)
    pallas_call x6, Pallas kernels, vmem_call(): pl.pallas_call(kernel, out_shape=tuple(outs), in_specs=specs, out_specs=t...  27.1 us
    ppermute x8, starting transfers between devices, fetch(): return lax.ppermute(piece, AXES, neighbours(regions, tiles, dx, dy))  17.4 us
    all_to_all x1, blocking collectives, on_device(): lax.all_to_all(terms.reshape(devices, chunk, 128), AXES, 0, 0, tiled=True)  17.3 us
    ppermute x8, waiting for transfers between devices, fetch(): return lax.ppermute(piece, AXES, neighbours(regions, tiles, dx, dy))  12 us
    all_to_all x1, waiting for transfers between devices, on_device(): sums = lax.all_to_all(total, AXES, 0, 0, tiled=True)  6.7 us
    all_to_all x1, starting transfers between devices, on_device(): sums = lax.all_to_all(total, AXES, 0, 0, tiled=True)  2.72 us
  transfers between devices with their start and end apart: 9, of which 2 were waited for; matrix products, arithmetic and copies ran while one was open for 2% of the time, Pallas kernels for 10%

profile of v1, /device:TPU:0, one launch (start us, length us, event | category | flops | bytes accessed | tf_op | source)
XLA Modules:
  0.0 88.8 jit_solution(2546736236015695861)
XLA Ops:
  0.6 0.9 reshape.34
  1.5 0.1 copy.15
  1.6 0.7 reshape.35.cot_ref
  2.3 3.3 %shard_map.110 = (bf16[8,4,16,384]{3,2,1,0:T(8,128)(2,1)}, bf16[4,16,384]{2,1,0:T(8,128)(2,1)}, bf16[4,16,384]{2,1,0:T(8,128)(2,1)}, bf16[8,16,384]{2,1,0:T(8,12...) custom-call(s32[4]{0:T(128)} %cell_ref.3, ...), custom_call_target="tpu_custom_call" | custom-call | flops 905969664 | bytes 909328 | tf_op jit(solution)/shard_map/pallas_call | solution.py:365
  5.6 2.5 %collective-permute-start.2 = (bf16[8,16,384]{2,1,0:T(8,128)(2,1)}, bf16[8,16,384]{2,1,0:T(8,128)(2,1)S(1)}, u32[]{:S(2)}, u32[]{:S(2)}) collective-permute-start(bf16[8,16,384]{2,1,0:T(8,128)(2,1)} %get-tuple-element.32), channel_id=1, source_target_pairs={{0,1},{1,2},{2,3},{3,4},{4,5},{5,6},{6,7},{8,9},{9,10},{10,11},{11... | collective-permute-start | bytes 294920 | tf_op jit(solution)/shard_map/ppermute | solution.py:409
  8.1 1.3 %collective-permute-start.3 = (bf16[8,16,384]{2,1,0:T(8,128)(2,1)}, bf16[8,16,384]{2,1,0:T(8,128)(2,1)S(1)}, u32[]{:S(2)}, u32[]{:S(2)}) collective-permute-start(bf16[8,16,384]{2,1,0:T(8,128)(2,1)} %get-tuple-element.33), channel_id=1, source_target_pairs={{1,0},{2,1},{3,2},{4,3},{5,4},{6,5},{7,6},{9,8},{10,9},{11,10},{12... | collective-permute-start | bytes 294920 | tf_op jit(solution)/shard_map/ppermute | solution.py:409
  9.4 6.3 %collective-permute-start.4 = (bf16[16,384]{1,0:T(8,128)(2,1)}, bf16[16,384]{1,0:T(8,128)(2,1)S(1)}, u32[]{:S(2)}, u32[]{:S(2)}) collective-permute-start(bf16[16,384]{1,0:T(8,128)(2,1)} %get-tuple-element.34), channel_id=1, source_target_pairs={{0,9},{1,10},{2,11},{3,12},{4,13},{5,14},{6,15},{8,17},{9,18},{10,... | collective-permute-start | bytes 36872 | tf_op jit(solution)/shard_map/ppermute | solution.py:409
  15.7 3.4 %collective-permute-start = (bf16[4,16,384]{2,1,0:T(8,128)(2,1)}, bf16[4,16,384]{2,1,0:T(8,128)(2,1)S(1)}, u32[]{:S(2)}, u32[]{:S(2)}) collective-permute-start(bf16[4,16,384]{2,1,0:T(8,128)(2,1)} %get-tuple-element.30), channel_id=1, source_target_pairs={{0,8},{1,9},{2,10},{3,11},{4,12},{5,13},{6,14},{7,15},{8,16},{9,17... | collective-permute-start | bytes 147464 | tf_op jit(solution)/shard_map/ppermute | solution.py:409
  19.1 1.3 %collective-permute-start.1 = (bf16[4,16,384]{2,1,0:T(8,128)(2,1)}, bf16[4,16,384]{2,1,0:T(8,128)(2,1)S(1)}, u32[]{:S(2)}, u32[]{:S(2)}) collective-permute-start(bf16[4,16,384]{2,1,0:T(8,128)(2,1)} %get-tuple-element.31), channel_id=1, source_target_pairs={{8,0},{9,1},{10,2},{11,3},{12,4},{13,5},{14,6},{15,7},{16,8},{17,9... | collective-permute-start | bytes 147464 | tf_op jit(solution)/shard_map/ppermute | solution.py:409
  20.4 0.0 collective-permute-done.4.ll
  20.4 0.0 copy-start.5
  20.4 0.7 collective-permute-start.5
  21.1 0.7 collective-permute-start.6
  21.8 1.3 %collective-permute-start.7 = (bf16[16,384]{1,0:T(8,128)(2,1)S(1)}, bf16[16,384]{1,0:T(8,128)(2,1)S(1)}, u32[]{:S(2)}, u32[]{:S(2)}) collective-permute-start(bf16[16,384]{1,0:T(8,128)(2,1)S(1)} %copy-done.6), channel_id=1, source_target_pairs={{9,0},{10,1},{11,2},{12,3},{13,4},{14,5},{15,6},{17,8},{18,9},{19,... | collective-permute-start | bytes 36872 | tf_op jit(solution)/shard_map/ppermute | solution.py:409
  23.1 4.1 %shard_map.111 = (bf16[2048,256]{1,0:T(8,128)(2,1)}, bf16[2048,256]{1,0:T(8,128)(2,1)}, bf16[2048,256]{1,0:T(8,128)(2,1)}, bf16[2048,256]{1,0:T(8,128)(2,1)}, bf16[512,128]{1,0:T(8,128)(2,1)}) custom-call(bf16[864,32]{1,0:T(8,128)(2,1)} %bitcast.11, bf16[864,32]{1,0:T(8,128)(2,1)} %bitcast.12, bf16[8,32,64]{2,1,0:T(8,128)(2,1)} %dw_ref.1), custom_call_target="tpu_custom_call" | custom-call | flops 113246208 | bytes 4468736 | tf_op jit(solution)/shard_map/pallas_call | solution.py:365
  27.2 12.0 %collective-permute-done.7.hh = bf16[16,384]{1,0:T(8,128)(2,1)S(1)} collective-permute-done((bf16[16,384]{1,0:T(8,128)(2,1)S(1)}, bf16[16,384]{1,0:T(8,128)(2,1)S(1)}, u32[]{:S(2)}, u32[]{:S(2)}) %collective-permute-start.7) | collective-permute-done | bytes 12320 | tf_op jit(solution)/shard_map/ppermute | solution.py:409
  39.2 0.0 copy-start.2
  39.3 0.5 copy-done.9
  39.8 0.0 copy-done.3
  39.8 0.0 copy-done.4
  39.8 0.0 copy-done.1
  39.9 0.0 copy-done.2
  39.9 10.7 %shard_map.112 = (bf16[768,128]{1,0:T(8,128)(2,1)}, bf16[10,6,16,256]{3,2,1,0:T(8,128)(2,1)}, f32[8,4,16,256]{3,2,1,0:T(8,128)}, bf16[8,4,16,256]{3,2,1,0:T(8,128)(2,1)}, bf16[512,256]{1,0:T(8,128)(2,1)}) custom-call(bf16[8,4,16,384]{3,2,1,0:T(8,128)(2,1)} %get-tuple-element.29.own, bf16[4,16,384]{2,1,0:T(8,128)(2,1)} %copy-done.3, ...), custom_call_target="tpu_custom_call" | custom-call | flops 3623878656 | bytes 5750784 | tf_op jit(solution)/shard_map/pallas_call | solution.py:365
  50.6 17.3 %all_to_all.10.parts = bf16[32,24,128]{2,1,0:T(8,128)(2,1)} all-to-all(bf16[32,24,128]{2,1,0:T(8,128)(2,1)} %bitcast.13), channel_id=1, replica_groups=mesh['region'=4,'tile'=8] {'region','tile'}, dimensions={0} | all-to-all | bytes 393216 | tf_op jit(solution)/shard_map/all_to_all | solution.py:441
  67.9 1.7 %shard_map.114 = f32[32,24,128]{2,1,0:T(8,128)} custom-call(bf16[32,24,128]{2,1,0:T(8,128)(2,1)} %all_to_all.10.parts), custom_call_target="tpu_custom_call" | custom-call | bytes 589824 | tf_op jit(solution)/shard_map/pallas_call | solution.py:365
  69.6 2.7 %all-to-all-start.1 = ((f32[32,24,128]{2,1,0:T(8,128)}), f32[32,24,128]{2,1,0:T(8,128)S(1)}, u32[]{:S(2)}, u32[]{:S(2)}) async-start(f32[32,24,128]{2,1,0:T(8,128)} %shard_map.114), calls=%async_computation.1 | async-start | bytes 786432 | tf_op jit(solution)/shard_map/all_to_all | solution.py:443
  72.3 5.2 %shard_map.113 = (bf16[4,32,512]{2,1,0:T(8,128)(2,1)}, bf16[64,256]{1,0:T(8,128)(2,1)}) custom-call(s32[4]{0:T(128)} %cell_ref.3, bf16[10,6,16,256]{3,2,1,0:T(8,128)(2,1)} %get-tuple-element.42.fg, f32[8,4,16,256]{3,2,1,0:T(8,128)} %get-tuple-element.43.bkm, bf16[8,4,16,256]{3,2,1,0:T(8,128)(2,1)} %get-tuple-element.44.mask, ...), custom_call_target="tpu_custom_call" | custom-call | flops 1073741824 | bytes 2883600 | tf_op jit(solution)/shard_map/pallas_call | solution.py:365
  77.6 0.9 reshape.38
  78.4 0.7 reshape.39
  79.2 6.7 %all-to-all-done.1 = f32[32,24,128]{2,1,0:T(8,128)S(1)} async-done(((f32[32,24,128]{2,1,0:T(8,128)}), f32[32,24,128]{2,1,0:T(8,128)S(1)}, u32[]{:S(2)}, u32[]{:S(2)}) %all-to-all-start.1) | async-done | bytes 393248 | tf_op jit(solution)/shard_map/all_to_all | solution.py:443
  85.9 0.7 copy-done
  86.6 2.1 %shard_map.115 = (f32[27,32,32]{2,1,0:T(8,128)}, f32[27,32,32]{2,1,0:T(8,128)}, f32[8,32,64]{2,1,0:T(8,128)}) custom-call(f32[768,128]{1,0:T(8,128)} %bitcast.8), custom_call_target="tpu_custom_call" | custom-call | bytes 679936 | tf_op jit(solution)/shard_map/pallas_call | solution.py:365
  (19 shorter events, 0.1 us)
Async XLA Ops:
  5.6 16.2 %copy-start.6 = (bf16[16,384]{1,0:T(8,128)(2,1)S(1)}, bf16[16,384]{1,0:T(8,128)(2,1)}, u32[]{:S(2)}) copy-start(bf16[16,384]{1,0:T(8,128)(2,1)} %get-tuple-element.37) | copy-start | bytes 36868
  5.6 33.6 %collective-permute-start.2 = (bf16[8,16,384]{2,1,0:T(8,128)(2,1)}, bf16[8,16,384]{2,1,0:T(8,128)(2,1)S(1)}, u32[]{:S(2)}, u32[]{:S(2)}) collective-permute-start(bf16[8,16,384]{2,1,0:T(8,128)(2,1)} %get-tuple-element.32), channel_id=1, source_target_pairs={{0,1},{1,2},{2,3},{3,4},{4,5},{5,6},{6,7},{8,9},{9,10},{10,11},{11... | collective-permute-start | bytes 294920 | tf_op jit(solution)/shard_map/ppermute | solution.py:409
  8.1 31.2 %collective-permute-start.3 = (bf16[8,16,384]{2,1,0:T(8,128)(2,1)}, bf16[8,16,384]{2,1,0:T(8,128)(2,1)S(1)}, u32[]{:S(2)}, u32[]{:S(2)}) collective-permute-start(bf16[8,16,384]{2,1,0:T(8,128)(2,1)} %get-tuple-element.33), channel_id=1, source_target_pairs={{1,0},{2,1},{3,2},{4,3},{5,4},{6,5},{7,6},{9,8},{10,9},{11,10},{12... | collective-permute-start | bytes 294920 | tf_op jit(solution)/shard_map/ppermute | solution.py:409
  9.4 11.0 %collective-permute-start.4 = (bf16[16,384]{1,0:T(8,128)(2,1)}, bf16[16,384]{1,0:T(8,128)(2,1)S(1)}, u32[]{:S(2)}, u32[]{:S(2)}) collective-permute-start(bf16[16,384]{1,0:T(8,128)(2,1)} %get-tuple-element.34), channel_id=1, source_target_pairs={{0,9},{1,10},{2,11},{3,12},{4,13},{5,14},{6,15},{8,17},{9,18},{10,... | collective-permute-start | bytes 36872 | tf_op jit(solution)/shard_map/ppermute | solution.py:409
  15.7 23.5 %collective-permute-start = (bf16[4,16,384]{2,1,0:T(8,128)(2,1)}, bf16[4,16,384]{2,1,0:T(8,128)(2,1)S(1)}, u32[]{:S(2)}, u32[]{:S(2)}) collective-permute-start(bf16[4,16,384]{2,1,0:T(8,128)(2,1)} %get-tuple-element.30), channel_id=1, source_target_pairs={{0,8},{1,9},{2,10},{3,11},{4,12},{5,13},{6,14},{7,15},{8,16},{9,17... | collective-permute-start | bytes 147464 | tf_op jit(solution)/shard_map/ppermute | solution.py:409
  19.1 20.1 %collective-permute-start.1 = (bf16[4,16,384]{2,1,0:T(8,128)(2,1)}, bf16[4,16,384]{2,1,0:T(8,128)(2,1)S(1)}, u32[]{:S(2)}, u32[]{:S(2)}) collective-permute-start(bf16[4,16,384]{2,1,0:T(8,128)(2,1)} %get-tuple-element.31), channel_id=1, source_target_pairs={{8,0},{9,1},{10,2},{11,3},{12,4},{13,5},{14,6},{15,7},{16,8},{17,9... | collective-permute-start | bytes 147464 | tf_op jit(solution)/shard_map/ppermute | solution.py:409
  20.4 6.8 %copy-start.5 = (bf16[16,384]{1,0:T(8,128)(2,1)}, bf16[16,384]{1,0:T(8,128)(2,1)S(1)}, u32[]{:S(2)}) copy-start(bf16[16,384]{1,0:T(8,128)(2,1)S(1)} %collective-permute-done.4.ll) | copy-start | bytes 36868
  20.4 0.7 collective-permute-start.5
  21.1 6.1 %copy-start.7 = (bf16[16,384]{1,0:T(8,128)(2,1)}, bf16[16,384]{1,0:T(8,128)(2,1)S(1)}, u32[]{:S(2)}) copy-start(bf16[16,384]{1,0:T(8,128)(2,1)S(1)} %collective-permute-done.5.lh) | copy-start | bytes 36868
  21.1 0.7 collective-permute-start.6
  21.8 5.4 %copy-start.8 = (bf16[16,384]{1,0:T(8,128)(2,1)}, bf16[16,384]{1,0:T(8,128)(2,1)S(1)}, u32[]{:S(2)}) copy-start(bf16[16,384]{1,0:T(8,128)(2,1)S(1)} %collective-permute-done.6.hl) | copy-start | bytes 36868
  21.8 17.4 %collective-permute-start.7 = (bf16[16,384]{1,0:T(8,128)(2,1)S(1)}, bf16[16,384]{1,0:T(8,128)(2,1)S(1)}, u32[]{:S(2)}, u32[]{:S(2)}) collective-permute-start(bf16[16,384]{1,0:T(8,128)(2,1)S(1)} %copy-done.6), channel_id=1, source_target_pairs={{9,0},{10,1},{11,2},{12,3},{13,4},{14,5},{15,6},{17,8},{18,9},{19,... | collective-permute-start | bytes 36872 | tf_op jit(solution)/shard_map/ppermute | solution.py:409
  39.2 0.6 copy-start.9
  39.2 0.6 copy-start.3
  39.2 0.6 copy-start.4
  39.2 0.7 copy-start.1
  39.2 0.7 copy-start.2
  69.6 16.3 %all-to-all-start.1 = ((f32[32,24,128]{2,1,0:T(8,128)}), f32[32,24,128]{2,1,0:T(8,128)S(1)}, u32[]{:S(2)}, u32[]{:S(2)}) async-start(f32[32,24,128]{2,1,0:T(8,128)} %shard_map.114), calls=%async_computation.1 | async-start | bytes 786432 | tf_op jit(solution)/shard_map/all_to_all | solution.py:443
  85.9 0.8 copy-start

commit v2 on v1

--- a/solution.py
+++ b/solution.py
@@ -15,7 +15,6 @@
 NN = (((1,), (0,)), ((), ()))
 NT = (((1,), (1,)), ((), ()))
 AXES = ("region", "tile")
-VMEM_LIMIT = 56 * 1024 * 1024
 
 
 def dot(lhs, rhs, dims=NN):
@@ -61,7 +60,7 @@
     return jnp.where((cell == wanted) & (code == (lane & 63)), 1.0, 0.0).astype(BF)
 
 
-def gather_kernel(cell_ref, feat_ref, vmask_ref, cot_ref, own, xlo, xhi, ylo, yhi, ll, lh, hl, hh, lhs, rhs):
+def gather_kernel(cell_ref, feat_ref, vmask_ref, cot_ref, own, faces, ylo, yhi, lhs, rhs, shuffle):
     place_fine(cell_ref, lhs)
     for t in range(2):
         lhs[:, 2048 + t * 128 : 2048 + t * 128 + 128] = coarse_tile(cell_ref, t)
@@ -76,18 +75,48 @@
         rhs[320:336, cols] = jnp.concatenate([m8, jnp.zeros((8, 512), F32)], axis=0).astype(BF)
         rhs[336:384, cols] = jnp.zeros((48, 512), BF)
     rhs[0:256, 2048:2304] = jnp.zeros((256, 256), BF)
-    rhs[256:320, 2048:2304] = cot_ref[...]
+    for j in range(32):
+        shuffle[j, 0:4, :] = cot_ref[:, j * 128 : j * 128 + 128].astype(F32)
+    low = iota((32, 128), 1) < 64
+    for t in range(2):
+        first, second = shuffle[:, 2 * t, :], shuffle[:, 2 * t + 1, :]
+        cols = slice(2048 + t * 128, 2176 + t * 128)
+        rhs[256:288, cols] = jnp.where(low, first, pltpu.roll(second, 64, 1)).astype(BF)
+        rhs[288:320, cols] = jnp.where(low, pltpu.roll(first, 64, 1), second).astype(BF)
     rhs[320:384, 2048:2304] = jnp.zeros((64, 256), BF)
     field = dot(lhs[...], rhs[...], NT).astype(BF).reshape(8, 4, 16, 384)
     own[...] = field
-    xlo[...] = field[0]
-    xhi[...] = field[7]
     ylo[...] = field[:, 0]
     yhi[...] = field[:, 3]
-    ll[...] = field[0, 0]
-    lh[...] = field[0, 3]
-    hl[...] = field[7, 0]
-    hh[...] = field[7, 3]
+    here = lax.axis_index("region")
+    for p in range(faces.shape[0]):
+        faces[p] = own[jnp.where(p < here, 0, 7)]
+
+
+def x_halo(faces, place):
+    here = lax.axis_index("region")
+    count = faces.shape[0]
+    for at, there in ((0, here - 1), (9, here + 1)):
+        inside = (there >= 0) & (there < count)
+
+        @pl.when(inside)
+        def _():
+            place(at, faces[jnp.clip(there, 0, count - 1)])
+
+        @pl.when(jnp.logical_not(inside))
+        def _():
+            place(at, jnp.zeros(faces.shape[1:], BF))
+
+
+def extend_kernel(faces, ylo, yhi, low, high):
+    low[1:9] = ylo[...]
+    high[1:9] = yhi[...]
+
+    def place(at, face):
+        low[at] = face[0]
+        high[at] = face[3]
+
+    x_halo(faces, place)
 
 
 def tap_of(far, source, target):
@@ -128,9 +157,12 @@
                     zero = jnp.zeros((32, 128), BF)
                     big[first : first + 32, td * 128 : td * 128 + 128] = zero if plain is None else plain
                     big_t[first : first + 32, td * 128 : td * 128 + 128] = zero if turned is None else turned
+    column = iota((64, 64), 1)
+    order = jnp.where(iota((64, 64), 0) == 2 * (column & 31) + (column >> 5), 1.0, 0.0).astype(BF)
+    ordered = dot(dw_ref[...].reshape(256, 64), order).astype(BF)
     for e in range(8):
-        d, a, b = e >> 2, (e >> 1) & 1, e & 1
-        down_mat[e * 32 : e * 32 + 32, 0:64] = dw_ref[4 * a + 2 * b + d]
+        k = 4 * ((e >> 1) & 1) + 2 * (e & 1) + (e >> 2)
+        down_mat[e * 32 : e * 32 + 32, 0:64] = ordered[k * 32 : k * 32 + 32]
     down_mat[0:256, 64:128] = jnp.zeros((256, 64), BF)
     unit = iota((256, 128), 1) - 64 == (iota((256, 128), 0) >> 5)
     down_mat[256:512, :] = jnp.where(unit, 1.0, 0.0).astype(BF)
@@ -214,20 +246,19 @@
     return held
 
 
-def main_kernel(own, xlo, xhi, ylo, yhi, ll, lh, hl, hh, big1, big2, big2t, down_mat,
-                terms, fg_out, bkm_out, mask_out, sum_out,
-                field, ex, eg, eh, mk, ax, ag, ah, turned, products):
+def main_kernel(own, faces, ylo, yhi, big1, big2, big2t, down_mat,
+                terms, ef, bk, mk, summed,
+                field, ex, eg, eh, ax, ag, ah, turned, products, mixed):
     picks = lane_picks()
     field[1:9, 1:5] = own[...]
-    field[0, 1:5] = xlo[...]
-    field[9, 1:5] = xhi[...]
-    field[1:9, 0] = ylo[...]
-    field[1:9, 5] = yhi[...]
-    field[0, 0] = ll[...]
-    field[0, 5] = lh[...]
-    field[9, 0] = hl[...]
-    field[9, 5] = hh[...]
-    for store in (ex, eg, eh):
+    field[:, 0] = ylo[...]
+    field[:, 5] = yhi[...]
+
+    def place(at, face):
+        field[at, 1:5] = face
+
+    x_halo(faces, place)
+    for store in (ex, eg, eh, ef):
         clear_edges(store)
 
     def start(x, carry):
@@ -237,18 +268,11 @@
         mask = both[:, 256:512]
         bkm = both[:, 0:256] * mask
         mk[x] = mask.astype(BF).reshape(6, 16, 256)
-        products[pl.ds(pl.multiple_of(x * 96, 32), 96), 0:256] = bkm
+        bk[x] = bkm.reshape(6, 16, 256)
         put_field(eg, x + 1, 1, bkm.astype(BF).reshape(6, 16, 256))
         return carry
 
     lax.fori_loop(0, 10, start, 0)
-
-    def save(x, carry):
-        bkm_out[x] = products[pl.ds(pl.multiple_of((x + 1) * 96 + 16, 16), 64), 0:256].reshape(4, 16, 256)
-        mask_out[x] = mk[x + 1, 1:5]
-        return carry
-
-    lax.fori_loop(0, 8, save, 0)
 
     def first(i, carry):
         for j in range(2):
@@ -262,7 +286,7 @@
         grad = (spread * s * (1.0 + pre * (1.0 - s)) * mask).astype(BF).reshape(2, 6, 16, 256)
         for j in range(2):
             put_field(eh, 2 * i + j + 1, 1, hidden[j])
-            fg_out[2 * i + j] = grad[j]
+            put_field(ef, 2 * i + j + 1, 1, grad[j])
         return carry
 
     lax.fori_loop(0, 5, first, 0)
@@ -273,15 +297,14 @@
         pre = dot(ah[pl.ds(4 * i, 4)].reshape(256, 2048), big2[...])
         mask = mk[pl.ds(4 * i + 1, 4), 1:5].reshape(256, 256).astype(F32)
         inputs = field[pl.ds(4 * i + 1, 4), 1:5, :, 0:256].reshape(256, 256).astype(F32)
-        summed = (inputs + pre * mask).astype(BF)
-        sum_out[pl.ds(pl.multiple_of(256 * i, 256), 256), :] = summed
+        summed[pl.ds(pl.multiple_of(256 * i, 256), 256), :] = (inputs + pre * mask).astype(BF)
         return carry
 
     lax.fori_loop(0, 2, second, 0)
 
     held = None
-    for source, grads in ((1, fg_out[1:9, 1:5]), (2, eg[2:10, 2:6, :, 0:256])):
-        turned[...] = grads.reshape(512, 256).astype(F32).T.astype(BF)
+    for source, grads in ((1, ef), (2, eg)):
+        turned[...] = grads[2:10, 2:6, :, 0:256].reshape(512, 256).astype(F32).T.astype(BF)
         for s in range(8):
             cols = slice(s * 256, s * 256 + 256)
             wide = (ax[1:9, 1:5, :, cols] if source == 1 else ah[:, :, :, cols]).reshape(512, 256)
@@ -289,47 +312,49 @@
         held = fold_taps(products, terms, 27 * (source - 1), held)
     terms[416:448, :] = held.astype(terms.dtype)
     cot = field[1:9, 1:5, :, 256:384].reshape(512, 128).astype(F32).T.astype(BF)
-    grad_down = dot(cot, sum_out[...])
-    terms[448:512, :] = grad_down[0:64, 0:128].astype(terms.dtype)
-    terms[512:576, :] = grad_down[0:64, 128:256].astype(terms.dtype)
+    grad_down = dot(cot, summed[...])
+    for half in range(2):
+        for odd in range(2):
+            part = grad_down[odd * 32 : odd * 32 + 32, half * 128 : half * 128 + 128]
+            mixed[pl.ds(half * 64 + odd, 32, stride=2), :] = part
+    terms[448:576, :] = mixed[...].astype(terms.dtype)
     rest = terms.shape[0] - 576
     if rest:
         terms[576:, :] = jnp.zeros((rest, 128), terms.dtype)
 
 
-def tail_kernel(cell_ref, fg, bkm, mask, summed, big1t, down_mat, grad_features, down, ef, af, place, dense):
+def tail_kernel(cell_ref, ef, bk, mk, summed, big1t, down_mat, grad_features, down, ah, turned, dense, place_mat, shuffle):
     picks = lane_picks()
-    clear_edges(ef)
-
-    def start(x, carry):
-        put_field(ef, x + 1, 1, fg[x])
-        return carry
-
-    lax.fori_loop(0, 10, start, 0)
 
     def last(i, carry):
         for j in range(4):
-            widen(ef, af, 4 * i + j + 2, j, 2, 4, picks)
-        spread = dot(af[...].reshape(256, 2048), big1t[...])
-        rows = pl.ds(4 * i, 4)
-        grad = bkm[rows].reshape(256, 256) + spread * mask[rows].reshape(256, 256).astype(F32)
+            widen(ef, ah, 4 * i + j + 2, j, 2, 4, picks)
+        spread = dot(ah[...].reshape(256, 2048), big1t[...])
+        rows = pl.ds(4 * i + 1, 4)
+        mask = mk[rows, 1:5].reshape(256, 256).astype(F32)
+        grad = bk[rows, 1:5].reshape(256, 256) + spread * mask
         dense[pl.ds(pl.multiple_of(256 * i, 256), 256), :] = grad.astype(BF)
         return carry
 
     lax.fori_loop(0, 2, last, 0)
-    place_fine(cell_ref, place)
-    turned = dense[...].astype(F32).T.astype(BF)
+    place_fine(cell_ref, place_mat)
+    turned[...] = dense[...].astype(F32).T.astype(BF)
     pick = jnp.where(octant_rows(), 1.0, 0.0)
     for q in range(4):
-        moved = dot(turned, place[:, q * 512 : q * 512 + 512])
+        moved = dot(turned[...], place_mat[:, q * 512 : q * 512 + 512])
         total = moved[0:32] * pick[0:1]
         for e in range(1, 8):
             total = total + moved[e * 32 : e * 32 + 32] * pick[e : e + 1]
         grad_features[q] = total.astype(BF)
     lowered = dot(summed[...], down_mat[0:256, :]).T.astype(BF)
+    low = iota((32, 128), 1) < 64
     for t in range(2):
         moved = dot(lowered, coarse_tile(cell_ref, t))
-        down[:, t * 128 : t * 128 + 128] = moved[0:64].astype(BF)
+        even, odd = moved[0:32], moved[32:64]
+        shuffle[:, 2 * t, :] = jnp.where(low, even, pltpu.roll(odd, 64, 1))
+        shuffle[:, 2 * t + 1, :] = jnp.where(low, pltpu.roll(even, 64, 1), odd)
+    for j in range(32):
+        down[:, j * 128 : j * 128 + 128] = shuffle[j, 0:4, :].astype(BF)
 
 
 def reduce_kernel(parts, out):
@@ -338,7 +363,7 @@
     for i in range(1, count):
         total = total + parts[i].astype(F32)
     total = total.astype(out.dtype)
-    for i in range(count):
+    for i in range(out.shape[0]):
         out[i] = total
 
 
@@ -357,7 +382,7 @@
             down[4 * (g >> 1) + 2 * (g & 1) + half] = block[g * 32 : g * 32 + 32]
 
 
-def vmem_call(kernel, outs, ins, scratch=(), smem_first=False, flops=0):
+def vmem_call(kernel, outs, ins, scratch=(), smem_first=False, flops=0, limit=48):
     specs = [pl.BlockSpec(memory_space=pltpu.VMEM) for _ in ins]
     if smem_first:
         specs[0] = pl.BlockSpec(memory_space=pltpu.SMEM)
@@ -368,7 +393,7 @@
         in_specs=specs,
         out_specs=tuple(pl.BlockSpec(memory_space=pltpu.VMEM) for _ in outs),
         scratch_shapes=list(scratch),
-        compiler_params=pltpu.CompilerParams(vmem_limit_bytes=VMEM_LIMIT),
+        compiler_params=pltpu.CompilerParams(vmem_limit_bytes=limit * 1024 * 1024),
         cost_estimate=pl.CostEstimate(flops=flops, bytes_accessed=moved, transcendentals=0),
     )(*ins)
 
@@ -379,87 +404,80 @@
 
 def f32(*shape):
     return jax.ShapeDtypeStruct(shape, F32)
-
-
-def neighbours(regions, tiles, dx, dy):
-    pairs = []
-    for r in range(regions):
-        for t in range(tiles):
-            if 0 <= r + dx < regions and 0 <= t + dy < tiles:
-                pairs.append(((r + dx) * tiles + t + dy, r * tiles + t))
-    return pairs
 
 
 def on_device(features, voxel_mask, brick_cell, conv_one, conv_two, down_weight, cotangent):
     regions, tiles = lax.axis_size("region"), lax.axis_size("tile")
     devices = regions * tiles
     slots = features.shape[0]
-    cot = cotangent.reshape(slots, 64, 64).transpose(1, 0, 2).reshape(64, slots * 64)
-    pieces = vmem_call(
+    own, faces, ylo, yhi = vmem_call(
         gather_kernel,
-        [bf(8, 4, 16, 384), bf(4, 16, 384), bf(4, 16, 384), bf(8, 16, 384), bf(8, 16, 384)] + [bf(16, 384)] * 4,
-        (brick_cell, features, voxel_mask, cot),
-        [pltpu.VMEM((512, 2304), BF), pltpu.VMEM((384, 2304), BF)],
+        [bf(8, 4, 16, 384), bf(regions, 4, 16, 384), bf(8, 16, 384), bf(8, 16, 384)],
+        (brick_cell, features, voxel_mask, cotangent),
+        [pltpu.VMEM((512, 2304), BF), pltpu.VMEM((384, 2304), BF), pltpu.VMEM((32, 8, 128), F32)],
         smem_first=True,
         flops=2 * 512 * 2304 * 384,
-    )
-    own, xlo, xhi, ylo, yhi, ll, lh, hl, hh = pieces
-
-    def fetch(piece, dx, dy):
-        return lax.ppermute(piece, AXES, neighbours(regions, tiles, dx, dy))
-
-    halos = (
-        fetch(xhi, -1, 0), fetch(xlo, 1, 0), fetch(yhi, 0, -1), fetch(ylo, 0, 1),
-        fetch(hh, -1, -1), fetch(hl, -1, 1), fetch(lh, 1, -1), fetch(ll, 1, 1),
-    )
+        limit=16,
+    )
+    faces = lax.all_to_all(faces, "region", 0, 0, tiled=True)
+    low, high = vmem_call(extend_kernel, [bf(10, 16, 384), bf(10, 16, 384)], (faces, ylo, yhi), limit=4)
+    ups = [(i, i + 1) for i in range(tiles - 1)]
+    ylo = lax.ppermute(high, "tile", ups)
+    yhi = lax.ppermute(low, "tile", [(j, i) for i, j in ups])
     big1, big1t, big2, big2t, down_mat = vmem_call(
         weights_kernel,
         [bf(2048, 256)] * 4 + [bf(512, 128)],
         (conv_one.reshape(864, 32), conv_two.reshape(864, 32), down_weight),
         [pltpu.VMEM((27, 4, 32, 32), BF), pltpu.VMEM((864, 128), BF), pltpu.VMEM((32, 3456), BF)],
         flops=2 * 2 * 32 * 3456 * 256,
-    )
-    chunk = -(-(-(-576 // devices)) // 8) * 8
-    terms, fg, bkm, mask, summed = vmem_call(
+        limit=16,
+    )
+    chunk = -(-576 // (16 * tiles)) * 16
+    terms, ef, bk, mk, summed = vmem_call(
         main_kernel,
-        [bf(devices * chunk, 128), bf(10, 6, 16, 256), f32(8, 4, 16, 256), bf(8, 4, 16, 256), bf(512, 256)],
-        (own,) + halos + (big1, big2, big2t, down_mat),
+        [bf(tiles * chunk, 128), bf(12, 8, 16, 512), f32(10, 6, 16, 256), bf(10, 6, 16, 256), bf(512, 256)],
+        (own, faces, ylo, yhi, big1, big2, big2t, down_mat),
         [
             pltpu.VMEM((10, 6, 16, 384), BF),
             pltpu.VMEM((12, 8, 16, 512), BF),
             pltpu.VMEM((12, 8, 16, 512), BF),
             pltpu.VMEM((12, 8, 16, 512), BF),
-            pltpu.VMEM((10, 6, 16, 256), BF),
             pltpu.VMEM((10, 6, 16, 2048), BF),
             pltpu.VMEM((2, 6, 16, 2048), BF),
             pltpu.VMEM((8, 4, 16, 2048), BF),
             pltpu.VMEM((256, 512), BF),
-            pltpu.VMEM((960, 2048), F32),
+            pltpu.VMEM((256, 2048), F32),
+            pltpu.VMEM((128, 128), F32),
         ],
         flops=2 * 2048 * 256 * (960 * 2 + 512 * 3),
-    )
-    parts = lax.all_to_all(terms.reshape(devices, chunk, 128), AXES, 0, 0, tiled=True)
-    (total,) = vmem_call(reduce_kernel, [f32(devices, chunk, 128)], (parts,))
-    sums = lax.all_to_all(total, AXES, 0, 0, tiled=True)
+        limit=32,
+    )
+    parts = lax.all_to_all(terms.reshape(tiles, chunk, 128), "tile", 0, 0, tiled=True)
+    (total,) = vmem_call(reduce_kernel, [f32(regions, chunk, 128)], (parts,), limit=4)
+    parts = lax.all_to_all(total, "region", 0, 0, tiled=True)
+    (total,) = vmem_call(reduce_kernel, [bf(tiles, chunk, 128)], (parts,), limit=4)
+    sums = lax.all_to_all(total, "tile", 0, 0, tiled=True)
     grad_features, down = vmem_call(
         tail_kernel,
-        [bf(slots, 32, 512), bf(64, slots * 64)],
-        (brick_cell, fg, bkm, mask, summed, big1t, down_mat),
+        [bf(slots, 32, 512), bf(slots, 4096)],
+        (brick_cell, ef, bk, mk, summed, big1t, down_mat),
         [
-            pltpu.VMEM((12, 8, 16, 512), BF),
             pltpu.VMEM((4, 4, 16, 2048), BF),
+            pltpu.VMEM((256, 512), BF),
+            pltpu.VMEM((512, 256), BF),
             pltpu.VMEM((512, 2048), BF),
-            pltpu.VMEM((512, 256), BF),
+            pltpu.VMEM((32, 8, 128), F32),
         ],
         smem_first=True,
         flops=2 * 2048 * 512 * 512,
-    )
-    down = down.reshape(64, slots, 64).transpose(1, 0, 2).reshape(slots, 4096)
+        limit=16,
+    )
     scale = 1.0 / math.sqrt(devices * slots * 512.0)
     grad_one, grad_two, grad_down = vmem_call(
         functools.partial(finish_kernel, scale),
         [f32(27, 32, 32), f32(27, 32, 32), f32(8, 32, 64)],
-        (sums.reshape(devices * chunk, 128),),
+        (sums.reshape(tiles * chunk, 128),),
+        limit=8,
     )
     return down, grad_features, grad_one, grad_two, grad_down
 

time: 89.5 us -> 66.6 us (0.74)
  waiting for transfers between devices: 18.7 us -> 3.31 us
  blocking collectives: 17.3 us -> 32.4 us
  starting transfers between devices: 20.1 us -> 5.97 us
  Pallas kernels: 27.1 us -> 17.5 us
  local copies, waits for them, and re-layouts: 4.68 us -> 6.13 us
    all_to_all x1 -> x3, blocking collectives: 17.3 us -> 32.4 us  [the longest x1 14.1 us: on_device(): lax.all_to_all(terms.reshape(tiles, chunk, 128), 'tile', 0, 0, tiled=True)]
    ppermute x8 -> x2, starting transfers between devices: 17.4 us -> 2.59 us  [the longest x1 1.3 us: on_device(): ylo = lax.ppermute(high, 'tile', ups)]
    ppermute x8 -> x2, waiting for transfers between devices: 12 us -> 2.19 us  [the longest x1 2.18 us: on_device(): yhi = lax.ppermute(low, 'tile', [(j, i) for i, j in ups])]
    pallas_call x6 -> x8, Pallas kernels: 27.1 us -> 17.5 us  [vmem_call(): pl.pallas_call(kernel, out_shape=tuple(outs), in_specs=specs, out_specs=t...]
    all_to_all x1, waiting for transfers between devices: 6.7 us -> 1.12 us  [on_device(): sums = lax.all_to_all(total, 'tile', 0, 0, tiled=True)]
    unnamed x20 -> x24, local copies, waits for them, and re-layouts: 1.42 us -> 6.13 us
    reshape x5 -> x0, local copies, waits for them, and re-layouts: 3.24 us -> none  [the longest x3 1.66 us: on_device(): cotangent.reshape(slots, 64, 64).transpose(1, 0, 2).reshape(64, slots * 64)]
  transfers between devices with their start and end apart: 9 -> 3, of which waited for: 2 -> 2; matrix products, arithmetic and copies ran while one was open for 2% -> 0% of each run, Pallas kernels for 10% -> 8%
where the time goes in v2:
time: 66.6 us; the launch traced here: 66.1 us
  blocking collectives  32.4 us (49%)
  Pallas kernels  17.5 us (26%)
  local copies, waits for them, and re-layouts  6.13 us (9%)
  starting transfers between devices  5.97 us (9%)
  waiting for transfers between devices  3.31 us (5%)
  between operations  0.78 us (1%)
    pallas_call x8, Pallas kernels, vmem_call(): pl.pallas_call(kernel, out_shape=tuple(outs), in_specs=specs, out_specs=t...  17.5 us
    all_to_all x1, blocking collectives, on_device(): lax.all_to_all(terms.reshape(tiles, chunk, 128), 'tile', 0, 0, tiled=True)  14.1 us
    all_to_all x1, blocking collectives, on_device(): faces = lax.all_to_all(faces, 'region', 0, 0, tiled=True)  10.5 us
    all_to_all x1, blocking collectives, on_device(): parts = lax.all_to_all(total, 'region', 0, 0, tiled=True)  7.82 us
    unnamed x24, local copies, waits for them, and re-layouts  6.13 us
    all_to_all x1, starting transfers between devices, on_device(): sums = lax.all_to_all(total, 'tile', 0, 0, tiled=True)  3.38 us
    ppermute x1, waiting for transfers between devices, on_device(): yhi = lax.ppermute(low, 'tile', [(j, i) for i, j in ups])  2.18 us
  transfers between devices with their start and end apart: 3, of which 2 were waited for; matrix products, arithmetic and copies ran while one was open for 0% of the time, Pallas kernels for 8%

profile of v2, /device:TPU:0, one launch (start us, length us, event | category | flops | bytes accessed | tf_op | source)
XLA Modules:
  0.0 66.1 jit_solution(8340432329328942887)
XLA Ops:
  0.6 0.0 copy-start.6
  0.6 0.0 copy-start.3
  0.7 0.0 copy-start.7
  0.7 0.7 %copy-done.7 = s32[4]{0:T(128)S(1)} copy-done((s32[4]{0:T(128)S(1)}, s32[4]{0:T(128)}, u32[]{:S(2)}) %copy-start.7) | copy-done | bytes 40
  1.4 0.9 %copy-done.9 = bf16[4,32,512]{2,1,0:T(8,128)(2,1)S(1)} copy-done((bf16[4,32,512]{2,1,0:T(8,128)(2,1)S(1)}, bf16[4,32,512]{2,1,0:T(8,128)(2,1)}, u32[]{:S(2)}) %copy-start.9) | copy-done | bytes 131096
  2.3 0.8 %copy-done.10 = bf16[4,4096]{1,0:T(4,128)(2,1)S(1)} copy-done((bf16[4,4096]{1,0:T(4,128)(2,1)S(1)}, bf16[4,4096]{1,0:T(4,128)(2,1)}, u32[]{:S(2)}) %copy-start.10) | copy-done | bytes 32792
  3.0 0.7 %copy-done.11 = s32[4,512]{1,0:T(4,128)S(1)} copy-done((s32[4,512]{1,0:T(4,128)S(1)}, s32[4,512]{1,0:T(4,128)}, u32[]{:S(2)}) %copy-start.11) | copy-done | bytes 8216
  3.7 2.2 %shard_map.110 = (bf16[8,4,16,384]{3,2,1,0:T(8,128)(2,1)S(1)}, bf16[4,4,16,384]{3,2,1,0:T(8,128)(2,1)S(1)}, bf16[8,16,384]{2,1,0:T(8,128)(2,1)S(1)}, bf16[8,16,384]{2,1,0:T(8,128)(2,1)S(1)}) custom-call(s32[4]{0:T(128)S(1)} %copy-done.7, bf16[4,32,512]{2,1,0:T(8,128)(2,1)S(1)} %copy-done.9, s32[4,512]{1,0:T(4,128)S(1)} %copy-done.11, ...), custom_call_target="tpu_custom_call" | custom-call | flops 905969664 | bytes 958480 | tf_op jit(solution)/shard_map/pallas_call | solution.py:390
  5.9 10.5 %all_to_all.20.faces = bf16[4,4,16,384]{3,2,1,0:T(8,128)(2,1)S(1)} all-to-all(bf16[4,4,16,384]{3,2,1,0:T(8,128)(2,1)S(1)} %get-tuple-element.27), channel_id=1, replica_groups=mesh['region'=4,'tile'=8] {'region'}, dimensions={0} | all-to-all | bytes 393216 | tf_op jit(solution)/shard_map/all_to_all | solution.py:422
  16.4 1.3 %collective-permute-start = (bf16[10,16,384]{2,1,0:T(8,128)(2,1)S(1)}, bf16[10,16,384]{2,1,0:T(8,128)(2,1)S(1)}, u32[]{:S(2)}, u32[]{:S(2)}) collective-permute-start(bf16[10,16,384]{2,1,0:T(8,128)(2,1)S(1)} %get-tuple-element.30), channel_id=1, source_target_pairs={{0,1},{1,2},{2,3},{3,4},{4,5},{5,6},{6,7},{8,9},{9,10},{10,11},{11... | collective-permute-start | bytes 368648 | tf_op jit(solution)/shard_map/ppermute | solution.py:425
  17.7 1.3 %collective-permute-start.1 = (bf16[10,16,384]{2,1,0:T(8,128)(2,1)S(1)}, bf16[10,16,384]{2,1,0:T(8,128)(2,1)S(1)}, u32[]{:S(2)}, u32[]{:S(2)}) collective-permute-start(bf16[10,16,384]{2,1,0:T(8,128)(2,1)S(1)} %get-tuple-element.31), channel_id=1, source_target_pairs={{1,0},{2,1},{3,2},{4,3},{5,4},{6,5},{7,6},{9,8},{10,9},{11,10},{12... | collective-permute-start | bytes 368648 | tf_op jit(solution)/shard_map/ppermute | solution.py:426
  19.0 0.0 copy-done.6
  19.1 0.0 copy-done.3
  19.1 0.0 copy-done.2
  19.1 1.5 %shard_map.112 = (bf16[2048,256]{1,0:T(8,128)(2,1)S(1)}, bf16[2048,256]{1,0:T(8,128)(2,1)S(1)}, bf16[2048,256]{1,0:T(8,128)(2,1)S(1)}, bf16[2048,256]{1,0:T(8,128)(2,1)S(1)}, bf16[512,128]{1,0:T(8,128)(2,1)S(1)}) custom-call(bf16[864,32]{1,0:T(8,128)(2,1)S(1)} %bitcast.5, bf16[864,32]{1,0:T(8,128)(2,1)S(1)} %bitcast.6, bf16[8,32,64]{2,1,0:T(8,128)(2,1)S(1)} %copy-done.6), custom_call_target="tpu_custom_call" | custom-call | flops 113246208 | bytes 4468736 | tf_op jit(solution)/shard_map/pallas_call | solution.py:390
  20.6 0.0 copy-start.4
  20.6 0.0 collective-permute-done.ylo
  20.6 2.2 %collective-permute-done.1.yhi = bf16[10,16,384]{2,1,0:T(8,128)(2,1)S(1)} collective-permute-done((bf16[10,16,384]{2,1,0:T(8,128)(2,1)S(1)}, bf16[10,16,384]{2,1,0:T(8,128)(2,1)S(1)}, u32[]{:S(2)}, u32[]{:S(2)}) %collective-permute-start.1) | collective-permute-done | bytes 122912 | tf_op jit(solution)/shard_map/ppermute | solution.py:426
  22.8 8.0 %shard_map.113 = (bf16[640,128]{1,0:T(8,128)(2,1)S(1)}, bf16[12,8,16,512]{3,2,1,0:T(8,128)(2,1)S(1)}, f32[10,6,16,256]{3,2,1,0:T(8,128)S(1)}, bf16[10,6,16,256]{3,2,1,0:T(8,128)(2,1)S(1)}, bf16[512,256]{1,0:T(8,128)(2,1)S(1)}) custom-call(bf16[8,4,16,384]{3,2,1,0:T(8,128)(2,1)S(1)} %get-tuple-element.26.own, bf16[4,4,16,384]{3,2,1,0:T(8,128)(2,1)S(1)} %all_to_all.20.faces, ...), custom_call_target="tpu_custom_call" | custom-call | flops 3623878656 | bytes 7585792 | tf_op jit(solution)/shard_map/pallas_call | solution.py:390
  30.8 0.0 copy-done.4
  30.8 0.0 copy-start
  30.8 1.0 %copy-done = f32[10,6,16,256]{3,2,1,0:T(8,128)} copy-done((f32[10,6,16,256]{3,2,1,0:T(8,128)}, f32[10,6,16,256]{3,2,1,0:T(8,128)S(1)}, u32[]{:S(2)}) %copy-start) | copy-done | bytes 983064
  31.8 14.1 %all_to_all.21.parts = bf16[8,80,128]{2,1,0:T(8,128)(2,1)S(1)} all-to-all(bf16[8,80,128]{2,1,0:T(8,128)(2,1)S(1)} %bitcast.7), channel_id=1, replica_groups=mesh['region'=4,'tile'=8] {'tile'}, dimensions={0} | all-to-all | bytes 327680 | tf_op jit(solution)/shard_map/all_to_all | solution.py:455
  45.9 7.8 %all_to_all.22.parts = f32[4,80,128]{2,1,0:T(8,128)S(1)} all-to-all(f32[4,80,128]{2,1,0:T(8,128)S(1)} %shard_map.115), channel_id=1, replica_groups=mesh['region'=4,'tile'=8] {'region'}, dimensions={0} | all-to-all | bytes 327680 | tf_op jit(solution)/shard_map/all_to_all | solution.py:457
  53.7 0.7 %shard_map.116 = bf16[8,80,128]{2,1,0:T(8,128)(2,1)} custom-call(f32[4,80,128]{2,1,0:T(8,128)S(1)} %all_to_all.22.parts), custom_call_target="tpu_custom_call" | custom-call | bytes 327680 | tf_op jit(solution)/shard_map/pallas_call | solution.py:390
  54.4 3.4 %all-to-all-start.3 = ((bf16[8,80,128]{2,1,0:T(8,128)(2,1)}), bf16[8,80,128]{2,1,0:T(8,128)(2,1)S(1)}, u32[]{:S(2)}, u32[]{:S(2)}) async-start(bf16[8,80,128]{2,1,0:T(8,128)(2,1)} %shard_map.116), calls=%async_computation.3 | async-start | bytes 327680 | tf_op jit(solution)/shard_map/all_to_all | solution.py:459
  57.8 0.0 copy-done.8
  57.8 1.2 %copy-done.1 = f32[10,6,16,256]{3,2,1,0:T(8,128)S(1)} copy-done((f32[10,6,16,256]{3,2,1,0:T(8,128)S(1)}, f32[10,6,16,256]{3,2,1,0:T(8,128)}, u32[]{:S(2)}) %copy-start.1) | copy-done | bytes 983064
  59.0 0.9 %copy-done.5 = bf16[512,128]{1,0:T(8,128)(2,1)S(1)} copy-done((bf16[512,128]{1,0:T(8,128)(2,1)S(1)}, bf16[512,128]{1,0:T(8,128)(2,1)}, u32[]{:S(2)}) %copy-start.5) | copy-done | bytes 131096
  59.9 3.9 %shard_map.114 = (bf16[4,32,512]{2,1,0:T(8,128)(2,1)}, bf16[4,4096]{1,0:T(4,128)(2,1)}) custom-call(s32[4]{0:T(128)S(1)} %copy-done.8, bf16[12,8,16,512]{3,2,1,0:T(8,128)(2,1)S(1)} %get-tuple-element.36.ef, f32[10,6,16,256]{3,2,1,0:T(8,128)S(1)} %copy-done.1, bf16[10,6,16,256]{3,2,1,0:T(8,128)(2,1)S(1)} %get-tuple-element.38.mk, ...), custom_call_target="tpu_custom_call" | custom-call | flops 1073741824 | bytes 4653072 | tf_op jit(solution)/shard_map/pallas_call | solution.py:390
  63.8 1.1 %all-to-all-done.3 = bf16[8,80,128]{2,1,0:T(8,128)(2,1)S(1)} async-done(((bf16[8,80,128]{2,1,0:T(8,128)(2,1)}), bf16[8,80,128]{2,1,0:T(8,128)(2,1)S(1)}, u32[]{:S(2)}, u32[]{:S(2)}) %all-to-all-start.3) | async-done | bytes 163872 | tf_op jit(solution)/shard_map/all_to_all | solution.py:459
  64.9 1.2 %shard_map.117 = (f32[27,32,32]{2,1,0:T(8,128)}, f32[27,32,32]{2,1,0:T(8,128)}, f32[8,32,64]{2,1,0:T(8,128)}) custom-call(bf16[640,128]{1,0:T(8,128)(2,1)S(1)} %bitcast.4), custom_call_target="tpu_custom_call" | custom-call | bytes 450560 | tf_op jit(solution)/shard_map/pallas_call | solution.py:390
  (9 shorter events, 0.1 us)
Async XLA Ops:
  0.6 18.4 %copy-start.6 = (bf16[8,32,64]{2,1,0:T(8,128)(2,1)S(1)}, bf16[8,32,64]{2,1,0:T(8,128)(2,1)}, u32[]{:S(2)}) copy-start(bf16[8,32,64]{2,1,0:T(8,128)(2,1)} %dw_ref.1) | copy-start | bytes 98308
  0.6 18.4 %copy-start.3 = (bf16[27,32,32]{2,1,0:T(8,128)(2,1)S(1)}, bf16[27,32,32]{2,1,0:T(8,128)(2,1)}, u32[]{:S(2)}) copy-start(bf16[27,32,32]{2,1,0:T(8,128)(2,1)} %param.11) | copy-start | bytes 165892
  0.7 0.7 %copy-start.7 = (s32[4]{0:T(128)S(1)}, s32[4]{0:T(128)}, u32[]{:S(2)}) copy-start(s32[4]{0:T(128)} %cell_ref.3) | copy-start | bytes 52
  1.4 0.9 %copy-start.9 = (bf16[4,32,512]{2,1,0:T(8,128)(2,1)S(1)}, bf16[4,32,512]{2,1,0:T(8,128)(2,1)}, u32[]{:S(2)}) copy-start(bf16[4,32,512]{2,1,0:T(8,128)(2,1)} %feat_ref.1) | copy-start | bytes 393220
  2.3 0.8 %copy-start.10 = (bf16[4,4096]{1,0:T(4,128)(2,1)S(1)}, bf16[4,4096]{1,0:T(4,128)(2,1)}, u32[]{:S(2)}) copy-start(bf16[4,4096]{1,0:T(4,128)(2,1)} %cot_ref.1) | copy-start | bytes 98308
  3.0 0.7 %copy-start.11 = (s32[4,512]{1,0:T(4,128)S(1)}, s32[4,512]{1,0:T(4,128)}, u32[]{:S(2)}) copy-start(s32[4,512]{1,0:T(4,128)} %vmask_ref.1) | copy-start | bytes 24580
  3.7 15.3 %copy-start.2 = (bf16[27,32,32]{2,1,0:T(8,128)(2,1)S(1)}, bf16[27,32,32]{2,1,0:T(8,128)(2,1)}, u32[]{:S(2)}) copy-start(bf16[27,32,32]{2,1,0:T(8,128)(2,1)} %param.10) | copy-start | bytes 165892
  16.4 4.1 %collective-permute-start = (bf16[10,16,384]{2,1,0:T(8,128)(2,1)S(1)}, bf16[10,16,384]{2,1,0:T(8,128)(2,1)S(1)}, u32[]{:S(2)}, u32[]{:S(2)}) collective-permute-start(bf16[10,16,384]{2,1,0:T(8,128)(2,1)S(1)} %get-tuple-element.30), channel_id=1, source_target_pairs={{0,1},{1,2},{2,3},{3,4},{4,5},{5,6},{6,7},{8,9},{9,10},{10,11},{11... | collective-permute-start | bytes 368648 | tf_op jit(solution)/shard_map/ppermute | solution.py:425
  17.7 5.0 %collective-permute-start.1 = (bf16[10,16,384]{2,1,0:T(8,128)(2,1)S(1)}, bf16[10,16,384]{2,1,0:T(8,128)(2,1)S(1)}, u32[]{:S(2)}, u32[]{:S(2)}) collective-permute-start(bf16[10,16,384]{2,1,0:T(8,128)(2,1)S(1)} %get-tuple-element.31), channel_id=1, source_target_pairs={{1,0},{2,1},{3,2},{4,3},{5,4},{6,5},{7,6},{9,8},{10,9},{11,10},{12... | collective-permute-start | bytes 368648 | tf_op jit(solution)/shard_map/ppermute | solution.py:426
  20.6 10.2 %copy-start.4 = (bf16[512,128]{1,0:T(8,128)(2,1)}, bf16[512,128]{1,0:T(8,128)(2,1)S(1)}, u32[]{:S(2)}) copy-start(bf16[512,128]{1,0:T(8,128)(2,1)S(1)} %get-tuple-element.35.down_mat) | copy-start | bytes 393220
  30.8 1.0 %copy-start = (f32[10,6,16,256]{3,2,1,0:T(8,128)}, f32[10,6,16,256]{3,2,1,0:T(8,128)S(1)}, u32[]{:S(2)}) copy-start(f32[10,6,16,256]{3,2,1,0:T(8,128)S(1)} %get-tuple-element.37.bk) | copy-start | bytes 2949124
  31.8 26.0 %copy-start.8 = (s32[4]{0:T(128)S(1)}, s32[4]{0:T(128)}, u32[]{:S(2)}) copy-start(s32[4]{0:T(128)} %cell_ref.3) | copy-start | bytes 52
  54.4 10.5 %all-to-all-start.3 = ((bf16[8,80,128]{2,1,0:T(8,128)(2,1)}), bf16[8,80,128]{2,1,0:T(8,128)(2,1)S(1)}, u32[]{:S(2)}, u32[]{:S(2)}) async-start(bf16[8,80,128]{2,1,0:T(8,128)(2,1)} %shard_map.116), calls=%async_computation.3 | async-start | bytes 327680 | tf_op jit(solution)/shard_map/all_to_all | solution.py:459
  57.8 1.2 %copy-start.1 = (f32[10,6,16,256]{3,2,1,0:T(8,128)S(1)}, f32[10,6,16,256]{3,2,1,0:T(8,128)}, u32[]{:S(2)}) copy-start(f32[10,6,16,256]{3,2,1,0:T(8,128)} %copy-done) | copy-start | bytes 2949124
  59.0 0.9 %copy-start.5 = (bf16[512,128]{1,0:T(8,128)(2,1)S(1)}, bf16[512,128]{1,0:T(8,128)(2,1)}, u32[]{:S(2)}) copy-start(bf16[512,128]{1,0:T(8,128)(2,1)} %copy-done.4) | copy-start | bytes 393220

commit v3 on v2

--- a/solution.py
+++ b/solution.py
@@ -60,10 +60,22 @@
     return jnp.where((cell == wanted) & (code == (lane & 63)), 1.0, 0.0).astype(BF)
 
 
-def gather_kernel(cell_ref, feat_ref, vmask_ref, cot_ref, own, faces, ylo, yhi, lhs, rhs, shuffle):
+def gather_kernel(cell_hbm, feat_hbm, vmask_hbm, cot_hbm, own, faces, ylo, yhi,
+                  lhs, rhs, shuffle, cell_ref, feat_ref, vmask_ref, cot_ref, sems):
+    moves = [
+        pltpu.make_async_copy(source, target, sems.at[i])
+        for i, (source, target) in enumerate(
+            ((cell_hbm, cell_ref), (vmask_hbm, vmask_ref), (feat_hbm, feat_ref), (cot_hbm, cot_ref))
+        )
+    ]
+    for move in moves:
+        move.start()
+    moves[0].wait()
     place_fine(cell_ref, lhs)
     for t in range(2):
         lhs[:, 2048 + t * 128 : 2048 + t * 128 + 128] = coarse_tile(cell_ref, t)
+    for move in moves[1:]:
+        move.wait()
     match = octant_rows()
     for q in range(4):
         cols = slice(q * 512, q * 512 + 512)
@@ -247,8 +259,8 @@
 
 
 def main_kernel(own, faces, ylo, yhi, big1, big2, big2t, down_mat,
-                terms, ef, bk, mk, summed,
-                field, ex, eg, eh, ax, ag, ah, turned, products, mixed):
+                terms, ef, summed,
+                field, ex, eg, eh, mk, ax, ag, ah, turned, products, mixed):
     picks = lane_picks()
     field[1:9, 1:5] = own[...]
     field[:, 0] = ylo[...]
@@ -261,46 +273,35 @@
     for store in (ex, eg, eh, ef):
         clear_edges(store)
 
-    def start(x, carry):
-        row = field[x]
-        put_field(ex, x + 1, 1, row[:, :, 0:256])
-        both = dot(row[:, :, 256:384].reshape(96, 128), down_mat[...], NT)
+    for x in range(0, 10, 2):
+        rows = field[x : x + 2]
+        both = dot(rows[:, :, :, 256:384].reshape(192, 128), down_mat[...], NT)
         mask = both[:, 256:512]
-        bkm = both[:, 0:256] * mask
-        mk[x] = mask.astype(BF).reshape(6, 16, 256)
-        bk[x] = bkm.reshape(6, 16, 256)
-        put_field(eg, x + 1, 1, bkm.astype(BF).reshape(6, 16, 256))
-        return carry
-
-    lax.fori_loop(0, 10, start, 0)
-
-    def first(i, carry):
+        mk[x : x + 2] = mask.astype(BF).reshape(2, 6, 16, 256)
+        grad = (both[:, 0:256] * mask).astype(BF).reshape(2, 6, 16, 256)
         for j in range(2):
-            widen(ex, ax, 2 * i + j + 1, 2 * i + j, 1, 6, picks)
-            widen(eg, ag, 2 * i + j + 1, j, 1, 6, picks)
-        mask = mk[pl.ds(2 * i, 2)].reshape(192, 256).astype(F32)
-        pre = dot(ax[pl.ds(2 * i, 2)].reshape(192, 2048), big1[...]) * mask
-        spread = dot(ag[...].reshape(192, 2048), big2t[...])
+            put_field(ex, x + j + 1, 1, rows[j, :, :, 0:256])
+            put_field(eg, x + j + 1, 1, grad[j])
+    for x in range(0, 10, 2):
+        for j in range(2):
+            widen(ex, ax, x + j + 1, x + j, 1, 6, picks)
+            widen(eg, ag, x + j + 1, x + j, 1, 6, picks)
+        mask = mk[x : x + 2].reshape(192, 256).astype(F32)
+        pre = dot(ax[x : x + 2].reshape(192, 2048), big1[...]) * mask
+        spread = dot(ag[x : x + 2].reshape(192, 2048), big2t[...])
         s = jax.nn.sigmoid(pre)
         hidden = (pre * s).astype(BF).reshape(2, 6, 16, 256)
         grad = (spread * s * (1.0 + pre * (1.0 - s)) * mask).astype(BF).reshape(2, 6, 16, 256)
         for j in range(2):
-            put_field(eh, 2 * i + j + 1, 1, hidden[j])
-            put_field(ef, 2 * i + j + 1, 1, grad[j])
-        return carry
-
-    lax.fori_loop(0, 5, first, 0)
-
-    def second(i, carry):
+            put_field(eh, x + j + 1, 1, hidden[j])
+            put_field(ef, x + j + 1, 1, grad[j])
+    for x in range(0, 8, 4):
         for j in range(4):
-            widen(eh, ah, 4 * i + j + 2, 4 * i + j, 2, 4, picks)
-        pre = dot(ah[pl.ds(4 * i, 4)].reshape(256, 2048), big2[...])
-        mask = mk[pl.ds(4 * i + 1, 4), 1:5].reshape(256, 256).astype(F32)
-        inputs = field[pl.ds(4 * i + 1, 4), 1:5, :, 0:256].reshape(256, 256).astype(F32)
-        summed[pl.ds(pl.multiple_of(256 * i, 256), 256), :] = (inputs + pre * mask).astype(BF)
-        return carry
-
-    lax.fori_loop(0, 2, second, 0)
+            widen(eh, ah, x + j + 2, x + j, 2, 4, picks)
+        pre = dot(ah[x : x + 4].reshape(256, 2048), big2[...])
+        mask = mk[x + 1 : x + 5, 1:5].reshape(256, 256).astype(F32)
+        inputs = field[x + 1 : x + 5, 1:5, :, 0:256].reshape(256, 256).astype(F32)
+        summed[x * 64 : x * 64 + 256, :] = (inputs + pre * mask).astype(BF)
 
     held = None
     for source, grads in ((1, ef), (2, eg)):
@@ -323,20 +324,16 @@
         terms[576:, :] = jnp.zeros((rest, 128), terms.dtype)
 
 
-def tail_kernel(cell_ref, ef, bk, mk, summed, big1t, down_mat, grad_features, down, ah, turned, dense, place_mat, shuffle):
+def tail_kernel(cell_ref, own, ef, summed, big1t, down_mat, grad_features, down, ah, turned, dense, place_mat, shuffle):
     picks = lane_picks()
 
-    def last(i, carry):
+    for x in range(0, 8, 4):
         for j in range(4):
-            widen(ef, ah, 4 * i + j + 2, j, 2, 4, picks)
-        spread = dot(ah[...].reshape(256, 2048), big1t[...])
-        rows = pl.ds(4 * i + 1, 4)
-        mask = mk[rows, 1:5].reshape(256, 256).astype(F32)
-        grad = bk[rows, 1:5].reshape(256, 256) + spread * mask
-        dense[pl.ds(pl.multiple_of(256 * i, 256), 256), :] = grad.astype(BF)
-        return carry
-
-    lax.fori_loop(0, 2, last, 0)
+            widen(ef, ah, x + j + 2, x + j, 2, 4, picks)
+        spread = dot(ah[x : x + 4].reshape(256, 2048), big1t[...])
+        both = dot(own[x : x + 4, :, :, 256:384].reshape(256, 128), down_mat[...], NT)
+        grad = (both[:, 0:256] + spread) * both[:, 256:512]
+        dense[x * 64 : x * 64 + 256, :] = grad.astype(BF)
     place_fine(cell_ref, place_mat)
     turned[...] = dense[...].astype(F32).T.astype(BF)
     pick = jnp.where(octant_rows(), 1.0, 0.0)
@@ -382,8 +379,8 @@
             down[4 * (g >> 1) + 2 * (g & 1) + half] = block[g * 32 : g * 32 + 32]
 
 
-def vmem_call(kernel, outs, ins, scratch=(), smem_first=False, flops=0, limit=48):
-    specs = [pl.BlockSpec(memory_space=pltpu.VMEM) for _ in ins]
+def vmem_call(kernel, outs, ins, scratch=(), smem_first=False, flops=0, limit=48, in_space=pltpu.VMEM):
+    specs = [pl.BlockSpec(memory_space=in_space) for _ in ins]
     if smem_first:
         specs[0] = pl.BlockSpec(memory_space=pltpu.SMEM)
     moved = sum(math.prod(x.shape) * x.dtype.itemsize for x in tuple(ins) + tuple(outs))
@@ -414,8 +411,10 @@
         gather_kernel,
         [bf(8, 4, 16, 384), bf(regions, 4, 16, 384), bf(8, 16, 384), bf(8, 16, 384)],
         (brick_cell, features, voxel_mask, cotangent),
-        [pltpu.VMEM((512, 2304), BF), pltpu.VMEM((384, 2304), BF), pltpu.VMEM((32, 8, 128), F32)],
-        smem_first=True,
+        [pltpu.VMEM((512, 2304), BF), pltpu.VMEM((384, 2304), BF), pltpu.VMEM((32, 8, 128), F32),
+         pltpu.SMEM(brick_cell.shape, I32), pltpu.VMEM(features.shape, BF), pltpu.VMEM(voxel_mask.shape, I32),
+         pltpu.VMEM(cotangent.shape, BF), pltpu.SemaphoreType.DMA((4,))],
+        in_space=pltpu.HBM,
         flops=2 * 512 * 2304 * 384,
         limit=16,
     )
@@ -432,18 +431,19 @@
         flops=2 * 2 * 32 * 3456 * 256,
         limit=16,
     )
-    chunk = -(-576 // (16 * tiles)) * 16
-    terms, ef, bk, mk, summed = vmem_call(
+    chunk = -(-576 // (8 * tiles)) * 8
+    terms, ef, summed = vmem_call(
         main_kernel,
-        [bf(tiles * chunk, 128), bf(12, 8, 16, 512), f32(10, 6, 16, 256), bf(10, 6, 16, 256), bf(512, 256)],
+        [bf(tiles * chunk, 128), bf(12, 8, 16, 512), bf(512, 256)],
         (own, faces, ylo, yhi, big1, big2, big2t, down_mat),
         [
             pltpu.VMEM((10, 6, 16, 384), BF),
             pltpu.VMEM((12, 8, 16, 512), BF),
             pltpu.VMEM((12, 8, 16, 512), BF),
             pltpu.VMEM((12, 8, 16, 512), BF),
+            pltpu.VMEM((10, 6, 16, 256), BF),
             pltpu.VMEM((10, 6, 16, 2048), BF),
-            pltpu.VMEM((2, 6, 16, 2048), BF),
+            pltpu.VMEM((10, 6, 16, 2048), BF),
             pltpu.VMEM((8, 4, 16, 2048), BF),
             pltpu.VMEM((256, 512), BF),
             pltpu.VMEM((256, 2048), F32),
@@ -460,9 +460,9 @@
     grad_features, down = vmem_call(
         tail_kernel,
         [bf(slots, 32, 512), bf(slots, 4096)],
-        (brick_cell, ef, bk, mk, summed, big1t, down_mat),
+        (brick_cell, own, ef, summed, big1t, down_mat),
         [
-            pltpu.VMEM((4, 4, 16, 2048), BF),
+            pltpu.VMEM((8, 4, 16, 2048), BF),
             pltpu.VMEM((256, 512), BF),
             pltpu.VMEM((512, 256), BF),
             pltpu.VMEM((512, 2048), BF),

time: 66.6 us -> 62.8 us (0.943)
  Pallas kernels: 17.5 us -> 15.1 us
  local copies, waits for them, and re-layouts: 6.13 us -> 4.02 us
  waiting for transfers between devices: 3.31 us -> 4.41 us
    pallas_call x8, Pallas kernels: 17.5 us -> 15.1 us  [vmem_call(): pl.pallas_call(kernel, out_shape=tuple(outs), in_specs=specs, out_specs=t...]
    unnamed x24 -> x20, local copies, waits for them, and re-layouts: 6.13 us -> 4.02 us
    all_to_all x1, waiting for transfers between devices: 1.12 us -> 2.21 us  [on_device(): sums = lax.all_to_all(total, 'tile', 0, 0, tiled=True)]
where the time goes in v3:
time: 62.8 us; the launch traced here: 62.2 us
  blocking collectives  32 us (51%)
  Pallas kernels  15.1 us (24%)
  starting transfers between devices  5.97 us (10%)
  waiting for transfers between devices  4.41 us (7%)
  local copies, waits for them, and re-layouts  4.02 us (6%)
  between operations  0.78 us (1%)
    pallas_call x8, Pallas kernels, vmem_call(): pl.pallas_call(kernel, out_shape=tuple(outs), in_specs=specs, out_specs=t...  15.1 us
    all_to_all x1, blocking collectives, on_device(): lax.all_to_all(terms.reshape(tiles, chunk, 128), 'tile', 0, 0, tiled=True)  13.7 us
    all_to_all x1, blocking collectives, on_device(): faces = lax.all_to_all(faces, 'region', 0, 0, tiled=True)  10.5 us
    all_to_all x1, blocking collectives, on_device(): parts = lax.all_to_all(total, 'region', 0, 0, tiled=True)  7.77 us
    unnamed x20, local copies, waits for them, and re-layouts  4.02 us
    all_to_all x1, starting transfers between devices, on_device(): sums = lax.all_to_all(total, 'tile', 0, 0, tiled=True)  3.38 us
    all_to_all x1, waiting for transfers between devices, on_device(): sums = lax.all_to_all(total, 'tile', 0, 0, tiled=True)  2.21 us
    ppermute x1, waiting for transfers between devices, on_device(): yhi = lax.ppermute(low, 'tile', [(j, i) for i, j in ups])  2.2 us
  transfers between devices with their start and end apart: 3, of which 2 were waited for; matrix products, arithmetic and copies ran while one was open for 0% of the time, Pallas kernels for 8%

profile of v3, /device:TPU:0, one launch (start us, length us, event | category | flops | bytes accessed | tf_op | source)
XLA Modules:
  0.0 62.2 jit_solution(4149503278768124198)
XLA Ops:
  0.6 0.0 copy-start.2
  0.6 0.0 copy-start.1
  0.7 0.0 copy-start.3
  0.7 0.9 %copy-done.3 = bf16[4,32,512]{2,1,0:T(8,128)(2,1)S(1)} copy-done((bf16[4,32,512]{2,1,0:T(8,128)(2,1)S(1)}, bf16[4,32,512]{2,1,0:T(8,128)(2,1)}, u32[]{:S(2)}) %copy-start.3) | copy-done | bytes 131096
  1.6 0.0 copy-start.4
  1.6 0.8 %copy-done.4 = bf16[4,4096]{1,0:T(4,128)(2,1)S(1)} copy-done((bf16[4,4096]{1,0:T(4,128)(2,1)S(1)}, bf16[4,4096]{1,0:T(4,128)(2,1)}, u32[]{:S(2)}) %copy-start.4) | copy-done | bytes 32792
  2.4 0.0 copy-start.5
  2.4 0.7 %copy-done.5 = s32[4,512]{1,0:T(4,128)S(1)} copy-done((s32[4,512]{1,0:T(4,128)S(1)}, s32[4,512]{1,0:T(4,128)}, u32[]{:S(2)}) %copy-start.5) | copy-done | bytes 8216
  3.1 0.7 %copy-done.6 = s32[4]{0:T(128)S(1)} copy-done((s32[4]{0:T(128)S(1)}, s32[4]{0:T(128)}, u32[]{:S(2)}) %copy-start.6) | copy-done | bytes 40
  3.7 2.7 %shard_map.110 = (bf16[8,4,16,384]{3,2,1,0:T(8,128)(2,1)S(1)}, bf16[4,4,16,384]{3,2,1,0:T(8,128)(2,1)S(1)}, bf16[8,16,384]{2,1,0:T(8,128)(2,1)S(1)}, bf16[8,16,384]{2,1,0:T(8,128)(2,1)S(1)}) custom-call(s32[4]{0:T(128)S(1)} %copy-done.6, bf16[4,32,512]{2,1,0:T(8,128)(2,1)S(1)} %copy-done.3, s32[4,512]{1,0:T(4,128)S(1)} %copy-done.5, ...), custom_call_target="tpu_custom_call" | custom-call | flops 905969664 | bytes 958480 | tf_op jit(solution)/shard_map/pallas_call | solution.py:387
  6.5 10.5 %all_to_all.20.faces = bf16[4,4,16,384]{3,2,1,0:T(8,128)(2,1)S(1)} all-to-all(bf16[4,4,16,384]{3,2,1,0:T(8,128)(2,1)S(1)} %get-tuple-element.25), channel_id=1, replica_groups=mesh['region'=4,'tile'=8] {'region'}, dimensions={0} | all-to-all | bytes 393216 | tf_op jit(solution)/shard_map/all_to_all | solution.py:421
  17.0 1.3 %collective-permute-start = (bf16[10,16,384]{2,1,0:T(8,128)(2,1)S(1)}, bf16[10,16,384]{2,1,0:T(8,128)(2,1)S(1)}, u32[]{:S(2)}, u32[]{:S(2)}) collective-permute-start(bf16[10,16,384]{2,1,0:T(8,128)(2,1)S(1)} %get-tuple-element.28), channel_id=1, source_target_pairs={{0,1},{1,2},{2,3},{3,4},{4,5},{5,6},{6,7},{8,9},{9,10},{10,11},{11... | collective-permute-start | bytes 368648 | tf_op jit(solution)/shard_map/ppermute | solution.py:424
  18.3 1.3 %collective-permute-start.1 = (bf16[10,16,384]{2,1,0:T(8,128)(2,1)S(1)}, bf16[10,16,384]{2,1,0:T(8,128)(2,1)S(1)}, u32[]{:S(2)}, u32[]{:S(2)}) collective-permute-start(bf16[10,16,384]{2,1,0:T(8,128)(2,1)S(1)} %get-tuple-element.29), channel_id=1, source_target_pairs={{1,0},{2,1},{3,2},{4,3},{5,4},{6,5},{7,6},{9,8},{10,9},{11,10},{12... | collective-permute-start | bytes 368648 | tf_op jit(solution)/shard_map/ppermute | solution.py:425
  19.6 0.0 copy-done.2
  19.6 0.0 copy-done.1
  19.6 0.0 copy-done
  19.7 1.5 %shard_map.112 = (bf16[2048,256]{1,0:T(8,128)(2,1)S(1)}, bf16[2048,256]{1,0:T(8,128)(2,1)S(1)}, bf16[2048,256]{1,0:T(8,128)(2,1)S(1)}, bf16[2048,256]{1,0:T(8,128)(2,1)S(1)}, bf16[512,128]{1,0:T(8,128)(2,1)S(1)}) custom-call(bf16[864,32]{1,0:T(8,128)(2,1)S(1)} %bitcast.5, bf16[864,32]{1,0:T(8,128)(2,1)S(1)} %bitcast.6, bf16[8,32,64]{2,1,0:T(8,128)(2,1)S(1)} %copy-done.2), custom_call_target="tpu_custom_call" | custom-call | flops 113246208 | bytes 4468736 | tf_op jit(solution)/shard_map/pallas_call | solution.py:387
  21.2 0.0 collective-permute-done.ylo
  21.2 2.2 %collective-permute-done.1.yhi = bf16[10,16,384]{2,1,0:T(8,128)(2,1)S(1)} collective-permute-done((bf16[10,16,384]{2,1,0:T(8,128)(2,1)S(1)}, bf16[10,16,384]{2,1,0:T(8,128)(2,1)S(1)}, u32[]{:S(2)}, u32[]{:S(2)}) %collective-permute-start.1) | collective-permute-done | bytes 122912 | tf_op jit(solution)/shard_map/ppermute | solution.py:425
  23.4 5.2 %shard_map.113 = (bf16[576,128]{1,0:T(8,128)(2,1)S(1)}, bf16[12,8,16,512]{3,2,1,0:T(8,128)(2,1)S(1)}, bf16[512,256]{1,0:T(8,128)(2,1)S(1)}) custom-call(bf16[8,4,16,384]{3,2,1,0:T(8,128)(2,1)S(1)} %get-tuple-element.24.own, bf16[4,4,16,384]{3,2,1,0:T(8,128)(2,1)S(1)} %all_to_all.20.faces, bf16[10,16,384]{2,1,0:T(8,128)(2,1)S(1)} %collective-permute-done.ylo, ...), custom_call_target="tpu_custom_call" | custom-call | flops 3623878656 | bytes 6094848 | tf_op jit(solution)/shard_map/pallas_call | solution.py:387
  28.5 0.0 copy-start.8
  28.6 13.7 %all_to_all.21.parts = bf16[8,72,128]{2,1,0:T(8,128)(2,1)S(1)} all-to-all(bf16[8,72,128]{2,1,0:T(8,128)(2,1)S(1)} %bitcast.7), channel_id=1, replica_groups=mesh['region'=4,'tile'=8] {'tile'}, dimensions={0} | all-to-all | bytes 294912 | tf_op jit(solution)/shard_map/all_to_all | solution.py:455
  42.3 7.8 %all_to_all.22.parts = f32[4,72,128]{2,1,0:T(8,128)S(1)} all-to-all(f32[4,72,128]{2,1,0:T(8,128)S(1)} %shard_map.115), channel_id=1, replica_groups=mesh['region'=4,'tile'=8] {'region'}, dimensions={0} | all-to-all | bytes 294912 | tf_op jit(solution)/shard_map/all_to_all | solution.py:457
  50.1 0.0 copy-done.8
  50.1 0.7 %shard_map.116 = bf16[8,72,128]{2,1,0:T(8,128)(2,1)} custom-call(f32[4,72,128]{2,1,0:T(8,128)S(1)} %all_to_all.22.parts), custom_call_target="tpu_custom_call" | custom-call | bytes 294912 | tf_op jit(solution)/shard_map/pallas_call | solution.py:387
  50.8 3.4 %all-to-all-start.3 = ((bf16[8,72,128]{2,1,0:T(8,128)(2,1)}), bf16[8,72,128]{2,1,0:T(8,128)(2,1)S(1)}, u32[]{:S(2)}, u32[]{:S(2)}) async-start(bf16[8,72,128]{2,1,0:T(8,128)(2,1)} %shard_map.116), calls=%async_computation.3 | async-start | bytes 294912 | tf_op jit(solution)/shard_map/all_to_all | solution.py:459
  54.2 0.0 copy-done.7
  54.2 0.0 copy-start.9
  54.2 0.9 %copy-done.9 = bf16[512,256]{1,0:T(8,128)(2,1)S(1)} copy-done((bf16[512,256]{1,0:T(8,128)(2,1)S(1)}, bf16[512,256]{1,0:T(8,128)(2,1)}, u32[]{:S(2)}) %copy-start.9) | copy-done | bytes 262168
  55.1 3.8 %shard_map.114 = (bf16[4,32,512]{2,1,0:T(8,128)(2,1)}, bf16[4,4096]{1,0:T(4,128)(2,1)}) custom-call(s32[4]{0:T(128)S(1)} %copy-done.7, bf16[8,4,16,384]{3,2,1,0:T(8,128)(2,1)S(1)} %get-tuple-element.24.own, bf16[12,8,16,512]{3,2,1,0:T(8,128)(2,1)S(1)} %get-tuple-element.34.ef, bf16[512,256]{1,0:T(8,128)(2,1)S(1)} %copy-done.9, ...), custom_call_target="tpu_custom_call" | custom-call | flops 1073741824 | bytes 3571728 | tf_op jit(solution)/shard_map/pallas_call | solution.py:387
  58.9 2.2 %all-to-all-done.3 = bf16[8,72,128]{2,1,0:T(8,128)(2,1)S(1)} async-done(((bf16[8,72,128]{2,1,0:T(8,128)(2,1)}), bf16[8,72,128]{2,1,0:T(8,128)(2,1)S(1)}, u32[]{:S(2)}, u32[]{:S(2)}) %all-to-all-start.3) | async-done | bytes 147488 | tf_op jit(solution)/shard_map/all_to_all | solution.py:459
  61.1 1.2 %shard_map.117 = (f32[27,32,32]{2,1,0:T(8,128)}, f32[27,32,32]{2,1,0:T(8,128)}, f32[8,32,64]{2,1,0:T(8,128)}) custom-call(bf16[576,128]{1,0:T(8,128)(2,1)S(1)} %bitcast.4), custom_call_target="tpu_custom_call" | custom-call | bytes 434176 | tf_op jit(solution)/shard_map/pallas_call | solution.py:387
  (5 shorter events, 0.1 us)
Async XLA Ops:
  0.6 19.0 %copy-start.2 = (bf16[8,32,64]{2,1,0:T(8,128)(2,1)S(1)}, bf16[8,32,64]{2,1,0:T(8,128)(2,1)}, u32[]{:S(2)}) copy-start(bf16[8,32,64]{2,1,0:T(8,128)(2,1)} %dw_ref.1) | copy-start | bytes 98308
  0.6 19.0 %copy-start.1 = (bf16[27,32,32]{2,1,0:T(8,128)(2,1)S(1)}, bf16[27,32,32]{2,1,0:T(8,128)(2,1)}, u32[]{:S(2)}) copy-start(bf16[27,32,32]{2,1,0:T(8,128)(2,1)} %param.11) | copy-start | bytes 165892
  0.7 0.9 %copy-start.3 = (bf16[4,32,512]{2,1,0:T(8,128)(2,1)S(1)}, bf16[4,32,512]{2,1,0:T(8,128)(2,1)}, u32[]{:S(2)}) copy-start(bf16[4,32,512]{2,1,0:T(8,128)(2,1)} %feat_hbm.1) | copy-start | bytes 393220
  1.6 0.8 %copy-start.4 = (bf16[4,4096]{1,0:T(4,128)(2,1)S(1)}, bf16[4,4096]{1,0:T(4,128)(2,1)}, u32[]{:S(2)}) copy-start(bf16[4,4096]{1,0:T(4,128)(2,1)} %cot_hbm.1) | copy-start | bytes 98308
  2.4 0.7 %copy-start.5 = (s32[4,512]{1,0:T(4,128)S(1)}, s32[4,512]{1,0:T(4,128)}, u32[]{:S(2)}) copy-start(s32[4,512]{1,0:T(4,128)} %vmask_hbm.1) | copy-start | bytes 24580
  3.1 0.7 %copy-start.6 = (s32[4]{0:T(128)S(1)}, s32[4]{0:T(128)}, u32[]{:S(2)}) copy-start(s32[4]{0:T(128)} %cell_ref.1) | copy-start | bytes 52
  3.7 15.9 %copy-start = (bf16[27,32,32]{2,1,0:T(8,128)(2,1)S(1)}, bf16[27,32,32]{2,1,0:T(8,128)(2,1)}, u32[]{:S(2)}) copy-start(bf16[27,32,32]{2,1,0:T(8,128)(2,1)} %param.10) | copy-start | bytes 165892
  17.0 4.1 %collective-permute-start = (bf16[10,16,384]{2,1,0:T(8,128)(2,1)S(1)}, bf16[10,16,384]{2,1,0:T(8,128)(2,1)S(1)}, u32[]{:S(2)}, u32[]{:S(2)}) collective-permute-start(bf16[10,16,384]{2,1,0:T(8,128)(2,1)S(1)} %get-tuple-element.28), channel_id=1, source_target_pairs={{0,1},{1,2},{2,3},{3,4},{4,5},{5,6},{6,7},{8,9},{9,10},{10,11},{11... | collective-permute-start | bytes 368648 | tf_op jit(solution)/shard_map/ppermute | solution.py:424
  18.3 5.0 %collective-permute-start.1 = (bf16[10,16,384]{2,1,0:T(8,128)(2,1)S(1)}, bf16[10,16,384]{2,1,0:T(8,128)(2,1)S(1)}, u32[]{:S(2)}, u32[]{:S(2)}) collective-permute-start(bf16[10,16,384]{2,1,0:T(8,128)(2,1)S(1)} %get-tuple-element.29), channel_id=1, source_target_pairs={{1,0},{2,1},{3,2},{4,3},{5,4},{6,5},{7,6},{9,8},{10,9},{11,10},{12... | collective-permute-start | bytes 368648 | tf_op jit(solution)/shard_map/ppermute | solution.py:425
  23.4 30.8 %copy-start.7 = (s32[4]{0:T(128)S(1)}, s32[4]{0:T(128)}, u32[]{:S(2)}) copy-start(s32[4]{0:T(128)} %cell_ref.1) | copy-start | bytes 52
  28.5 21.5 %copy-start.8 = (bf16[512,256]{1,0:T(8,128)(2,1)}, bf16[512,256]{1,0:T(8,128)(2,1)S(1)}, u32[]{:S(2)}) copy-start(bf16[512,256]{1,0:T(8,128)(2,1)S(1)} %get-tuple-element.35.summed) | copy-start | bytes 786436
  50.8 10.3 %all-to-all-start.3 = ((bf16[8,72,128]{2,1,0:T(8,128)(2,1)}), bf16[8,72,128]{2,1,0:T(8,128)(2,1)S(1)}, u32[]{:S(2)}, u32[]{:S(2)}) async-start(bf16[8,72,128]{2,1,0:T(8,128)(2,1)} %shard_map.116), calls=%async_computation.3 | async-start | bytes 294912 | tf_op jit(solution)/shard_map/all_to_all | solution.py:459
  54.2 1.0 %copy-start.9 = (bf16[512,256]{1,0:T(8,128)(2,1)S(1)}, bf16[512,256]{1,0:T(8,128)(2,1)}, u32[]{:S(2)}) copy-start(bf16[512,256]{1,0:T(8,128)(2,1)} %copy-done.8) | copy-start | bytes 786436

commit v4 on v3

--- a/solution.py
+++ b/solution.py
@@ -60,7 +60,7 @@
     return jnp.where((cell == wanted) & (code == (lane & 63)), 1.0, 0.0).astype(BF)
 
 
-def gather_kernel(cell_hbm, feat_hbm, vmask_hbm, cot_hbm, own, faces, ylo, yhi,
+def gather_kernel(cell_hbm, feat_hbm, vmask_hbm, cot_hbm, own, faces,
                   lhs, rhs, shuffle, cell_ref, feat_ref, vmask_ref, cot_ref, sems):
     moves = [
         pltpu.make_async_copy(source, target, sems.at[i])
@@ -98,8 +98,6 @@
     rhs[320:384, 2048:2304] = jnp.zeros((64, 256), BF)
     field = dot(lhs[...], rhs[...], NT).astype(BF).reshape(8, 4, 16, 384)
     own[...] = field
-    ylo[...] = field[:, 0]
-    yhi[...] = field[:, 3]
     here = lax.axis_index("region")
     for p in range(faces.shape[0]):
         faces[p] = own[jnp.where(p < here, 0, 7)]
@@ -120,15 +118,21 @@
             place(at, jnp.zeros(faces.shape[1:], BF))
 
 
-def extend_kernel(faces, ylo, yhi, low, high):
-    low[1:9] = ylo[...]
-    high[1:9] = yhi[...]
-
-    def place(at, face):
-        low[at] = face[0]
-        high[at] = face[3]
-
-    x_halo(faces, place)
+def extend_kernel(own, faces, far, near):
+    odd = lax.rem(lax.axis_index("tile"), 2)
+
+    def fill(low, high):
+        low[1:9] = own[:, 0]
+        high[1:9] = own[:, 3]
+
+        def place(at, face):
+            low[at] = face[0]
+            high[at] = face[3]
+
+        x_halo(faces, place)
+
+    pl.when(odd == 1)(lambda: fill(near, far))
+    pl.when(odd == 0)(lambda: fill(far, near))
 
 
 def tap_of(far, source, target):
@@ -258,13 +262,14 @@
     return held
 
 
-def main_kernel(own, faces, ylo, yhi, big1, big2, big2t, down_mat,
+def main_kernel(own, faces, far, near, big1, big2, big2t, down_mat,
                 terms, ef, summed,
                 field, ex, eg, eh, mk, ax, ag, ah, turned, products, mixed):
     picks = lane_picks()
     field[1:9, 1:5] = own[...]
-    field[:, 0] = ylo[...]
-    field[:, 5] = yhi[...]
+    odd = lax.rem(lax.axis_index("tile"), 2)
+    field[:, 5 * odd] = far[...]
+    field[:, 5 - 5 * odd] = near[...]
 
     def place(at, face):
         field[at, 1:5] = face
@@ -407,22 +412,26 @@
     regions, tiles = lax.axis_size("region"), lax.axis_size("tile")
     devices = regions * tiles
     slots = features.shape[0]
-    own, faces, ylo, yhi = vmem_call(
+    own, faces = vmem_call(
         gather_kernel,
-        [bf(8, 4, 16, 384), bf(regions, 4, 16, 384), bf(8, 16, 384), bf(8, 16, 384)],
+        [bf(8, 4, 16, 384), bf(regions, 4, 16, 384)],
         (brick_cell, features, voxel_mask, cotangent),
         [pltpu.VMEM((512, 2304), BF), pltpu.VMEM((384, 2304), BF), pltpu.VMEM((32, 8, 128), F32),
          pltpu.SMEM(brick_cell.shape, I32), pltpu.VMEM(features.shape, BF), pltpu.VMEM(voxel_mask.shape, I32),
          pltpu.VMEM(cotangent.shape, BF), pltpu.SemaphoreType.DMA((4,))],
         in_space=pltpu.HBM,
         flops=2 * 512 * 2304 * 384,
-        limit=16,
+        limit=60,
     )
     faces = lax.all_to_all(faces, "region", 0, 0, tiled=True)
-    low, high = vmem_call(extend_kernel, [bf(10, 16, 384), bf(10, 16, 384)], (faces, ylo, yhi), limit=4)
-    ups = [(i, i + 1) for i in range(tiles - 1)]
-    ylo = lax.ppermute(high, "tile", ups)
-    yhi = lax.ppermute(low, "tile", [(j, i) for i, j in ups])
+    far, near = vmem_call(extend_kernel, [bf(10, 16, 384), bf(10, 16, 384)], (own, faces), limit=4)
+
+    def swap(face, start):
+        pairs = [(i, i + 1) for i in range(start, tiles - 1, 2)]
+        return lax.ppermute(face, "tile", pairs + [(j, i) for i, j in pairs])
+
+    far = swap(far, 1)
+    near = swap(near, 0)
     big1, big1t, big2, big2t, down_mat = vmem_call(
         weights_kernel,
         [bf(2048, 256)] * 4 + [bf(512, 128)],
@@ -435,7 +444,7 @@
     terms, ef, summed = vmem_call(
         main_kernel,
         [bf(tiles * chunk, 128), bf(12, 8, 16, 512), bf(512, 256)],
-        (own, faces, ylo, yhi, big1, big2, big2t, down_mat),
+        (own, faces, far, near, big1, big2, big2t, down_mat),
         [
             pltpu.VMEM((10, 6, 16, 384), BF),
             pltpu.VMEM((12, 8, 16, 512), BF),
@@ -453,7 +462,7 @@
         limit=32,
     )
     parts = lax.all_to_all(terms.reshape(tiles, chunk, 128), "tile", 0, 0, tiled=True)
-    (total,) = vmem_call(reduce_kernel, [f32(regions, chunk, 128)], (parts,), limit=4)
+    (total,) = vmem_call(reduce_kernel, [bf(regions, chunk, 128)], (parts,), limit=4)
     parts = lax.all_to_all(total, "region", 0, 0, tiled=True)
     (total,) = vmem_call(reduce_kernel, [bf(tiles, chunk, 128)], (parts,), limit=4)
     sums = lax.all_to_all(total, "tile", 0, 0, tiled=True)

time: 62.8 us -> 60.3 us (0.960)
  waiting for transfers between devices: 4.41 us -> 2.2 us
  blocking collectives: 32 us -> 30.6 us
  starting transfers between devices: 5.97 us -> 7.04 us
  local copies, waits for them, and re-layouts: 4.02 us -> 2.96 us
  Pallas kernels: 15.1 us -> 16.1 us
    ppermute x2, waiting for transfers between devices: 2.2 us -> 0.01 us  [swap(): return lax.ppermute(face, 'tile', pairs + [(j, i) for i, j in pairs])]
    ppermute x2, starting transfers between devices: 2.59 us -> 3.67 us  [swap(): return lax.ppermute(face, 'tile', pairs + [(j, i) for i, j in pairs])]
    pallas_call x8, Pallas kernels: 15.1 us -> 16.1 us  [vmem_call(): pl.pallas_call(kernel, out_shape=tuple(outs), in_specs=specs, out_specs=t...]
    all_to_all x1, blocking collectives: 13.7 us -> 12.7 us  [on_device(): lax.all_to_all(terms.reshape(tiles, chunk, 128), 'tile', 0, 0, tiled=True)]
    unnamed x20 -> x18, local copies, waits for them, and re-layouts: 4.02 us -> 2.96 us
  transfers between devices with their start and end apart: 3 -> 3, of which waited for: 2 -> 1; matrix products, arithmetic and copies ran while one was open for 0% -> 0% of each run, Pallas kernels for 8% -> 9%
where the time goes in v4:
time: 60.3 us; the launch traced here: 59.7 us
  blocking collectives  30.6 us (51%)
  Pallas kernels  16.1 us (27%)
  starting transfers between devices  7.04 us (12%)
  local copies, waits for them, and re-layouts  2.96 us (5%)
  waiting for transfers between devices  2.2 us (4%)
  between operations  0.77 us (1%)
    pallas_call x8, Pallas kernels, vmem_call(): pl.pallas_call(kernel, out_shape=tuple(outs), in_specs=specs, out_specs=t...  16.1 us
    all_to_all x1, blocking collectives, on_device(): lax.all_to_all(terms.reshape(tiles, chunk, 128), 'tile', 0, 0, tiled=True)  12.7 us
    all_to_all x1, blocking collectives, on_device(): faces = lax.all_to_all(faces, 'region', 0, 0, tiled=True)  10.7 us
    all_to_all x1, blocking collectives, on_device(): parts = lax.all_to_all(total, 'region', 0, 0, tiled=True)  7.24 us
    ppermute x2, starting transfers between devices, swap(): return lax.ppermute(face, 'tile', pairs + [(j, i) for i, j in pairs])  3.67 us
    all_to_all x1, starting transfers between devices, on_device(): sums = lax.all_to_all(total, 'tile', 0, 0, tiled=True)  3.38 us
    unnamed x18, local copies, waits for them, and re-layouts  2.96 us
    all_to_all x1, waiting for transfers between devices, on_device(): sums = lax.all_to_all(total, 'tile', 0, 0, tiled=True)  2.2 us
  transfers between devices with their start and end apart: 3, of which 1 were waited for; matrix products, arithmetic and copies ran while one was open for 0% of the time, Pallas kernels for 9%

profile of v4, /device:TPU:0, one launch (start us, length us, event | category | flops | bytes accessed | tf_op | source)
XLA Modules:
  0.0 59.7 jit_solution(7037026836757007940)
XLA Ops:
  0.6 0.0 copy-start.5
  0.6 0.0 copy-start.4
  0.7 0.0 copy-start.3
  0.7 3.8 %shard_map.110 = (bf16[8,4,16,384]{3,2,1,0:T(8,128)(2,1)}, bf16[4,4,16,384]{3,2,1,0:T(8,128)(2,1)}) custom-call(s32[4]{0:T(128)} %cell_ref.1, bf16[4,32,512]{2,1,0:T(8,128)(2,1)} %feat_hbm.1, s32[4,512]{1,0:T(4,128)} %vmask_hbm.1, bf16[4,4096]{1,0:T(4,128)(2,1)} %cot_hbm.1), custom_call_target="tpu_custom_call" | custom-call | flops 905969664 | bytes 761872 | tf_op jit(solution)/shard_map/pallas_call | solution.py:392
  4.5 10.7 %all_to_all.20.faces = bf16[4,4,16,384]{3,2,1,0:T(8,128)(2,1)S(1)} all-to-all(bf16[4,4,16,384]{3,2,1,0:T(8,128)(2,1)} %get-tuple-element.23), channel_id=1, replica_groups=mesh['region'=4,'tile'=8] {'region'}, dimensions={0} | all-to-all | bytes 393216 | tf_op jit(solution)/shard_map/all_to_all | solution.py:426
  15.2 0.0 copy-start
  15.2 1.0 %copy-done = bf16[8,4,16,384]{3,2,1,0:T(8,128)(2,1)S(1)} copy-done((bf16[8,4,16,384]{3,2,1,0:T(8,128)(2,1)S(1)}, bf16[8,4,16,384]{3,2,1,0:T(8,128)(2,1)}, u32[]{:S(2)}) %copy-start) | copy-done | bytes 393240
  16.2 0.7 %collective-permute-start = (bf16[10,16,384]{2,1,0:T(8,128)(2,1)S(1)}, bf16[10,16,384]{2,1,0:T(8,128)(2,1)S(1)}, u32[]{:S(2)}, u32[]{:S(2)}) collective-permute-start(bf16[10,16,384]{2,1,0:T(8,128)(2,1)S(1)} %get-tuple-element.24), channel_id=1, source_target_pairs={{1,2},{3,4},{5,6},{2,1},{4,3},{6,5},{9,10},{11,12},{13,14},{10,9},... | collective-permute-start | bytes 368648 | tf_op jit(solution)/shard_map/ppermute | solution.py:431
  16.9 3.0 %collective-permute-start.1 = (bf16[10,16,384]{2,1,0:T(8,128)(2,1)S(1)}, bf16[10,16,384]{2,1,0:T(8,128)(2,1)S(1)}, u32[]{:S(2)}, u32[]{:S(2)}) collective-permute-start(bf16[10,16,384]{2,1,0:T(8,128)(2,1)S(1)} %get-tuple-element.25), channel_id=1, source_target_pairs={{0,1},{2,3},{4,5},{6,7},{1,0},{3,2},{5,4},{7,6},{8,9},{10,11},{12,... | collective-permute-start | bytes 368648 | tf_op jit(solution)/shard_map/ppermute | solution.py:431
  19.9 0.0 copy-done.5
  19.9 0.0 copy-done.4
  19.9 0.0 copy-done.3
  19.9 1.5 %shard_map.112 = (bf16[2048,256]{1,0:T(8,128)(2,1)S(1)}, bf16[2048,256]{1,0:T(8,128)(2,1)S(1)}, bf16[2048,256]{1,0:T(8,128)(2,1)S(1)}, bf16[2048,256]{1,0:T(8,128)(2,1)S(1)}, bf16[512,128]{1,0:T(8,128)(2,1)S(1)}) custom-call(bf16[864,32]{1,0:T(8,128)(2,1)S(1)} %bitcast.5, bf16[864,32]{1,0:T(8,128)(2,1)S(1)} %bitcast.6, bf16[8,32,64]{2,1,0:T(8,128)(2,1)S(1)} %copy-done.5), custom_call_target="tpu_custom_call" | custom-call | flops 113246208 | bytes 4468736 | tf_op jit(solution)/shard_map/pallas_call | solution.py:392
  21.4 0.0 collective-permute-done.far
  21.4 0.0 collective-permute-done.1.near
  21.4 0.0 copy-start.1
  21.4 1.0 %copy-done.1 = bf16[8,4,16,384]{3,2,1,0:T(8,128)(2,1)S(1)} copy-done((bf16[8,4,16,384]{3,2,1,0:T(8,128)(2,1)S(1)}, bf16[8,4,16,384]{3,2,1,0:T(8,128)(2,1)}, u32[]{:S(2)}) %copy-start.1) | copy-done | bytes 393240
  22.4 0.0 copy-start.2
  22.4 5.2 %shard_map.113 = (bf16[576,128]{1,0:T(8,128)(2,1)S(1)}, bf16[12,8,16,512]{3,2,1,0:T(8,128)(2,1)S(1)}, bf16[512,256]{1,0:T(8,128)(2,1)S(1)}) custom-call(bf16[8,4,16,384]{3,2,1,0:T(8,128)(2,1)S(1)} %copy-done.1, bf16[4,4,16,384]{3,2,1,0:T(8,128)(2,1)S(1)} %all_to_all.20.faces, bf16[10,16,384]{2,1,0:T(8,128)(2,1)S(1)} %collective-permute-done.far, ...), custom_call_target="tpu_custom_call" | custom-call | flops 3623878656 | bytes 6094848 | tf_op jit(solution)/shard_map/pallas_call | solution.py:392
  27.6 0.0 copy-start.7
  27.6 12.7 %all_to_all.21.parts = bf16[8,72,128]{2,1,0:T(8,128)(2,1)S(1)} all-to-all(bf16[8,72,128]{2,1,0:T(8,128)(2,1)S(1)} %bitcast.7), channel_id=1, replica_groups=mesh['region'=4,'tile'=8] {'tile'}, dimensions={0} | all-to-all | bytes 294912 | tf_op jit(solution)/shard_map/all_to_all | solution.py:464
  40.3 7.2 %all_to_all.22.parts = bf16[4,72,128]{2,1,0:T(8,128)(2,1)S(1)} all-to-all(bf16[4,72,128]{2,1,0:T(8,128)(2,1)S(1)} %shard_map.115), channel_id=1, replica_groups=mesh['region'=4,'tile'=8] {'region'}, dimensions={0} | all-to-all | bytes 147456 | tf_op jit(solution)/shard_map/all_to_all | solution.py:466
  47.6 0.0 copy-done.7
  47.6 0.7 %shard_map.116 = bf16[8,72,128]{2,1,0:T(8,128)(2,1)} custom-call(bf16[4,72,128]{2,1,0:T(8,128)(2,1)S(1)} %all_to_all.22.parts), custom_call_target="tpu_custom_call" | custom-call | bytes 221184 | tf_op jit(solution)/shard_map/pallas_call | solution.py:392
  48.3 3.4 %all-to-all-start.3 = ((bf16[8,72,128]{2,1,0:T(8,128)(2,1)}), bf16[8,72,128]{2,1,0:T(8,128)(2,1)S(1)}, u32[]{:S(2)}, u32[]{:S(2)}) async-start(bf16[8,72,128]{2,1,0:T(8,128)(2,1)} %shard_map.116), calls=%async_computation.3 | async-start | bytes 294912 | tf_op jit(solution)/shard_map/all_to_all | solution.py:468
  51.6 0.0 copy-done.2
  51.7 0.0 copy-done.6
  51.7 0.0 copy-start.8
  51.7 0.9 %copy-done.8 = bf16[512,256]{1,0:T(8,128)(2,1)S(1)} copy-done((bf16[512,256]{1,0:T(8,128)(2,1)S(1)}, bf16[512,256]{1,0:T(8,128)(2,1)}, u32[]{:S(2)}) %copy-start.8) | copy-done | bytes 262168
  52.6 3.8 %shard_map.114 = (bf16[4,32,512]{2,1,0:T(8,128)(2,1)}, bf16[4,4096]{1,0:T(4,128)(2,1)}) custom-call(s32[4]{0:T(128)S(1)} %copy-done.6, bf16[8,4,16,384]{3,2,1,0:T(8,128)(2,1)S(1)} %copy-done.2, bf16[12,8,16,512]{3,2,1,0:T(8,128)(2,1)S(1)} %get-tuple-element.30.ef, bf16[512,256]{1,0:T(8,128)(2,1)S(1)} %copy-done.8, ...), custom_call_target="tpu_custom_call" | custom-call | flops 1073741824 | bytes 3571728 | tf_op jit(solution)/shard_map/pallas_call | solution.py:392
  56.4 2.2 %all-to-all-done.3 = bf16[8,72,128]{2,1,0:T(8,128)(2,1)S(1)} async-done(((bf16[8,72,128]{2,1,0:T(8,128)(2,1)}), bf16[8,72,128]{2,1,0:T(8,128)(2,1)S(1)}, u32[]{:S(2)}, u32[]{:S(2)}) %all-to-all-start.3) | async-done | bytes 147488 | tf_op jit(solution)/shard_map/all_to_all | solution.py:468
  58.6 1.2 %shard_map.117 = (f32[27,32,32]{2,1,0:T(8,128)}, f32[27,32,32]{2,1,0:T(8,128)}, f32[8,32,64]{2,1,0:T(8,128)}) custom-call(bf16[576,128]{1,0:T(8,128)(2,1)S(1)} %bitcast.4), custom_call_target="tpu_custom_call" | custom-call | bytes 434176 | tf_op jit(solution)/shard_map/pallas_call | solution.py:392
  (3 shorter events, 0.1 us)
Async XLA Ops:
  0.6 19.3 %copy-start.5 = (bf16[8,32,64]{2,1,0:T(8,128)(2,1)S(1)}, bf16[8,32,64]{2,1,0:T(8,128)(2,1)}, u32[]{:S(2)}) copy-start(bf16[8,32,64]{2,1,0:T(8,128)(2,1)} %dw_ref.1) | copy-start | bytes 98308
  0.6 19.3 %copy-start.4 = (bf16[27,32,32]{2,1,0:T(8,128)(2,1)S(1)}, bf16[27,32,32]{2,1,0:T(8,128)(2,1)}, u32[]{:S(2)}) copy-start(bf16[27,32,32]{2,1,0:T(8,128)(2,1)} %param.11) | copy-start | bytes 165892
  0.7 19.2 %copy-start.3 = (bf16[27,32,32]{2,1,0:T(8,128)(2,1)S(1)}, bf16[27,32,32]{2,1,0:T(8,128)(2,1)}, u32[]{:S(2)}) copy-start(bf16[27,32,32]{2,1,0:T(8,128)(2,1)} %param.10) | copy-start | bytes 165892
  15.2 1.0 %copy-start = (bf16[8,4,16,384]{3,2,1,0:T(8,128)(2,1)S(1)}, bf16[8,4,16,384]{3,2,1,0:T(8,128)(2,1)}, u32[]{:S(2)}) copy-start(bf16[8,4,16,384]{3,2,1,0:T(8,128)(2,1)} %get-tuple-element.22.own) | copy-start | bytes 1179652
  16.2 5.2 %collective-permute-start = (bf16[10,16,384]{2,1,0:T(8,128)(2,1)S(1)}, bf16[10,16,384]{2,1,0:T(8,128)(2,1)S(1)}, u32[]{:S(2)}, u32[]{:S(2)}) collective-permute-start(bf16[10,16,384]{2,1,0:T(8,128)(2,1)S(1)} %get-tuple-element.24), channel_id=1, source_target_pairs={{1,2},{3,4},{5,6},{2,1},{4,3},{6,5},{9,10},{11,12},{13,14},{10,9},... | collective-permute-start | bytes 368648 | tf_op jit(solution)/shard_map/ppermute | solution.py:431
  16.9 4.5 %collective-permute-start.1 = (bf16[10,16,384]{2,1,0:T(8,128)(2,1)S(1)}, bf16[10,16,384]{2,1,0:T(8,128)(2,1)S(1)}, u32[]{:S(2)}, u32[]{:S(2)}) collective-permute-start(bf16[10,16,384]{2,1,0:T(8,128)(2,1)S(1)} %get-tuple-element.25), channel_id=1, source_target_pairs={{0,1},{2,3},{4,5},{6,7},{1,0},{3,2},{5,4},{7,6},{8,9},{10,11},{12,... | collective-permute-start | bytes 368648 | tf_op jit(solution)/shard_map/ppermute | solution.py:431
  21.4 1.0 %copy-start.1 = (bf16[8,4,16,384]{3,2,1,0:T(8,128)(2,1)S(1)}, bf16[8,4,16,384]{3,2,1,0:T(8,128)(2,1)}, u32[]{:S(2)}) copy-start(bf16[8,4,16,384]{3,2,1,0:T(8,128)(2,1)} %get-tuple-element.22.own) | copy-start | bytes 1179652
  22.4 29.2 %copy-start.2 = (bf16[8,4,16,384]{3,2,1,0:T(8,128)(2,1)S(1)}, bf16[8,4,16,384]{3,2,1,0:T(8,128)(2,1)}, u32[]{:S(2)}) copy-start(bf16[8,4,16,384]{3,2,1,0:T(8,128)(2,1)} %get-tuple-element.22.own) | copy-start | bytes 1179652
  22.4 29.2 %copy-start.6 = (s32[4]{0:T(128)S(1)}, s32[4]{0:T(128)}, u32[]{:S(2)}) copy-start(s32[4]{0:T(128)} %cell_ref.1) | copy-start | bytes 52
  27.6 19.9 %copy-start.7 = (bf16[512,256]{1,0:T(8,128)(2,1)}, bf16[512,256]{1,0:T(8,128)(2,1)S(1)}, u32[]{:S(2)}) copy-start(bf16[512,256]{1,0:T(8,128)(2,1)S(1)} %get-tuple-element.31.summed) | copy-start | bytes 786436
  48.3 10.3 %all-to-all-start.3 = ((bf16[8,72,128]{2,1,0:T(8,128)(2,1)}), bf16[8,72,128]{2,1,0:T(8,128)(2,1)S(1)}, u32[]{:S(2)}, u32[]{:S(2)}) async-start(bf16[8,72,128]{2,1,0:T(8,128)(2,1)} %shard_map.116), calls=%async_computation.3 | async-start | bytes 294912 | tf_op jit(solution)/shard_map/all_to_all | solution.py:468
  51.7 1.0 %copy-start.8 = (bf16[512,256]{1,0:T(8,128)(2,1)S(1)}, bf16[512,256]{1,0:T(8,128)(2,1)}, u32[]{:S(2)}) copy-start(bf16[512,256]{1,0:T(8,128)(2,1)} %copy-done.7) | copy-start | bytes 786436

commit v5 on v4

--- a/solution.py
+++ b/solution.py
@@ -61,7 +61,7 @@
 
 
 def gather_kernel(cell_hbm, feat_hbm, vmask_hbm, cot_hbm, own, faces,
-                  lhs, rhs, shuffle, cell_ref, feat_ref, vmask_ref, cot_ref, sems):
+                  lhs, rhs, cots, box, shuffle, cell_ref, feat_ref, vmask_ref, cot_ref, sems):
     moves = [
         pltpu.make_async_copy(source, target, sems.at[i])
         for i, (source, target) in enumerate(
@@ -70,11 +70,14 @@
     ]
     for move in moves:
         move.start()
-    moves[0].wait()
-    place_fine(cell_ref, lhs)
-    for t in range(2):
-        lhs[:, 2048 + t * 128 : 2048 + t * 128 + 128] = coarse_tile(cell_ref, t)
-    for move in moves[1:]:
+    row = iota((128, 128), 0)
+    code = (row >> 5) * 16 + ((row >> 3) & 3) * 4 + (row & 3)
+    for t in range(4):
+        v = iota((1, 128), 1) + 128 * t
+        vcode = (v >> 7) * 16 + ((v >> 4) & 3) * 4 + ((v >> 1) & 3)
+        lhs[:, t * 128 : t * 128 + 128] = jnp.where(code == vcode, 1.0, 0.0).astype(BF)
+    box[...] = jnp.zeros((8, 4, 16, 384), F32)
+    for move in moves:
         move.wait()
     match = octant_rows()
     for q in range(4):
@@ -86,17 +89,32 @@
         rhs[256:320, cols] = jnp.zeros((64, 512), BF)
         rhs[320:336, cols] = jnp.concatenate([m8, jnp.zeros((8, 512), F32)], axis=0).astype(BF)
         rhs[336:384, cols] = jnp.zeros((48, 512), BF)
-    rhs[0:256, 2048:2304] = jnp.zeros((256, 256), BF)
+    cots[64:128, :] = jnp.zeros((64, 256), BF)
     for j in range(32):
         shuffle[j, 0:4, :] = cot_ref[:, j * 128 : j * 128 + 128].astype(F32)
     low = iota((32, 128), 1) < 64
     for t in range(2):
         first, second = shuffle[:, 2 * t, :], shuffle[:, 2 * t + 1, :]
-        cols = slice(2048 + t * 128, 2176 + t * 128)
-        rhs[256:288, cols] = jnp.where(low, first, pltpu.roll(second, 64, 1)).astype(BF)
-        rhs[288:320, cols] = jnp.where(low, pltpu.roll(first, 64, 1), second).astype(BF)
-    rhs[320:384, 2048:2304] = jnp.zeros((64, 256), BF)
-    field = dot(lhs[...], rhs[...], NT).astype(BF).reshape(8, 4, 16, 384)
+        cols = slice(t * 128, t * 128 + 128)
+        cots[0:32, cols] = jnp.where(low, first, pltpu.roll(second, 64, 1)).astype(BF)
+        cots[32:64, cols] = jnp.where(low, pltpu.roll(first, 64, 1), second).astype(BF)
+    wide_code = iota((128, 256), 0)
+    wide_code = (wide_code >> 5) * 16 + ((wide_code >> 3) & 3) * 4 + (wide_code & 3)
+    z_part = iota((16, 128), 0) >> 2
+    for q in range(4):
+        cell = cell_ref[q]
+        here_z = jnp.where(cell < 0, -1, cell & 3)
+        half = pl.ds(4 * (jnp.maximum(cell, 0) >> 2), 4)
+        pick = jnp.where(iota((128, 256), 1) - 64 * q == wide_code, 1.0, 0.0).astype(BF)
+        fine = dot(lhs[...], rhs[:, q * 512 : q * 512 + 512], NT)
+        third = fine[:, 256:384] + dot(pick, cots[...], NT)
+        for t, part in enumerate((fine[:, 0:128], fine[:, 128:256], third)):
+            part = part.reshape(4, 4, 8, 128)
+            part = jnp.concatenate([part, part], axis=2)
+            part = jnp.where((z_part == here_z)[None, None], part, 0.0)
+            cols = slice(t * 128, t * 128 + 128)
+            box[half, :, :, cols] = box[half, :, :, cols] + part
+    field = box[...].astype(BF)
     own[...] = field
     here = lax.axis_index("region")
     for p in range(faces.shape[0]):
@@ -118,7 +136,8 @@
             place(at, jnp.zeros(faces.shape[1:], BF))
 
 
-def extend_kernel(own, faces, far, near):
+def extend_kernel(own, faces, far, near, own_on):
+    own_on[...] = own[...]
     odd = lax.rem(lax.axis_index("tile"), 2)
 
     def fill(low, high):
@@ -416,15 +435,18 @@
         gather_kernel,
         [bf(8, 4, 16, 384), bf(regions, 4, 16, 384)],
         (brick_cell, features, voxel_mask, cotangent),
-        [pltpu.VMEM((512, 2304), BF), pltpu.VMEM((384, 2304), BF), pltpu.VMEM((32, 8, 128), F32),
+        [pltpu.VMEM((128, 512), BF), pltpu.VMEM((384, 2048), BF), pltpu.VMEM((128, 256), BF),
+         pltpu.VMEM((8, 4, 16, 384), F32), pltpu.VMEM((32, 8, 128), F32),
          pltpu.SMEM(brick_cell.shape, I32), pltpu.VMEM(features.shape, BF), pltpu.VMEM(voxel_mask.shape, I32),
          pltpu.VMEM(cotangent.shape, BF), pltpu.SemaphoreType.DMA((4,))],
         in_space=pltpu.HBM,
-        flops=2 * 512 * 2304 * 384,
+        flops=2 * 128 * 4 * 768 * 384,
         limit=60,
     )
     faces = lax.all_to_all(faces, "region", 0, 0, tiled=True)
-    far, near = vmem_call(extend_kernel, [bf(10, 16, 384), bf(10, 16, 384)], (own, faces), limit=4)
+    far, near, own = vmem_call(
+        extend_kernel, [bf(10, 16, 384), bf(10, 16, 384), bf(8, 4, 16, 384)], (own, faces), limit=4
+    )
 
     def swap(face, start):
         pairs = [(i, i + 1) for i in range(start, tiles - 1, 2)]

time: 60.3 us -> 58 us (0.962)
  Pallas kernels: 16.1 us -> 14.9 us
  local copies, waits for them, and re-layouts: 2.96 us -> 1.97 us
    pallas_call x8, Pallas kernels: 16.1 us -> 14.9 us  [vmem_call(): pl.pallas_call(kernel, out_shape=tuple(outs), in_specs=specs, out_specs=t...]
    unnamed x18 -> x14, local copies, waits for them, and re-layouts: 2.96 us -> 1.97 us
where the time goes in v5:
time: 58 us; the launch traced here: 57.5 us
  blocking collectives  30.6 us (53%)
  Pallas kernels  14.9 us (26%)
  starting transfers between devices  7.04 us (12%)
  waiting for transfers between devices  2.22 us (4%)
  local copies, waits for them, and re-layouts  1.97 us (3%)
  between operations  0.76 us (1%)
    pallas_call x8, Pallas kernels, vmem_call(): pl.pallas_call(kernel, out_shape=tuple(outs), in_specs=specs, out_specs=t...  14.9 us
    all_to_all x1, blocking collectives, on_device(): lax.all_to_all(terms.reshape(tiles, chunk, 128), 'tile', 0, 0, tiled=True)  12.7 us
    all_to_all x1, blocking collectives, on_device(): faces = lax.all_to_all(faces, 'region', 0, 0, tiled=True)  10.7 us
    all_to_all x1, blocking collectives, on_device(): parts = lax.all_to_all(total, 'region', 0, 0, tiled=True)  7.24 us
    ppermute x2, starting transfers between devices, swap(): return lax.ppermute(face, 'tile', pairs + [(j, i) for i, j in pairs])  3.67 us
    all_to_all x1, starting transfers between devices, on_device(): sums = lax.all_to_all(total, 'tile', 0, 0, tiled=True)  3.38 us
    all_to_all x1, waiting for transfers between devices, on_device(): sums = lax.all_to_all(total, 'tile', 0, 0, tiled=True)  2.22 us
    unnamed x14, local copies, waits for them, and re-layouts  1.97 us
  transfers between devices with their start and end apart: 3, of which 1 were waited for; matrix products, arithmetic and copies ran while one was open for 0% of the time, Pallas kernels for 9%

profile of v5, /device:TPU:0, one launch (start us, length us, event | category | flops | bytes accessed | tf_op | source)
XLA Modules:
  0.0 57.5 jit_solution(587699113868752321)
XLA Ops:
  0.6 0.0 copy-start.3
  0.6 0.0 copy-start.2
  0.7 0.0 copy-start.1
  0.7 2.6 %shard_map.110 = (bf16[8,4,16,384]{3,2,1,0:T(8,128)(2,1)}, bf16[4,4,16,384]{3,2,1,0:T(8,128)(2,1)}) custom-call(s32[4]{0:T(128)} %cell_ref.1, bf16[4,32,512]{2,1,0:T(8,128)(2,1)} %feat_hbm.1, s32[4,512]{1,0:T(4,128)} %vmask_hbm.1, bf16[4,4096]{1,0:T(4,128)(2,1)} %cot_hbm.1), custom_call_target="tpu_custom_call" | custom-call | flops 301989888 | bytes 761872 | tf_op jit(solution)/shard_map/pallas_call | solution.py:411
  3.2 10.7 %all_to_all.20.faces = bf16[4,4,16,384]{3,2,1,0:T(8,128)(2,1)S(1)} all-to-all(bf16[4,4,16,384]{3,2,1,0:T(8,128)(2,1)} %get-tuple-element.24), channel_id=1, replica_groups=mesh['region'=4,'tile'=8] {'region'}, dimensions={0} | all-to-all | bytes 393216 | tf_op jit(solution)/shard_map/all_to_all | solution.py:446
  14.0 0.0 copy-start
  14.0 1.0 %copy-done = bf16[8,4,16,384]{3,2,1,0:T(8,128)(2,1)S(1)} copy-done((bf16[8,4,16,384]{3,2,1,0:T(8,128)(2,1)S(1)}, bf16[8,4,16,384]{3,2,1,0:T(8,128)(2,1)}, u32[]{:S(2)}) %copy-start) | copy-done | bytes 393240
  15.0 0.1 shard_map.111
  15.0 0.7 %collective-permute-start = (bf16[10,16,384]{2,1,0:T(8,128)(2,1)S(1)}, bf16[10,16,384]{2,1,0:T(8,128)(2,1)S(1)}, u32[]{:S(2)}, u32[]{:S(2)}) collective-permute-start(bf16[10,16,384]{2,1,0:T(8,128)(2,1)S(1)} %get-tuple-element.26), channel_id=1, source_target_pairs={{1,2},{3,4},{5,6},{2,1},{4,3},{6,5},{9,10},{11,12},{13,14},{10,9},... | collective-permute-start | bytes 368648 | tf_op jit(solution)/shard_map/ppermute | solution.py:453
  15.7 3.0 %collective-permute-start.1 = (bf16[10,16,384]{2,1,0:T(8,128)(2,1)S(1)}, bf16[10,16,384]{2,1,0:T(8,128)(2,1)S(1)}, u32[]{:S(2)}, u32[]{:S(2)}) collective-permute-start(bf16[10,16,384]{2,1,0:T(8,128)(2,1)S(1)} %get-tuple-element.27), channel_id=1, source_target_pairs={{0,1},{2,3},{4,5},{6,7},{1,0},{3,2},{5,4},{7,6},{8,9},{10,11},{12,... | collective-permute-start | bytes 368648 | tf_op jit(solution)/shard_map/ppermute | solution.py:453
  18.7 0.0 copy-done.3
  18.7 0.0 copy-done.2
  18.7 0.0 copy-done.1
  18.7 1.5 %shard_map.112 = (bf16[2048,256]{1,0:T(8,128)(2,1)S(1)}, bf16[2048,256]{1,0:T(8,128)(2,1)S(1)}, bf16[2048,256]{1,0:T(8,128)(2,1)S(1)}, bf16[2048,256]{1,0:T(8,128)(2,1)S(1)}, bf16[512,128]{1,0:T(8,128)(2,1)S(1)}) custom-call(bf16[864,32]{1,0:T(8,128)(2,1)S(1)} %bitcast.5, bf16[864,32]{1,0:T(8,128)(2,1)S(1)} %bitcast.6, bf16[8,32,64]{2,1,0:T(8,128)(2,1)S(1)} %copy-done.3), custom_call_target="tpu_custom_call" | custom-call | flops 113246208 | bytes 4468736 | tf_op jit(solution)/shard_map/pallas_call | solution.py:411
  20.2 0.0 collective-permute-done.far
  20.2 0.0 collective-permute-done.1.near
  20.2 0.0 copy-start.4
  20.3 5.2 %shard_map.113 = (bf16[576,128]{1,0:T(8,128)(2,1)S(1)}, bf16[12,8,16,512]{3,2,1,0:T(8,128)(2,1)S(1)}, bf16[512,256]{1,0:T(8,128)(2,1)S(1)}) custom-call(bf16[8,4,16,384]{3,2,1,0:T(8,128)(2,1)S(1)} %get-tuple-element.25.own, bf16[4,4,16,384]{3,2,1,0:T(8,128)(2,1)S(1)} %all_to_all.20.faces, bf16[10,16,384]{2,1,0:T(8,128)(2,1)S(1)} %collective-permute-done.far, ...), custom_call_target="tpu_custom_call" | custom-call | flops 3623878656 | bytes 6094848 | tf_op jit(solution)/shard_map/pallas_call | solution.py:411
  25.5 0.0 copy-start.5
  25.5 12.7 %all_to_all.21.parts = bf16[8,72,128]{2,1,0:T(8,128)(2,1)S(1)} all-to-all(bf16[8,72,128]{2,1,0:T(8,128)(2,1)S(1)} %bitcast.7), channel_id=1, replica_groups=mesh['region'=4,'tile'=8] {'tile'}, dimensions={0} | all-to-all | bytes 294912 | tf_op jit(solution)/shard_map/all_to_all | solution.py:486
  38.1 7.2 %all_to_all.22.parts = bf16[4,72,128]{2,1,0:T(8,128)(2,1)S(1)} all-to-all(bf16[4,72,128]{2,1,0:T(8,128)(2,1)S(1)} %shard_map.115), channel_id=1, replica_groups=mesh['region'=4,'tile'=8] {'region'}, dimensions={0} | all-to-all | bytes 147456 | tf_op jit(solution)/shard_map/all_to_all | solution.py:488
  45.4 0.0 copy-done.5
  45.4 0.7 %shard_map.116 = bf16[8,72,128]{2,1,0:T(8,128)(2,1)} custom-call(bf16[4,72,128]{2,1,0:T(8,128)(2,1)S(1)} %all_to_all.22.parts), custom_call_target="tpu_custom_call" | custom-call | bytes 221184 | tf_op jit(solution)/shard_map/pallas_call | solution.py:411
  46.1 3.4 %all-to-all-start.3 = ((bf16[8,72,128]{2,1,0:T(8,128)(2,1)}), bf16[8,72,128]{2,1,0:T(8,128)(2,1)S(1)}, u32[]{:S(2)}, u32[]{:S(2)}) async-start(bf16[8,72,128]{2,1,0:T(8,128)(2,1)} %shard_map.116), calls=%async_computation.3 | async-start | bytes 294912 | tf_op jit(solution)/shard_map/all_to_all | solution.py:490
  49.4 0.0 copy-done.4
  49.5 0.0 copy-start.6
  49.5 0.9 %copy-done.6 = bf16[512,256]{1,0:T(8,128)(2,1)S(1)} copy-done((bf16[512,256]{1,0:T(8,128)(2,1)S(1)}, bf16[512,256]{1,0:T(8,128)(2,1)}, u32[]{:S(2)}) %copy-start.6) | copy-done | bytes 262168
  50.4 3.8 %shard_map.114 = (bf16[4,32,512]{2,1,0:T(8,128)(2,1)}, bf16[4,4096]{1,0:T(4,128)(2,1)}) custom-call(s32[4]{0:T(128)S(1)} %copy-done.4, bf16[8,4,16,384]{3,2,1,0:T(8,128)(2,1)S(1)} %get-tuple-element.25.own, bf16[12,8,16,512]{3,2,1,0:T(8,128)(2,1)S(1)} %get-tuple-element.32.ef, bf16[512,256]{1,0:T(8,128)(2,1)S(1)} %copy-done.6, ...), custom_call_target="tpu_custom_call" | custom-call | flops 1073741824 | bytes 3571728 | tf_op jit(solution)/shard_map/pallas_call | solution.py:411
  54.2 2.2 %all-to-all-done.3 = bf16[8,72,128]{2,1,0:T(8,128)(2,1)S(1)} async-done(((bf16[8,72,128]{2,1,0:T(8,128)(2,1)}), bf16[8,72,128]{2,1,0:T(8,128)(2,1)S(1)}, u32[]{:S(2)}, u32[]{:S(2)}) %all-to-all-start.3) | async-done | bytes 147488 | tf_op jit(solution)/shard_map/all_to_all | solution.py:490
  56.4 1.2 %shard_map.117 = (f32[27,32,32]{2,1,0:T(8,128)}, f32[27,32,32]{2,1,0:T(8,128)}, f32[8,32,64]{2,1,0:T(8,128)}) custom-call(bf16[576,128]{1,0:T(8,128)(2,1)S(1)} %bitcast.4), custom_call_target="tpu_custom_call" | custom-call | bytes 434176 | tf_op jit(solution)/shard_map/pallas_call | solution.py:411
  (1 shorter events, 0.0 us)
Async XLA Ops:
  0.6 18.1 %copy-start.3 = (bf16[8,32,64]{2,1,0:T(8,128)(2,1)S(1)}, bf16[8,32,64]{2,1,0:T(8,128)(2,1)}, u32[]{:S(2)}) copy-start(bf16[8,32,64]{2,1,0:T(8,128)(2,1)} %dw_ref.1) | copy-start | bytes 98308
  0.6 18.1 %copy-start.2 = (bf16[27,32,32]{2,1,0:T(8,128)(2,1)S(1)}, bf16[27,32,32]{2,1,0:T(8,128)(2,1)}, u32[]{:S(2)}) copy-start(bf16[27,32,32]{2,1,0:T(8,128)(2,1)} %param.11) | copy-start | bytes 165892
  0.7 18.1 %copy-start.1 = (bf16[27,32,32]{2,1,0:T(8,128)(2,1)S(1)}, bf16[27,32,32]{2,1,0:T(8,128)(2,1)}, u32[]{:S(2)}) copy-start(bf16[27,32,32]{2,1,0:T(8,128)(2,1)} %param.10) | copy-start | bytes 165892
  14.0 1.0 %copy-start = (bf16[8,4,16,384]{3,2,1,0:T(8,128)(2,1)S(1)}, bf16[8,4,16,384]{3,2,1,0:T(8,128)(2,1)}, u32[]{:S(2)}) copy-start(bf16[8,4,16,384]{3,2,1,0:T(8,128)(2,1)} %get-tuple-element.23.own) | copy-start | bytes 1179652
  15.0 5.2 %collective-permute-start = (bf16[10,16,384]{2,1,0:T(8,128)(2,1)S(1)}, bf16[10,16,384]{2,1,0:T(8,128)(2,1)S(1)}, u32[]{:S(2)}, u32[]{:S(2)}) collective-permute-start(bf16[10,16,384]{2,1,0:T(8,128)(2,1)S(1)} %get-tuple-element.26), channel_id=1, source_target_pairs={{1,2},{3,4},{5,6},{2,1},{4,3},{6,5},{9,10},{11,12},{13,14},{10,9},... | collective-permute-start | bytes 368648 | tf_op jit(solution)/shard_map/ppermute | solution.py:453
  15.7 4.5 %collective-permute-start.1 = (bf16[10,16,384]{2,1,0:T(8,128)(2,1)S(1)}, bf16[10,16,384]{2,1,0:T(8,128)(2,1)S(1)}, u32[]{:S(2)}, u32[]{:S(2)}) collective-permute-start(bf16[10,16,384]{2,1,0:T(8,128)(2,1)S(1)} %get-tuple-element.27), channel_id=1, source_target_pairs={{0,1},{2,3},{4,5},{6,7},{1,0},{3,2},{5,4},{7,6},{8,9},{10,11},{12,... | collective-permute-start | bytes 368648 | tf_op jit(solution)/shard_map/ppermute | solution.py:453
  20.2 29.2 %copy-start.4 = (s32[4]{0:T(128)S(1)}, s32[4]{0:T(128)}, u32[]{:S(2)}) copy-start(s32[4]{0:T(128)} %cell_ref.1) | copy-start | bytes 52
  25.5 19.9 %copy-start.5 = (bf16[512,256]{1,0:T(8,128)(2,1)}, bf16[512,256]{1,0:T(8,128)(2,1)S(1)}, u32[]{:S(2)}) copy-start(bf16[512,256]{1,0:T(8,128)(2,1)S(1)} %get-tuple-element.33.summed) | copy-start | bytes 786436
  46.1 10.3 %all-to-all-start.3 = ((bf16[8,72,128]{2,1,0:T(8,128)(2,1)}), bf16[8,72,128]{2,1,0:T(8,128)(2,1)S(1)}, u32[]{:S(2)}, u32[]{:S(2)}) async-start(bf16[8,72,128]{2,1,0:T(8,128)(2,1)} %shard_map.116), calls=%async_computation.3 | async-start | bytes 294912 | tf_op jit(solution)/shard_map/all_to_all | solution.py:490
  49.5 1.0 %copy-start.6 = (bf16[512,256]{1,0:T(8,128)(2,1)S(1)}, bf16[512,256]{1,0:T(8,128)(2,1)}, u32[]{:S(2)}) copy-start(bf16[512,256]{1,0:T(8,128)(2,1)} %copy-done.5) | copy-start | bytes 786436

commit v6 on v5

--- a/solution.py
+++ b/solution.py
@@ -282,8 +282,8 @@
 
 
 def main_kernel(own, faces, far, near, big1, big2, big2t, down_mat,
-                terms, ef, summed,
-                field, ex, eg, eh, mk, ax, ag, ah, turned, products, mixed):
+                give, keep, ef, summed,
+                terms, field, ex, eg, eh, mk, ax, ag, ah, turned, products, mixed):
     picks = lane_picks()
     field[1:9, 1:5] = own[...]
     odd = lax.rem(lax.axis_index("tile"), 2)
@@ -338,14 +338,16 @@
     terms[416:448, :] = held.astype(terms.dtype)
     cot = field[1:9, 1:5, :, 256:384].reshape(512, 128).astype(F32).T.astype(BF)
     grad_down = dot(cot, summed[...])
-    for half in range(2):
-        for odd in range(2):
-            part = grad_down[odd * 32 : odd * 32 + 32, half * 128 : half * 128 + 128]
-            mixed[pl.ds(half * 64 + odd, 32, stride=2), :] = part
+    for i in range(2):
+        for j in range(2):
+            mixed[pl.ds(i * 64 + j, 32, stride=2), :] = grad_down[j * 32 : j * 32 + 32, i * 128 : i * 128 + 128]
     terms[448:576, :] = mixed[...].astype(terms.dtype)
     rest = terms.shape[0] - 576
     if rest:
         terms[576:, :] = jnp.zeros((rest, 128), terms.dtype)
+    half = give.shape[0]
+    give[...] = terms[pl.ds(pl.multiple_of((1 - odd) * half, 8), half), :]
+    keep[...] = terms[pl.ds(pl.multiple_of(odd * half, 8), half), :]
 
 
 def tail_kernel(cell_ref, own, ef, summed, big1t, down_mat, grad_features, down, ah, turned, dense, place_mat, shuffle):
@@ -378,6 +380,10 @@
         down[:, j * 128 : j * 128 + 128] = shuffle[j, 0:4, :].astype(BF)
 
 
+def pair_kernel(mine, other, out):
+    out[...] = (mine[...] + other[...]).astype(out.dtype).reshape(out.shape)
+
+
 def reduce_kernel(parts, out):
     count = parts.shape[0]
     total = parts[0].astype(F32)
@@ -388,9 +394,13 @@
         out[i] = total
 
 
-def finish_kernel(scale, sums, one, two, down):
+def finish_kernel(scale, mine, other, one, two, down, sums):
+    odd = lax.rem(lax.axis_index("tile"), 2)
+    half = mine.shape[0]
+    sums[pl.ds(pl.multiple_of(odd * half, 8), half), :] = mine[...].astype(F32)
+    sums[pl.ds(pl.multiple_of((1 - odd) * half, 8), half), :] = other[...].astype(F32)
     for m in range(14):
-        block = (sums[m * 32 : m * 32 + 32, :].astype(F32) * scale).T
+        block = (sums[m * 32 : m * 32 + 32, :] * scale).T
         for g in range(4):
             k = 4 * m + g
             if k < 27:
@@ -398,7 +408,7 @@
             elif k < 54:
                 two[k - 27] = block[g * 32 : g * 32 + 32]
     for half in range(2):
-        block = (sums[448 + 64 * half : 512 + 64 * half, :].astype(F32) * scale).T
+        block = (sums[448 + 64 * half : 512 + 64 * half, :] * scale).T
         for g in range(4):
             down[4 * (g >> 1) + 2 * (g & 1) + half] = block[g * 32 : g * 32 + 32]
 
@@ -463,11 +473,13 @@
         limit=16,
     )
     chunk = -(-576 // (8 * tiles)) * 8
-    terms, ef, summed = vmem_call(
+    half = tiles // 2 * chunk
+    give, keep, ef, summed = vmem_call(
         main_kernel,
-        [bf(tiles * chunk, 128), bf(12, 8, 16, 512), bf(512, 256)],
+        [f32(half, 128), f32(half, 128), bf(12, 8, 16, 512), bf(512, 256)],
         (own, faces, far, near, big1, big2, big2t, down_mat),
         [
+            pltpu.VMEM((tiles * chunk, 128), F32),
             pltpu.VMEM((10, 6, 16, 384), BF),
             pltpu.VMEM((12, 8, 16, 512), BF),
             pltpu.VMEM((12, 8, 16, 512), BF),
@@ -483,11 +495,15 @@
         flops=2 * 2048 * 256 * (960 * 2 + 512 * 3),
         limit=32,
     )
-    parts = lax.all_to_all(terms.reshape(tiles, chunk, 128), "tile", 0, 0, tiled=True)
+    groups = [list(range(core, tiles, 2)) for core in range(2)]
+    (pairs,) = vmem_call(pair_kernel, [bf(tiles // 2, chunk, 128)], (keep, swap(give, 0)), limit=4)
+    parts = lax.all_to_all(pairs, "tile", 0, 0, axis_index_groups=groups, tiled=True)
     (total,) = vmem_call(reduce_kernel, [bf(regions, chunk, 128)], (parts,), limit=4)
     parts = lax.all_to_all(total, "region", 0, 0, tiled=True)
-    (total,) = vmem_call(reduce_kernel, [bf(tiles, chunk, 128)], (parts,), limit=4)
-    sums = lax.all_to_all(total, "tile", 0, 0, tiled=True)
+    (total,) = vmem_call(reduce_kernel, [bf(tiles // 2, chunk, 128)], (parts,), limit=4)
+    mine = lax.all_to_all(total, "tile", 0, 0, axis_index_groups=groups, tiled=True)
+    mine = mine.reshape(half, 128)
+    other = swap(mine, 0)
     grad_features, down = vmem_call(
         tail_kernel,
         [bf(slots, 32, 512), bf(slots, 4096)],
@@ -507,7 +523,8 @@
     grad_one, grad_two, grad_down = vmem_call(
         functools.partial(finish_kernel, scale),
         [f32(27, 32, 32), f32(27, 32, 32), f32(8, 32, 64)],
-        (sums.reshape(tiles * chunk, 128),),
+        (mine, other),
+        [pltpu.VMEM((tiles * chunk, 128), F32)],
         limit=8,
     )
     return down, grad_features, grad_one, grad_two, grad_down

time: 58 us -> 59.1 us (1.019)
  blocking collectives: 30.6 us -> 36.9 us
  starting transfers between devices: 7.04 us -> 4.67 us
  waiting for transfers between devices: 2.22 us -> 1.02 us
  local copies, waits for them, and re-layouts: 1.97 us -> 1.01 us
  Pallas kernels: 14.9 us -> 14.3 us
    all_to_all x1 -> x2, blocking collectives: 12.7 us -> 19 us  [the longest x1 10.8 us: on_device(): lax.all_to_all(pairs, 'tile', 0, 0, axis_index_groups=groups, tiled=True)]
    all_to_all x1 -> x0, starting transfers between devices: 3.38 us -> none  [on_device(): sums = lax.all_to_all(total, 'tile', 0, 0, tiled=True)]
    all_to_all x1 -> x0, waiting for transfers between devices: 2.22 us -> none  [on_device(): sums = lax.all_to_all(total, 'tile', 0, 0, tiled=True)]
    ppermute x2 -> x4, waiting for transfers between devices: 0.01 us -> 1.02 us  [swap(): return lax.ppermute(face, 'tile', pairs + [(j, i) for i, j in pairs])]
    ppermute x2 -> x4, starting transfers between devices: 3.67 us -> 4.67 us  [swap(): return lax.ppermute(face, 'tile', pairs + [(j, i) for i, j in pairs])]
    unnamed x14 -> x10, local copies, waits for them, and re-layouts: 1.97 us -> 1.01 us
    pallas_call x8 -> x9, Pallas kernels: 14.9 us -> 14.3 us  [vmem_call(): pl.pallas_call(kernel, out_shape=tuple(outs), in_specs=specs, out_specs=t...]
  transfers between devices with their start and end apart: 3 -> 4, of which waited for: 1 -> 1; matrix products, arithmetic and copies ran while one was open for 0% -> 0% of each run, Pallas kernels for 9% -> 9%
where the time goes in v6:
time: 59.1 us; the launch traced here: 58.7 us
  blocking collectives  36.9 us (62%)
  Pallas kernels  14.3 us (24%)
  starting transfers between devices  4.67 us (8%)
  waiting for transfers between devices  1.02 us (2%)
  local copies, waits for them, and re-layouts  1.01 us (2%)
  between operations  0.73 us (1%)
    pallas_call x9, Pallas kernels, vmem_call(): pl.pallas_call(kernel, out_shape=tuple(outs), in_specs=specs, out_specs=t...  14.3 us
    all_to_all x1, blocking collectives, on_device(): lax.all_to_all(pairs, 'tile', 0, 0, axis_index_groups=groups, tiled=True)  10.8 us
    all_to_all x1, blocking collectives, on_device(): faces = lax.all_to_all(faces, 'region', 0, 0, tiled=True)  10.7 us
    all_to_all x1, blocking collectives, on_device(): lax.all_to_all(total, 'tile', 0, 0, axis_index_groups=groups, tiled=True)  8.13 us
    all_to_all x1, blocking collectives, on_device(): parts = lax.all_to_all(total, 'region', 0, 0, tiled=True)  7.24 us
    ppermute x4, starting transfers between devices, swap(): return lax.ppermute(face, 'tile', pairs + [(j, i) for i, j in pairs])  4.67 us
  transfers between devices with their start and end apart: 4, of which 1 were waited for; matrix products, arithmetic and copies ran while one was open for 0% of the time, Pallas kernels for 9%

profile of v6, /device:TPU:0, one launch (start us, length us, event | category | flops | bytes accessed | tf_op | source)
XLA Modules:
  0.0 58.7 jit_solution(9087522954657397799)
XLA Ops:
  0.6 0.0 copy-start.3
  0.6 0.0 copy-start.2
  0.7 0.0 copy-start.1
  0.7 2.6 %shard_map.110 = (bf16[8,4,16,384]{3,2,1,0:T(8,128)(2,1)}, bf16[4,4,16,384]{3,2,1,0:T(8,128)(2,1)}) custom-call(s32[4]{0:T(128)} %cell_ref.1, bf16[4,32,512]{2,1,0:T(8,128)(2,1)} %feat_hbm.1, s32[4,512]{1,0:T(4,128)} %vmask_hbm.1, bf16[4,4096]{1,0:T(4,128)(2,1)} %cot_hbm.1), custom_call_target="tpu_custom_call" | custom-call | flops 301989888 | bytes 761872 | tf_op jit(solution)/shard_map/pallas_call | solution.py:421
  3.2 10.7 %all_to_all.20.faces = bf16[4,4,16,384]{3,2,1,0:T(8,128)(2,1)S(1)} all-to-all(bf16[4,4,16,384]{3,2,1,0:T(8,128)(2,1)} %get-tuple-element.25), channel_id=1, replica_groups=mesh['region'=4,'tile'=8] {'region'}, dimensions={0} | all-to-all | bytes 393216 | tf_op jit(solution)/shard_map/all_to_all | solution.py:456
  14.0 0.0 copy-start
  14.0 1.0 %copy-done = bf16[8,4,16,384]{3,2,1,0:T(8,128)(2,1)S(1)} copy-done((bf16[8,4,16,384]{3,2,1,0:T(8,128)(2,1)S(1)}, bf16[8,4,16,384]{3,2,1,0:T(8,128)(2,1)}, u32[]{:S(2)}) %copy-start) | copy-done | bytes 393240
  15.0 0.1 shard_map.111
  15.0 0.7 %collective-permute-start = (bf16[10,16,384]{2,1,0:T(8,128)(2,1)S(1)}, bf16[10,16,384]{2,1,0:T(8,128)(2,1)S(1)}, u32[]{:S(2)}, u32[]{:S(2)}) collective-permute-start(bf16[10,16,384]{2,1,0:T(8,128)(2,1)S(1)} %get-tuple-element.27), channel_id=1, source_target_pairs={{1,2},{3,4},{5,6},{2,1},{4,3},{6,5},{9,10},{11,12},{13,14},{10,9},... | collective-permute-start | bytes 368648 | tf_op jit(solution)/shard_map/ppermute | solution.py:463
  15.7 3.0 %collective-permute-start.1 = (bf16[10,16,384]{2,1,0:T(8,128)(2,1)S(1)}, bf16[10,16,384]{2,1,0:T(8,128)(2,1)S(1)}, u32[]{:S(2)}, u32[]{:S(2)}) collective-permute-start(bf16[10,16,384]{2,1,0:T(8,128)(2,1)S(1)} %get-tuple-element.28), channel_id=1, source_target_pairs={{0,1},{2,3},{4,5},{6,7},{1,0},{3,2},{5,4},{7,6},{8,9},{10,11},{12,... | collective-permute-start | bytes 368648 | tf_op jit(solution)/shard_map/ppermute | solution.py:463
  18.7 0.0 copy-done.3
  18.7 0.0 copy-done.2
  18.7 0.0 copy-done.1
  18.7 1.5 %shard_map.112 = (bf16[2048,256]{1,0:T(8,128)(2,1)S(1)}, bf16[2048,256]{1,0:T(8,128)(2,1)S(1)}, bf16[2048,256]{1,0:T(8,128)(2,1)S(1)}, bf16[2048,256]{1,0:T(8,128)(2,1)S(1)}, bf16[512,128]{1,0:T(8,128)(2,1)S(1)}) custom-call(bf16[864,32]{1,0:T(8,128)(2,1)S(1)} %bitcast.5, bf16[864,32]{1,0:T(8,128)(2,1)S(1)} %bitcast.6, bf16[8,32,64]{2,1,0:T(8,128)(2,1)S(1)} %copy-done.3), custom_call_target="tpu_custom_call" | custom-call | flops 113246208 | bytes 4468736 | tf_op jit(solution)/shard_map/pallas_call | solution.py:421
  20.2 0.0 collective-permute-done.far
  20.2 0.0 collective-permute-done.1.near
  20.2 0.0 copy-start.4
  20.3 5.2 %shard_map.113 = (f32[288,128]{1,0:T(8,128)S(1)}, f32[288,128]{1,0:T(8,128)S(1)}, bf16[12,8,16,512]{3,2,1,0:T(8,128)(2,1)S(1)}, bf16[512,256]{1,0:T(8,128)(2,1)S(1)}) custom-call(bf16[8,4,16,384]{3,2,1,0:T(8,128)(2,1)S(1)} %get-tuple-element.26.own, bf16[4,4,16,384]{3,2,1,0:T(8,128)(2,1)S(1)} %all_to_all.20.faces, ...), custom_call_target="tpu_custom_call" | custom-call | flops 3623878656 | bytes 6242304 | tf_op jit(solution)/shard_map/pallas_call | solution.py:421
  25.5 1.0 %collective-permute-start.2 = (f32[288,128]{1,0:T(8,128)S(1)}, f32[288,128]{1,0:T(8,128)S(1)}, u32[]{:S(2)}, u32[]{:S(2)}) collective-permute-start(f32[288,128]{1,0:T(8,128)S(1)} %get-tuple-element.39), channel_id=1, source_target_pairs={{0,1},{2,3},{4,5},{6,7},{1,0},{3,2},{5,4},{7,6},{8,9},{10,11},{12,... | collective-permute-start | bytes 442376 | tf_op jit(solution)/shard_map/ppermute | solution.py:463
  26.5 1.0 %collective-permute-done.2.other = f32[288,128]{1,0:T(8,128)S(1)} collective-permute-done((f32[288,128]{1,0:T(8,128)S(1)}, f32[288,128]{1,0:T(8,128)S(1)}, u32[]{:S(2)}, u32[]{:S(2)}) %collective-permute-start.2) | collective-permute-done | bytes 147488 | tf_op jit(solution)/shard_map/ppermute | solution.py:463
  27.5 10.8 %all_to_all.21.parts = bf16[4,72,128]{2,1,0:T(8,128)(2,1)S(1)} all-to-all(bf16[4,72,128]{2,1,0:T(8,128)(2,1)S(1)} %shard_map.115), channel_id=1, replica_groups={{0,2,4,6},{1,3,5,7},{8,10,12,14},{9,11,13,15},{16,18,20,22},{17,19,21,2..., dimensions={0} | all-to-all | bytes 147456 | tf_op jit(solution)/shard_map/all_to_all | solution.py:500
  38.4 7.2 %all_to_all.22.parts = bf16[4,72,128]{2,1,0:T(8,128)(2,1)S(1)} all-to-all(bf16[4,72,128]{2,1,0:T(8,128)(2,1)S(1)} %shard_map.116), channel_id=1, replica_groups=mesh['region'=4,'tile'=8] {'region'}, dimensions={0} | all-to-all | bytes 147456 | tf_op jit(solution)/shard_map/all_to_all | solution.py:502
  45.6 8.1 %all_to_all.23 = bf16[4,72,128]{2,1,0:T(8,128)(2,1)S(1)} all-to-all(bf16[4,72,128]{2,1,0:T(8,128)(2,1)S(1)} %shard_map.117), channel_id=1, replica_groups={{0,2,4,6},{1,3,5,7},{8,10,12,14},{9,11,13,15},{16,18,20,22},{17,19,21,2..., dimensions={0} | all-to-all | bytes 147456 | tf_op jit(solution)/shard_map/all_to_all | solution.py:504
  53.8 0.0 collective-permute-start.3
  53.8 0.0 copy-done.4
  53.8 3.7 %shard_map.114 = (bf16[4,32,512]{2,1,0:T(8,128)(2,1)}, bf16[4,4096]{1,0:T(4,128)(2,1)}) custom-call(s32[4]{0:T(128)S(1)} %copy-done.4, bf16[8,4,16,384]{3,2,1,0:T(8,128)(2,1)S(1)} %get-tuple-element.26.own, bf16[12,8,16,512]{3,2,1,0:T(8,128)(2,1)S(1)} %get-tuple-element.33.ef, bf16[512,256]{1,0:T(8,128)(2,1)S(1)} %get-tuple-element.34.summed, ...), custom_call_target="tpu_custom_call" | custom-call | flops 1073741824 | bytes 3571728 | tf_op jit(solution)/shard_map/pallas_call | solution.py:421
  57.5 0.0 collective-permute-done.3.other
  57.5 1.2 %shard_map.118 = (f32[27,32,32]{2,1,0:T(8,128)}, f32[27,32,32]{2,1,0:T(8,128)}, f32[8,32,64]{2,1,0:T(8,128)}) custom-call(bf16[288,128]{1,0:T(8,128)(2,1)S(1)} %bitcast.4, bf16[288,128]{1,0:T(8,128)(2,1)S(1)} %collective-permute-done.3.other), custom_call_target="tpu_custom_call" | custom-call | bytes 434176 | tf_op jit(solution)/shard_map/pallas_call | solution.py:421
  (3 shorter events, 0.0 us)
Async XLA Ops:
  0.6 18.1 %copy-start.3 = (bf16[8,32,64]{2,1,0:T(8,128)(2,1)S(1)}, bf16[8,32,64]{2,1,0:T(8,128)(2,1)}, u32[]{:S(2)}) copy-start(bf16[8,32,64]{2,1,0:T(8,128)(2,1)} %dw_ref.1) | copy-start | bytes 98308
  0.6 18.1 %copy-start.2 = (bf16[27,32,32]{2,1,0:T(8,128)(2,1)S(1)}, bf16[27,32,32]{2,1,0:T(8,128)(2,1)}, u32[]{:S(2)}) copy-start(bf16[27,32,32]{2,1,0:T(8,128)(2,1)} %param.11) | copy-start | bytes 165892
  0.7 18.1 %copy-start.1 = (bf16[27,32,32]{2,1,0:T(8,128)(2,1)S(1)}, bf16[27,32,32]{2,1,0:T(8,128)(2,1)}, u32[]{:S(2)}) copy-start(bf16[27,32,32]{2,1,0:T(8,128)(2,1)} %param.10) | copy-start | bytes 165892
  14.0 1.0 %copy-start = (bf16[8,4,16,384]{3,2,1,0:T(8,128)(2,1)S(1)}, bf16[8,4,16,384]{3,2,1,0:T(8,128)(2,1)}, u32[]{:S(2)}) copy-start(bf16[8,4,16,384]{3,2,1,0:T(8,128)(2,1)} %get-tuple-element.24.own) | copy-start | bytes 1179652
  15.0 5.2 %collective-permute-start = (bf16[10,16,384]{2,1,0:T(8,128)(2,1)S(1)}, bf16[10,16,384]{2,1,0:T(8,128)(2,1)S(1)}, u32[]{:S(2)}, u32[]{:S(2)}) collective-permute-start(bf16[10,16,384]{2,1,0:T(8,128)(2,1)S(1)} %get-tuple-element.27), channel_id=1, source_target_pairs={{1,2},{3,4},{5,6},{2,1},{4,3},{6,5},{9,10},{11,12},{13,14},{10,9},... | collective-permute-start | bytes 368648 | tf_op jit(solution)/shard_map/ppermute | solution.py:463
  15.7 4.5 %collective-permute-start.1 = (bf16[10,16,384]{2,1,0:T(8,128)(2,1)S(1)}, bf16[10,16,384]{2,1,0:T(8,128)(2,1)S(1)}, u32[]{:S(2)}, u32[]{:S(2)}) collective-permute-start(bf16[10,16,384]{2,1,0:T(8,128)(2,1)S(1)} %get-tuple-element.28), channel_id=1, source_target_pairs={{0,1},{2,3},{4,5},{6,7},{1,0},{3,2},{5,4},{7,6},{8,9},{10,11},{12,... | collective-permute-start | bytes 368648 | tf_op jit(solution)/shard_map/ppermute | solution.py:463
  20.2 33.5 %copy-start.4 = (s32[4]{0:T(128)S(1)}, s32[4]{0:T(128)}, u32[]{:S(2)}) copy-start(s32[4]{0:T(128)} %cell_ref.1) | copy-start | bytes 52
  25.5 2.0 %collective-permute-start.2 = (f32[288,128]{1,0:T(8,128)S(1)}, f32[288,128]{1,0:T(8,128)S(1)}, u32[]{:S(2)}, u32[]{:S(2)}) collective-permute-start(f32[288,128]{1,0:T(8,128)S(1)} %get-tuple-element.39), channel_id=1, source_target_pairs={{0,1},{2,3},{4,5},{6,7},{1,0},{3,2},{5,4},{7,6},{8,9},{10,11},{12,... | collective-permute-start | bytes 442376 | tf_op jit(solution)/shard_map/ppermute | solution.py:463
  53.8 3.7 %collective-permute-start.3 = (bf16[288,128]{1,0:T(8,128)(2,1)S(1)}, bf16[288,128]{1,0:T(8,128)(2,1)S(1)}, u32[]{:S(2)}, u32[]{:S(2)}) collective-permute-start(bf16[288,128]{1,0:T(8,128)(2,1)S(1)} %bitcast.3), channel_id=1, source_target_pairs={{0,1},{2,3},{4,5},{6,7},{1,0},{3,2},{5,4},{7,6},{8,9},{10,11},{12,... | collective-permute-start | bytes 221192 | tf_op jit(solution)/shard_map/ppermute | solution.py:463

commit v7 on v6

--- a/solution.py
+++ b/solution.py
@@ -350,7 +350,7 @@
     keep[...] = terms[pl.ds(pl.multiple_of(odd * half, 8), half), :]
 
 
-def tail_kernel(cell_ref, own, ef, summed, big1t, down_mat, grad_features, down, ah, turned, dense, place_mat, shuffle):
+def tail_kernel(cell_ref, own, ef, summed, big1t, down_mat, grad_features, down, token, ah, turned, dense, place_mat, shuffle):
     picks = lane_picks()
 
     for x in range(0, 8, 4):
@@ -378,6 +378,12 @@
         shuffle[:, 2 * t + 1, :] = jnp.where(low, pltpu.roll(even, 64, 1), odd)
     for j in range(32):
         down[:, j * 128 : j * 128 + 128] = shuffle[j, 0:4, :].astype(BF)
+    token[...] = jnp.zeros((8, 128), F32)
+
+
+def after_kernel(mine, token, out):
+    del token
+    out[...] = mine[...]
 
 
 def pair_kernel(mine, other, out):
@@ -503,10 +509,9 @@
     (total,) = vmem_call(reduce_kernel, [bf(tiles // 2, chunk, 128)], (parts,), limit=4)
     mine = lax.all_to_all(total, "tile", 0, 0, axis_index_groups=groups, tiled=True)
     mine = mine.reshape(half, 128)
-    other = swap(mine, 0)
-    grad_features, down = vmem_call(
+    grad_features, down, token = vmem_call(
         tail_kernel,
-        [bf(slots, 32, 512), bf(slots, 4096)],
+        [bf(slots, 32, 512), bf(slots, 4096), f32(8, 128)],
         (brick_cell, own, ef, summed, big1t, down_mat),
         [
             pltpu.VMEM((8, 4, 16, 2048), BF),
@@ -519,6 +524,8 @@
         flops=2 * 2048 * 512 * 512,
         limit=16,
     )
+    (mine,) = vmem_call(after_kernel, [bf(half, 128)], (mine, token), limit=4)
+    other = swap(mine, 0)
     scale = 1.0 / math.sqrt(devices * slots * 512.0)
     grad_one, grad_two, grad_down = vmem_call(
         functools.partial(finish_kernel, scale),

time: 59.1 us -> 58.2 us (0.985)
  blocking collectives: 36.9 us -> 28.8 us
  starting transfers between devices: 4.67 us -> 7.95 us
  waiting for transfers between devices: 1.02 us -> 4.22 us
  Pallas kernels: 14.3 us -> 15 us
    all_to_all x1 -> x0, blocking collectives: 8.13 us -> none  [on_device(): lax.all_to_all(total, 'tile', 0, 0, axis_index_groups=groups, tiled=True)]
    all_to_all x0 -> x1, starting transfers between devices: none -> 3.29 us  [on_device(): lax.all_to_all(total, 'tile', 0, 0, axis_index_groups=groups, tiled=True)]
    all_to_all x0 -> x1, waiting for transfers between devices: none -> 1.95 us  [on_device(): lax.all_to_all(total, 'tile', 0, 0, axis_index_groups=groups, tiled=True)]
    ppermute x4, waiting for transfers between devices: 1.02 us -> 2.27 us  [swap(): return lax.ppermute(face, 'tile', pairs + [(j, i) for i, j in pairs])]
    pallas_call x9 -> x10, Pallas kernels: 14.3 us -> 15 us  [vmem_call(): pl.pallas_call(kernel, out_shape=tuple(outs), in_specs=specs, out_specs=t...]
  transfers between devices with their start and end apart: 4 -> 5, of which waited for: 1 -> 3; matrix products, arithmetic and copies ran while one was open for 0% -> 0% of each run, Pallas kernels for 9% -> 9%
where the time goes in v7:
time: 58.2 us; the launch traced here: 57.7 us
  blocking collectives  28.8 us (49%)
  Pallas kernels  15 us (26%)
  starting transfers between devices  7.95 us (14%)
  waiting for transfers between devices  4.22 us (7%)
  local copies, waits for them, and re-layouts  1.01 us (2%)
  between operations  0.75 us (1%)
    pallas_call x10, Pallas kernels, vmem_call(): pl.pallas_call(kernel, out_shape=tuple(outs), in_specs=specs, out_specs=t...  15 us
    all_to_all x1, blocking collectives, on_device(): lax.all_to_all(pairs, 'tile', 0, 0, axis_index_groups=groups, tiled=True)  10.8 us
    all_to_all x1, blocking collectives, on_device(): faces = lax.all_to_all(faces, 'region', 0, 0, tiled=True)  10.7 us
    all_to_all x1, blocking collectives, on_device(): parts = lax.all_to_all(total, 'region', 0, 0, tiled=True)  7.24 us
    ppermute x4, starting transfers between devices, swap(): return lax.ppermute(face, 'tile', pairs + [(j, i) for i, j in pairs])  4.66 us
    all_to_all x1, starting transfers between devices, on_device(): lax.all_to_all(total, 'tile', 0, 0, axis_index_groups=groups, tiled=True)  3.29 us
    ppermute x4, waiting for transfers between devices, swap(): return lax.ppermute(face, 'tile', pairs + [(j, i) for i, j in pairs])  2.27 us
    all_to_all x1, waiting for transfers between devices, on_device(): lax.all_to_all(total, 'tile', 0, 0, axis_index_groups=groups, tiled=True)  1.95 us
  transfers between devices with their start and end apart: 5, of which 3 were waited for; matrix products, arithmetic and copies ran while one was open for 0% of the time, Pallas kernels for 9%

profile of v7, /device:TPU:0, one launch (start us, length us, event | category | flops | bytes accessed | tf_op | source)
XLA Modules:
  0.0 57.7 jit_solution(6311953157974510114)
XLA Ops:
  0.6 0.0 copy-start.3
  0.6 0.0 copy-start.2
  0.7 0.0 copy-start.1
  0.7 2.6 %shard_map.110 = (bf16[8,4,16,384]{3,2,1,0:T(8,128)(2,1)}, bf16[4,4,16,384]{3,2,1,0:T(8,128)(2,1)}) custom-call(s32[4]{0:T(128)} %cell_ref.1, bf16[4,32,512]{2,1,0:T(8,128)(2,1)} %feat_hbm.1, s32[4,512]{1,0:T(4,128)} %vmask_hbm.1, bf16[4,4096]{1,0:T(4,128)(2,1)} %cot_hbm.1), custom_call_target="tpu_custom_call" | custom-call | flops 301989888 | bytes 761872 | tf_op jit(solution)/shard_map/pallas_call | solution.py:427
  3.2 10.7 %all_to_all.20.faces = bf16[4,4,16,384]{3,2,1,0:T(8,128)(2,1)S(1)} all-to-all(bf16[4,4,16,384]{3,2,1,0:T(8,128)(2,1)} %get-tuple-element.26), channel_id=1, replica_groups=mesh['region'=4,'tile'=8] {'region'}, dimensions={0} | all-to-all | bytes 393216 | tf_op jit(solution)/shard_map/all_to_all | solution.py:462
  14.0 0.0 copy-start
  14.0 1.0 %copy-done = bf16[8,4,16,384]{3,2,1,0:T(8,128)(2,1)S(1)} copy-done((bf16[8,4,16,384]{3,2,1,0:T(8,128)(2,1)S(1)}, bf16[8,4,16,384]{3,2,1,0:T(8,128)(2,1)}, u32[]{:S(2)}) %copy-start) | copy-done | bytes 393240
  15.0 0.1 shard_map.111
  15.0 0.7 %collective-permute-start = (bf16[10,16,384]{2,1,0:T(8,128)(2,1)S(1)}, bf16[10,16,384]{2,1,0:T(8,128)(2,1)S(1)}, u32[]{:S(2)}, u32[]{:S(2)}) collective-permute-start(bf16[10,16,384]{2,1,0:T(8,128)(2,1)S(1)} %get-tuple-element.28), channel_id=1, source_target_pairs={{1,2},{3,4},{5,6},{2,1},{4,3},{6,5},{9,10},{11,12},{13,14},{10,9},... | collective-permute-start | bytes 368648 | tf_op jit(solution)/shard_map/ppermute | solution.py:469
  15.7 3.0 %collective-permute-start.1 = (bf16[10,16,384]{2,1,0:T(8,128)(2,1)S(1)}, bf16[10,16,384]{2,1,0:T(8,128)(2,1)S(1)}, u32[]{:S(2)}, u32[]{:S(2)}) collective-permute-start(bf16[10,16,384]{2,1,0:T(8,128)(2,1)S(1)} %get-tuple-element.29), channel_id=1, source_target_pairs={{0,1},{2,3},{4,5},{6,7},{1,0},{3,2},{5,4},{7,6},{8,9},{10,11},{12,... | collective-permute-start | bytes 368648 | tf_op jit(solution)/shard_map/ppermute | solution.py:469
  18.7 0.0 copy-done.3
  18.7 0.0 copy-done.2
  18.7 0.0 copy-done.1
  18.7 1.5 %shard_map.112 = (bf16[2048,256]{1,0:T(8,128)(2,1)S(1)}, bf16[2048,256]{1,0:T(8,128)(2,1)S(1)}, bf16[2048,256]{1,0:T(8,128)(2,1)S(1)}, bf16[2048,256]{1,0:T(8,128)(2,1)S(1)}, bf16[512,128]{1,0:T(8,128)(2,1)S(1)}) custom-call(bf16[864,32]{1,0:T(8,128)(2,1)S(1)} %bitcast.4, bf16[864,32]{1,0:T(8,128)(2,1)S(1)} %bitcast.5, bf16[8,32,64]{2,1,0:T(8,128)(2,1)S(1)} %copy-done.3), custom_call_target="tpu_custom_call" | custom-call | flops 113246208 | bytes 4468736 | tf_op jit(solution)/shard_map/pallas_call | solution.py:427
  20.2 0.0 collective-permute-done.far
  20.2 0.0 collective-permute-done.1.near
  20.2 0.0 copy-start.4
  20.3 5.2 %shard_map.113 = (f32[288,128]{1,0:T(8,128)S(1)}, f32[288,128]{1,0:T(8,128)S(1)}, bf16[12,8,16,512]{3,2,1,0:T(8,128)(2,1)S(1)}, bf16[512,256]{1,0:T(8,128)(2,1)S(1)}) custom-call(bf16[8,4,16,384]{3,2,1,0:T(8,128)(2,1)S(1)} %get-tuple-element.27.own, bf16[4,4,16,384]{3,2,1,0:T(8,128)(2,1)S(1)} %all_to_all.20.faces, ...), custom_call_target="tpu_custom_call" | custom-call | flops 3623878656 | bytes 6242304 | tf_op jit(solution)/shard_map/pallas_call | solution.py:427
  25.5 1.0 %collective-permute-start.2 = (f32[288,128]{1,0:T(8,128)S(1)}, f32[288,128]{1,0:T(8,128)S(1)}, u32[]{:S(2)}, u32[]{:S(2)}) collective-permute-start(f32[288,128]{1,0:T(8,128)S(1)} %get-tuple-element.40), channel_id=1, source_target_pairs={{0,1},{2,3},{4,5},{6,7},{1,0},{3,2},{5,4},{7,6},{8,9},{10,11},{12,... | collective-permute-start | bytes 442376 | tf_op jit(solution)/shard_map/ppermute | solution.py:469
  26.5 1.0 %collective-permute-done.2.other = f32[288,128]{1,0:T(8,128)S(1)} collective-permute-done((f32[288,128]{1,0:T(8,128)S(1)}, f32[288,128]{1,0:T(8,128)S(1)}, u32[]{:S(2)}, u32[]{:S(2)}) %collective-permute-start.2) | collective-permute-done | bytes 147488 | tf_op jit(solution)/shard_map/ppermute | solution.py:469
  27.5 10.8 %all_to_all.21.parts = bf16[4,72,128]{2,1,0:T(8,128)(2,1)S(1)} all-to-all(bf16[4,72,128]{2,1,0:T(8,128)(2,1)S(1)} %shard_map.115), channel_id=1, replica_groups={{0,2,4,6},{1,3,5,7},{8,10,12,14},{9,11,13,15},{16,18,20,22},{17,19,21,2..., dimensions={0} | all-to-all | bytes 147456 | tf_op jit(solution)/shard_map/all_to_all | solution.py:506
  38.4 7.2 %all_to_all.22.parts = bf16[4,72,128]{2,1,0:T(8,128)(2,1)S(1)} all-to-all(bf16[4,72,128]{2,1,0:T(8,128)(2,1)S(1)} %shard_map.116), channel_id=1, replica_groups=mesh['region'=4,'tile'=8] {'region'}, dimensions={0} | all-to-all | bytes 147456 | tf_op jit(solution)/shard_map/all_to_all | solution.py:508
  45.6 0.6 %shard_map.117 = bf16[4,72,128]{2,1,0:T(8,128)(2,1)} custom-call(bf16[4,72,128]{2,1,0:T(8,128)(2,1)S(1)} %all_to_all.22.parts), custom_call_target="tpu_custom_call" | custom-call | bytes 147456 | tf_op jit(solution)/shard_map/pallas_call | solution.py:427
  46.3 3.3 %all-to-all-start.3 = ((bf16[4,72,128]{2,1,0:T(8,128)(2,1)}), bf16[4,72,128]{2,1,0:T(8,128)(2,1)S(1)}, u32[]{:S(2)}, u32[]{:S(2)}) async-start(bf16[4,72,128]{2,1,0:T(8,128)(2,1)} %shard_map.117), calls=%async_computation.3 | async-start | bytes 147456 | tf_op jit(solution)/shard_map/all_to_all | solution.py:510
  49.5 0.0 copy-done.4
  49.6 3.8 %shard_map.114 = (bf16[4,32,512]{2,1,0:T(8,128)(2,1)}, bf16[4,4096]{1,0:T(4,128)(2,1)}, f32[8,128]{1,0:T(8,128)S(1)}) custom-call(s32[4]{0:T(128)S(1)} %copy-done.4, bf16[8,4,16,384]{3,2,1,0:T(8,128)(2,1)S(1)} %get-tuple-element.27.own, bf16[12,8,16,512]{3,2,1,0:T(8,128)(2,1)S(1)} %get-tuple-element.34.ef, bf16[512,256]{1,0:T(8,128)(2,1)S(1)} %get-tuple-element.35.summed, ...), custom_call_target="tpu_custom_call" | custom-call | flops 1073741824 | bytes 3575824 | tf_op jit(solution)/shard_map/pallas_call | solution.py:427
  53.3 1.9 %all-to-all-done.3 = bf16[4,72,128]{2,1,0:T(8,128)(2,1)S(1)} async-done(((bf16[4,72,128]{2,1,0:T(8,128)(2,1)}), bf16[4,72,128]{2,1,0:T(8,128)(2,1)S(1)}, u32[]{:S(2)}, u32[]{:S(2)}) %all-to-all-start.3) | async-done | bytes 73760 | tf_op jit(solution)/shard_map/all_to_all | solution.py:510
  55.3 0.0 collective-permute-start.3
  55.3 1.3 %collective-permute-done.3.other = bf16[288,128]{1,0:T(8,128)(2,1)S(1)} collective-permute-done((bf16[288,128]{1,0:T(8,128)(2,1)S(1)}, bf16[288,128]{1,0:T(8,128)(2,1)S(1)}, u32[]{:S(2)}, u32[]{:S(2)}) %collective-permute-start.3) | collective-permute-done | bytes 73760 | tf_op jit(solution)/shard_map/ppermute | solution.py:469
  56.6 1.2 %shard_map.119 = (f32[27,32,32]{2,1,0:T(8,128)}, f32[27,32,32]{2,1,0:T(8,128)}, f32[8,32,64]{2,1,0:T(8,128)}) custom-call(bf16[288,128]{1,0:T(8,128)(2,1)S(1)} %shard_map.118.mine, bf16[288,128]{1,0:T(8,128)(2,1)S(1)} %collective-permute-done.3.other), custom_call_target="tpu_custom_call" | custom-call | bytes 434176 | tf_op jit(solution)/shard_map/pallas_call | solution.py:427
  (3 shorter events, 0.0 us)
Async XLA Ops:
  0.6 18.1 %copy-start.3 = (bf16[8,32,64]{2,1,0:T(8,128)(2,1)S(1)}, bf16[8,32,64]{2,1,0:T(8,128)(2,1)}, u32[]{:S(2)}) copy-start(bf16[8,32,64]{2,1,0:T(8,128)(2,1)} %dw_ref.1) | copy-start | bytes 98308
  0.6 18.1 %copy-start.2 = (bf16[27,32,32]{2,1,0:T(8,128)(2,1)S(1)}, bf16[27,32,32]{2,1,0:T(8,128)(2,1)}, u32[]{:S(2)}) copy-start(bf16[27,32,32]{2,1,0:T(8,128)(2,1)} %param.11) | copy-start | bytes 165892
  0.7 18.1 %copy-start.1 = (bf16[27,32,32]{2,1,0:T(8,128)(2,1)S(1)}, bf16[27,32,32]{2,1,0:T(8,128)(2,1)}, u32[]{:S(2)}) copy-start(bf16[27,32,32]{2,1,0:T(8,128)(2,1)} %param.10) | copy-start | bytes 165892
  14.0 1.0 %copy-start = (bf16[8,4,16,384]{3,2,1,0:T(8,128)(2,1)S(1)}, bf16[8,4,16,384]{3,2,1,0:T(8,128)(2,1)}, u32[]{:S(2)}) copy-start(bf16[8,4,16,384]{3,2,1,0:T(8,128)(2,1)} %get-tuple-element.25.own) | copy-start | bytes 1179652
  15.0 5.2 %collective-permute-start = (bf16[10,16,384]{2,1,0:T(8,128)(2,1)S(1)}, bf16[10,16,384]{2,1,0:T(8,128)(2,1)S(1)}, u32[]{:S(2)}, u32[]{:S(2)}) collective-permute-start(bf16[10,16,384]{2,1,0:T(8,128)(2,1)S(1)} %get-tuple-element.28), channel_id=1, source_target_pairs={{1,2},{3,4},{5,6},{2,1},{4,3},{6,5},{9,10},{11,12},{13,14},{10,9},... | collective-permute-start | bytes 368648 | tf_op jit(solution)/shard_map/ppermute | solution.py:469
  15.7 4.5 %collective-permute-start.1 = (bf16[10,16,384]{2,1,0:T(8,128)(2,1)S(1)}, bf16[10,16,384]{2,1,0:T(8,128)(2,1)S(1)}, u32[]{:S(2)}, u32[]{:S(2)}) collective-permute-start(bf16[10,16,384]{2,1,0:T(8,128)(2,1)S(1)} %get-tuple-element.29), channel_id=1, source_target_pairs={{0,1},{2,3},{4,5},{6,7},{1,0},{3,2},{5,4},{7,6},{8,9},{10,11},{12,... | collective-permute-start | bytes 368648 | tf_op jit(solution)/shard_map/ppermute | solution.py:469
  20.2 29.3 %copy-start.4 = (s32[4]{0:T(128)S(1)}, s32[4]{0:T(128)}, u32[]{:S(2)}) copy-start(s32[4]{0:T(128)} %cell_ref.1) | copy-start | bytes 52
  25.5 2.0 %collective-permute-start.2 = (f32[288,128]{1,0:T(8,128)S(1)}, f32[288,128]{1,0:T(8,128)S(1)}, u32[]{:S(2)}, u32[]{:S(2)}) collective-permute-start(f32[288,128]{1,0:T(8,128)S(1)} %get-tuple-element.40), channel_id=1, source_target_pairs={{0,1},{2,3},{4,5},{6,7},{1,0},{3,2},{5,4},{7,6},{8,9},{10,11},{12,... | collective-permute-start | bytes 442376 | tf_op jit(solution)/shard_map/ppermute | solution.py:469
  46.3 9.0 %all-to-all-start.3 = ((bf16[4,72,128]{2,1,0:T(8,128)(2,1)}), bf16[4,72,128]{2,1,0:T(8,128)(2,1)S(1)}, u32[]{:S(2)}, u32[]{:S(2)}) async-start(bf16[4,72,128]{2,1,0:T(8,128)(2,1)} %shard_map.117), calls=%async_computation.3 | async-start | bytes 147456 | tf_op jit(solution)/shard_map/all_to_all | solution.py:510
  55.3 1.3 %collective-permute-start.3 = (bf16[288,128]{1,0:T(8,128)(2,1)S(1)}, bf16[288,128]{1,0:T(8,128)(2,1)S(1)}, u32[]{:S(2)}, u32[]{:S(2)}) collective-permute-start(bf16[288,128]{1,0:T(8,128)(2,1)S(1)} %shard_map.118.mine), channel_id=1, source_target_pairs={{0,1},{2,3},{4,5},{6,7},{1,0},{3,2},{5,4},{7,6},{8,9},{10,11},{12,... | collective-permute-start | bytes 221192 | tf_op jit(solution)/shard_map/ppermute | solution.py:469

commit v8 on v5

--- a/solution.py
+++ b/solution.py
@@ -306,17 +306,17 @@
         for j in range(2):
             put_field(ex, x + j + 1, 1, rows[j, :, :, 0:256])
             put_field(eg, x + j + 1, 1, grad[j])
-    for x in range(0, 10, 2):
-        for j in range(2):
+    for x in range(0, 10, 5):
+        for j in range(5):
             widen(ex, ax, x + j + 1, x + j, 1, 6, picks)
             widen(eg, ag, x + j + 1, x + j, 1, 6, picks)
-        mask = mk[x : x + 2].reshape(192, 256).astype(F32)
-        pre = dot(ax[x : x + 2].reshape(192, 2048), big1[...]) * mask
-        spread = dot(ag[x : x + 2].reshape(192, 2048), big2t[...])
+        mask = mk[x : x + 5].reshape(480, 256).astype(F32)
+        pre = dot(ax[x : x + 5].reshape(480, 2048), big1[...]) * mask
+        spread = dot(ag[x : x + 5].reshape(480, 2048), big2t[...])
         s = jax.nn.sigmoid(pre)
-        hidden = (pre * s).astype(BF).reshape(2, 6, 16, 256)
-        grad = (spread * s * (1.0 + pre * (1.0 - s)) * mask).astype(BF).reshape(2, 6, 16, 256)
-        for j in range(2):
+        hidden = (pre * s).astype(BF).reshape(5, 6, 16, 256)
+        grad = (spread * s * (1.0 + pre * (1.0 - s)) * mask).astype(BF).reshape(5, 6, 16, 256)
+        for j in range(5):
             put_field(eh, x + j + 1, 1, hidden[j])
             put_field(ef, x + j + 1, 1, grad[j])
     for x in range(0, 8, 4):

time: 58 us -> 58 us (level)
  no operation moved by 1% of the time
where the time goes in v8:
time: 58 us; the launch traced here: 57.5 us
  blocking collectives  30.6 us (53%)
  Pallas kernels  14.9 us (26%)
  starting transfers between devices  7.04 us (12%)
  waiting for transfers between devices  2.21 us (4%)
  local copies, waits for them, and re-layouts  1.97 us (3%)
  between operations  0.76 us (1%)
    pallas_call x8, Pallas kernels, vmem_call(): pl.pallas_call(kernel, out_shape=tuple(outs), in_specs=specs, out_specs=t...  14.9 us
    all_to_all x1, blocking collectives, on_device(): lax.all_to_all(terms.reshape(tiles, chunk, 128), 'tile', 0, 0, tiled=True)  12.7 us
    all_to_all x1, blocking collectives, on_device(): faces = lax.all_to_all(faces, 'region', 0, 0, tiled=True)  10.7 us
    all_to_all x1, blocking collectives, on_device(): parts = lax.all_to_all(total, 'region', 0, 0, tiled=True)  7.24 us
    ppermute x2, starting transfers between devices, swap(): return lax.ppermute(face, 'tile', pairs + [(j, i) for i, j in pairs])  3.67 us
    all_to_all x1, starting transfers between devices, on_device(): sums = lax.all_to_all(total, 'tile', 0, 0, tiled=True)  3.38 us
    all_to_all x1, waiting for transfers between devices, on_device(): sums = lax.all_to_all(total, 'tile', 0, 0, tiled=True)  2.2 us
    unnamed x14, local copies, waits for them, and re-layouts  1.97 us
  transfers between devices with their start and end apart: 3, of which 1 were waited for; matrix products, arithmetic and copies ran while one was open for 0% of the time, Pallas kernels for 9%

profile of v8, /device:TPU:0, one launch (start us, length us, event | category | flops | bytes accessed | tf_op | source)
XLA Modules:
  0.0 57.5 jit_solution(5256116964729074437)
XLA Ops:
  0.6 0.0 copy-start.3
  0.6 0.0 copy-start.2
  0.7 0.0 copy-start.1
  0.7 2.6 %shard_map.110 = (bf16[8,4,16,384]{3,2,1,0:T(8,128)(2,1)}, bf16[4,4,16,384]{3,2,1,0:T(8,128)(2,1)}) custom-call(s32[4]{0:T(128)} %cell_ref.1, bf16[4,32,512]{2,1,0:T(8,128)(2,1)} %feat_hbm.1, s32[4,512]{1,0:T(4,128)} %vmask_hbm.1, bf16[4,4096]{1,0:T(4,128)(2,1)} %cot_hbm.1), custom_call_target="tpu_custom_call" | custom-call | flops 301989888 | bytes 761872 | tf_op jit(solution)/shard_map/pallas_call | solution.py:411
  3.2 10.7 %all_to_all.20.faces = bf16[4,4,16,384]{3,2,1,0:T(8,128)(2,1)S(1)} all-to-all(bf16[4,4,16,384]{3,2,1,0:T(8,128)(2,1)} %get-tuple-element.24), channel_id=1, replica_groups=mesh['region'=4,'tile'=8] {'region'}, dimensions={0} | all-to-all | bytes 393216 | tf_op jit(solution)/shard_map/all_to_all | solution.py:446
  14.0 0.0 copy-start
  14.0 1.0 %copy-done = bf16[8,4,16,384]{3,2,1,0:T(8,128)(2,1)S(1)} copy-done((bf16[8,4,16,384]{3,2,1,0:T(8,128)(2,1)S(1)}, bf16[8,4,16,384]{3,2,1,0:T(8,128)(2,1)}, u32[]{:S(2)}) %copy-start) | copy-done | bytes 393240
  15.0 0.1 shard_map.111
  15.0 0.7 %collective-permute-start = (bf16[10,16,384]{2,1,0:T(8,128)(2,1)S(1)}, bf16[10,16,384]{2,1,0:T(8,128)(2,1)S(1)}, u32[]{:S(2)}, u32[]{:S(2)}) collective-permute-start(bf16[10,16,384]{2,1,0:T(8,128)(2,1)S(1)} %get-tuple-element.26), channel_id=1, source_target_pairs={{1,2},{3,4},{5,6},{2,1},{4,3},{6,5},{9,10},{11,12},{13,14},{10,9},... | collective-permute-start | bytes 368648 | tf_op jit(solution)/shard_map/ppermute | solution.py:453
  15.7 3.0 %collective-permute-start.1 = (bf16[10,16,384]{2,1,0:T(8,128)(2,1)S(1)}, bf16[10,16,384]{2,1,0:T(8,128)(2,1)S(1)}, u32[]{:S(2)}, u32[]{:S(2)}) collective-permute-start(bf16[10,16,384]{2,1,0:T(8,128)(2,1)S(1)} %get-tuple-element.27), channel_id=1, source_target_pairs={{0,1},{2,3},{4,5},{6,7},{1,0},{3,2},{5,4},{7,6},{8,9},{10,11},{12,... | collective-permute-start | bytes 368648 | tf_op jit(solution)/shard_map/ppermute | solution.py:453
  18.7 0.0 copy-done.3
  18.7 0.0 copy-done.2
  18.7 0.0 copy-done.1
  18.7 1.5 %shard_map.112 = (bf16[2048,256]{1,0:T(8,128)(2,1)S(1)}, bf16[2048,256]{1,0:T(8,128)(2,1)S(1)}, bf16[2048,256]{1,0:T(8,128)(2,1)S(1)}, bf16[2048,256]{1,0:T(8,128)(2,1)S(1)}, bf16[512,128]{1,0:T(8,128)(2,1)S(1)}) custom-call(bf16[864,32]{1,0:T(8,128)(2,1)S(1)} %bitcast.5, bf16[864,32]{1,0:T(8,128)(2,1)S(1)} %bitcast.6, bf16[8,32,64]{2,1,0:T(8,128)(2,1)S(1)} %copy-done.3), custom_call_target="tpu_custom_call" | custom-call | flops 113246208 | bytes 4468736 | tf_op jit(solution)/shard_map/pallas_call | solution.py:411
  20.2 0.0 collective-permute-done.far
  20.2 0.0 collective-permute-done.1.near
  20.2 0.0 copy-start.4
  20.3 5.2 %shard_map.113 = (bf16[576,128]{1,0:T(8,128)(2,1)S(1)}, bf16[12,8,16,512]{3,2,1,0:T(8,128)(2,1)S(1)}, bf16[512,256]{1,0:T(8,128)(2,1)S(1)}) custom-call(bf16[8,4,16,384]{3,2,1,0:T(8,128)(2,1)S(1)} %get-tuple-element.25.own, bf16[4,4,16,384]{3,2,1,0:T(8,128)(2,1)S(1)} %all_to_all.20.faces, bf16[10,16,384]{2,1,0:T(8,128)(2,1)S(1)} %collective-permute-done.far, ...), custom_call_target="tpu_custom_call" | custom-call | flops 3623878656 | bytes 6094848 | tf_op jit(solution)/shard_map/pallas_call | solution.py:411
  25.4 0.0 copy-start.5
  25.4 12.7 %all_to_all.21.parts = bf16[8,72,128]{2,1,0:T(8,128)(2,1)S(1)} all-to-all(bf16[8,72,128]{2,1,0:T(8,128)(2,1)S(1)} %bitcast.7), channel_id=1, replica_groups=mesh['region'=4,'tile'=8] {'tile'}, dimensions={0} | all-to-all | bytes 294912 | tf_op jit(solution)/shard_map/all_to_all | solution.py:486
  38.1 7.2 %all_to_all.22.parts = bf16[4,72,128]{2,1,0:T(8,128)(2,1)S(1)} all-to-all(bf16[4,72,128]{2,1,0:T(8,128)(2,1)S(1)} %shard_map.115), channel_id=1, replica_groups=mesh['region'=4,'tile'=8] {'region'}, dimensions={0} | all-to-all | bytes 147456 | tf_op jit(solution)/shard_map/all_to_all | solution.py:488
  45.4 0.0 copy-done.5
  45.4 0.7 %shard_map.116 = bf16[8,72,128]{2,1,0:T(8,128)(2,1)} custom-call(bf16[4,72,128]{2,1,0:T(8,128)(2,1)S(1)} %all_to_all.22.parts), custom_call_target="tpu_custom_call" | custom-call | bytes 221184 | tf_op jit(solution)/shard_map/pallas_call | solution.py:411
  46.1 3.4 %all-to-all-start.3 = ((bf16[8,72,128]{2,1,0:T(8,128)(2,1)}), bf16[8,72,128]{2,1,0:T(8,128)(2,1)S(1)}, u32[]{:S(2)}, u32[]{:S(2)}) async-start(bf16[8,72,128]{2,1,0:T(8,128)(2,1)} %shard_map.116), calls=%async_computation.3 | async-start | bytes 294912 | tf_op jit(solution)/shard_map/all_to_all | solution.py:490
  49.4 0.0 copy-done.4
  49.4 0.0 copy-start.6
  49.5 0.9 %copy-done.6 = bf16[512,256]{1,0:T(8,128)(2,1)S(1)} copy-done((bf16[512,256]{1,0:T(8,128)(2,1)S(1)}, bf16[512,256]{1,0:T(8,128)(2,1)}, u32[]{:S(2)}) %copy-start.6) | copy-done | bytes 262168
  50.4 3.8 %shard_map.114 = (bf16[4,32,512]{2,1,0:T(8,128)(2,1)}, bf16[4,4096]{1,0:T(4,128)(2,1)}) custom-call(s32[4]{0:T(128)S(1)} %copy-done.4, bf16[8,4,16,384]{3,2,1,0:T(8,128)(2,1)S(1)} %get-tuple-element.25.own, bf16[12,8,16,512]{3,2,1,0:T(8,128)(2,1)S(1)} %get-tuple-element.32.ef, bf16[512,256]{1,0:T(8,128)(2,1)S(1)} %copy-done.6, ...), custom_call_target="tpu_custom_call" | custom-call | flops 1073741824 | bytes 3571728 | tf_op jit(solution)/shard_map/pallas_call | solution.py:411
  54.2 2.2 %all-to-all-done.3 = bf16[8,72,128]{2,1,0:T(8,128)(2,1)S(1)} async-done(((bf16[8,72,128]{2,1,0:T(8,128)(2,1)}), bf16[8,72,128]{2,1,0:T(8,128)(2,1)S(1)}, u32[]{:S(2)}, u32[]{:S(2)}) %all-to-all-start.3) | async-done | bytes 147488 | tf_op jit(solution)/shard_map/all_to_all | solution.py:490
  56.4 1.2 %shard_map.117 = (f32[27,32,32]{2,1,0:T(8,128)}, f32[27,32,32]{2,1,0:T(8,128)}, f32[8,32,64]{2,1,0:T(8,128)}) custom-call(bf16[576,128]{1,0:T(8,128)(2,1)S(1)} %bitcast.4), custom_call_target="tpu_custom_call" | custom-call | bytes 434176 | tf_op jit(solution)/shard_map/pallas_call | solution.py:411
  (1 shorter events, 0.0 us)
Async XLA Ops:
  0.6 18.1 %copy-start.3 = (bf16[8,32,64]{2,1,0:T(8,128)(2,1)S(1)}, bf16[8,32,64]{2,1,0:T(8,128)(2,1)}, u32[]{:S(2)}) copy-start(bf16[8,32,64]{2,1,0:T(8,128)(2,1)} %dw_ref.1) | copy-start | bytes 98308
  0.6 18.1 %copy-start.2 = (bf16[27,32,32]{2,1,0:T(8,128)(2,1)S(1)}, bf16[27,32,32]{2,1,0:T(8,128)(2,1)}, u32[]{:S(2)}) copy-start(bf16[27,32,32]{2,1,0:T(8,128)(2,1)} %param.11) | copy-start | bytes 165892
  0.7 18.1 %copy-start.1 = (bf16[27,32,32]{2,1,0:T(8,128)(2,1)S(1)}, bf16[27,32,32]{2,1,0:T(8,128)(2,1)}, u32[]{:S(2)}) copy-start(bf16[27,32,32]{2,1,0:T(8,128)(2,1)} %param.10) | copy-start | bytes 165892
  14.0 1.0 %copy-start = (bf16[8,4,16,384]{3,2,1,0:T(8,128)(2,1)S(1)}, bf16[8,4,16,384]{3,2,1,0:T(8,128)(2,1)}, u32[]{:S(2)}) copy-start(bf16[8,4,16,384]{3,2,1,0:T(8,128)(2,1)} %get-tuple-element.23.own) | copy-start | bytes 1179652
  15.0 5.2 %collective-permute-start = (bf16[10,16,384]{2,1,0:T(8,128)(2,1)S(1)}, bf16[10,16,384]{2,1,0:T(8,128)(2,1)S(1)}, u32[]{:S(2)}, u32[]{:S(2)}) collective-permute-start(bf16[10,16,384]{2,1,0:T(8,128)(2,1)S(1)} %get-tuple-element.26), channel_id=1, source_target_pairs={{1,2},{3,4},{5,6},{2,1},{4,3},{6,5},{9,10},{11,12},{13,14},{10,9},... | collective-permute-start | bytes 368648 | tf_op jit(solution)/shard_map/ppermute | solution.py:453
  15.7 4.5 %collective-permute-start.1 = (bf16[10,16,384]{2,1,0:T(8,128)(2,1)S(1)}, bf16[10,16,384]{2,1,0:T(8,128)(2,1)S(1)}, u32[]{:S(2)}, u32[]{:S(2)}) collective-permute-start(bf16[10,16,384]{2,1,0:T(8,128)(2,1)S(1)} %get-tuple-element.27), channel_id=1, source_target_pairs={{0,1},{2,3},{4,5},{6,7},{1,0},{3,2},{5,4},{7,6},{8,9},{10,11},{12,... | collective-permute-start | bytes 368648 | tf_op jit(solution)/shard_map/ppermute | solution.py:453
  20.2 29.2 %copy-start.4 = (s32[4]{0:T(128)S(1)}, s32[4]{0:T(128)}, u32[]{:S(2)}) copy-start(s32[4]{0:T(128)} %cell_ref.1) | copy-start | bytes 52
  25.4 19.9 %copy-start.5 = (bf16[512,256]{1,0:T(8,128)(2,1)}, bf16[512,256]{1,0:T(8,128)(2,1)S(1)}, u32[]{:S(2)}) copy-start(bf16[512,256]{1,0:T(8,128)(2,1)S(1)} %get-tuple-element.33.summed) | copy-start | bytes 786436
  46.1 10.3 %all-to-all-start.3 = ((bf16[8,72,128]{2,1,0:T(8,128)(2,1)}), bf16[8,72,128]{2,1,0:T(8,128)(2,1)S(1)}, u32[]{:S(2)}, u32[]{:S(2)}) async-start(bf16[8,72,128]{2,1,0:T(8,128)(2,1)} %shard_map.116), calls=%async_computation.3 | async-start | bytes 294912 | tf_op jit(solution)/shard_map/all_to_all | solution.py:490
  49.4 1.0 %copy-start.6 = (bf16[512,256]{1,0:T(8,128)(2,1)S(1)}, bf16[512,256]{1,0:T(8,128)(2,1)}, u32[]{:S(2)}) copy-start(bf16[512,256]{1,0:T(8,128)(2,1)} %copy-done.5) | copy-start | bytes 786436
